TPU v7x, 32 devices: a whole 2x2x4 slice. The times are simulated.
32 devices in a mesh: dp: 2 (over y), context: 16 (over z, x, core).
Axes of the slice: x: 2, y: 2, z: 4, core: 2. Of those that a mesh axis runs over, the one named last changes fastest.
Arguments:
- codes: int32 [2, 16384], P('dp', 'context'), may hold values from 0 to 3
- variant_pos: int32 [2, 64], P('dp'), may hold values from 0 to 16383
- variant_shift: int32 [2, 64], P('dp'), may hold values from 1 to 3
- stem_weight: float32 [15, 4, 384], replicated, may hold values from -1.5 to 1.5
- conv_weight: bfloat16 [5, 384, 384], replicated, may hold values from -0.125 to 0.125
- cotangent: bfloat16 [2, 8192, 384], P('dp', 'context'), may hold values from -6 to 6
Outputs:
- features: bfloat16 [2, 8192, 384], P('dp', 'context')
- d_pooled: bfloat16 [2, 8192, 384], P('dp', 'context')
- conv_grad: float32 [5, 384, 384], replicated
- stem_grad: float32 [15, 4, 384], replicated
All inputs are finite; a program needn't handle non-finite values.
Results may differ from a plain program's by a relative error of at most 0.009.
Values may be sent and summed in bfloat16 or wider, within the bound.
No kernel may reach another device: no remote copies, remote signals or barrier semaphores. Data moves between devices by JAX's collectives and lax.ppermute only.
A program may use at most 64 MiB of HBM per device.

v0:
```python
import math

import jax
import jax.numpy as jnp
from jax import lax
from jax.sharding import PartitionSpec as P

root_scale = math.sqrt(2.0 / math.pi)
cubic = 0.044715


def with_halo(block, sides, width):
    for axis, dim in sides:
        count = lax.axis_size(axis)
        forward = [(i, i + 1) for i in range(count - 1)]
        backward = [(target, source) for source, target in forward]
        low = lax.ppermute(
            lax.slice_in_dim(block, block.shape[dim] - width, None, axis=dim), axis, forward
        )
        high = lax.ppermute(lax.slice_in_dim(block, 0, width, axis=dim), axis, backward)
        block = jnp.concatenate([low, block, high], axis=dim)
    return block


def gelu_tanh(value):
    return 0.5 * value * (1.0 + jnp.tanh(root_scale * (value + cubic * value * value * value)))


def gelu_slope(value):
    inner = jnp.tanh(root_scale * (value + cubic * value * value * value))
    return 0.5 * (1.0 + inner) + 0.5 * value * (1.0 - inner * inner) * root_scale * (
        1.0 + 3.0 * cubic * value * value
    )


def per_device(codes, variant_pos, variant_shift, stem_weight, conv_weight, cotangent):
    length = codes.shape[1]
    half_rows = length // 2
    width = stem_weight.shape[2]
    first_base = lax.axis_index("context") * length
    places = first_base + jnp.arange(length, dtype=jnp.int32)
    matches = (variant_pos[:, None, :] == places[None, :, None]).astype(jnp.int32)
    shifts = jnp.sum(matches * variant_shift[:, None, :], axis=2)
    mutated = (codes + shifts) % 4 + 1
    extended = with_halo(mutated, (("context", 1),), 7)
    onehot = (extended[:, :, None] == jnp.arange(1, 5, dtype=jnp.int32)[None, None, :]).astype(
        jnp.float32
    )
    windows = jnp.concatenate([onehot[:, k : k + length] for k in range(15)], axis=2)
    flat_stem = stem_weight.reshape(60, width)
    stem = jnp.einsum(
        "blk,kc->blc",
        windows,
        flat_stem,
        precision=lax.Precision.HIGHEST,
        preferred_element_type=jnp.float32,
    )
    active = gelu_tanh(stem)
    pooled = (0.5 * (active[:, 0::2] + active[:, 1::2])).astype(jnp.bfloat16)
    pooled_f = pooled.astype(jnp.float32)
    gated = gelu_tanh(pooled_f).astype(jnp.bfloat16)
    gated_ext = with_halo(gated, (("context", 1),), 2)
    cot_ext = with_halo(cotangent, (("context", 1),), 2)
    conv_out = jnp.zeros((gated.shape[0], half_rows, width), jnp.float32)
    back = jnp.zeros((gated.shape[0], half_rows, width), jnp.float32)
    for offset in range(5):
        conv_out = conv_out + jnp.einsum(
            "brc,cd->brd",
            gated_ext[:, offset : offset + half_rows],
            conv_weight[offset],
            preferred_element_type=jnp.float32,
        )
        back = back + jnp.einsum(
            "brd,cd->brc",
            cot_ext[:, 4 - offset : 4 - offset + half_rows],
            conv_weight[offset],
            preferred_element_type=jnp.float32,
        )
    features = (pooled_f + conv_out).astype(jnp.bfloat16)
    dpool = cotangent.astype(jnp.float32) + back * gelu_slope(pooled_f)
    d_pooled = dpool.astype(jnp.bfloat16)
    tap_grads = jnp.stack(
        [
            jnp.einsum(
                "brc,brd->cd",
                gated_ext[:, offset : offset + half_rows],
                cotangent,
                preferred_element_type=jnp.float32,
            )
            for offset in range(5)
        ]
    )
    dstem = 0.5 * jnp.repeat(dpool, 2, axis=1) * gelu_slope(stem)
    stem_part = jnp.einsum(
        "blk,blc->kc",
        windows,
        dstem,
        precision=lax.Precision.HIGHEST,
        preferred_element_type=jnp.float32,
    )
    stem_grad = lax.psum(stem_part, ("dp", "context")).reshape(15, 4, width)
    conv_grad = lax.psum(tap_grads, ("dp", "context"))
    return (features, d_pooled, conv_grad, stem_grad)


def solution(mesh):
    placed = (P("dp", "context"), P("dp", None), P("dp", None), P(), P(), P("dp", "context", None))
    return jax.shard_map(
        per_device,
        mesh=mesh,
        in_specs=placed,
        out_specs=(P("dp", "context", None), P("dp", "context", None), P(), P()),
        check_vma=False,
    )
```

profile of v0, /device:TPU:0, one launch (start us, length us, event | category | flops | bytes accessed | tf_op | source)
XLA Modules:
  0.0 210.6 jit_solution(9636843475704356709)
XLA Ops:
  8.8 1.3 collective-permute-start.1
  10.1 3.0 %collective-permute-start = (s32[1,7]{1,0:T(1,128)S(1)}, s32[1,7]{1,0:T(1,128)S(1)}, u32[]{:S(2)}, u32[]{:S(2)}) collective-permute-start(s32[1,7]{1,0:T(1,128)S(1)} %get-tuple-element.15), channel_id=1, source_target_pairs={{0,1},{1,2},{2,3},{3,4},{4,5},{5,6},{6,7},{7,8},{8,9},{9,10},{10,1... | collective-permute-start | bytes 92 | tf_op jit(solution)/shard_map/ppermute | solution.py:17
  13.1 1.3 fusion.112
  14.4 4.5 %collective-permute-start.5 = (bf16[1,2,384]{2,1,0:T(2,128)(2,1)}, bf16[1,2,384]{2,1,0:T(2,128)(2,1)S(1)}, u32[]{:S(2)}, u32[]{:S(2)}) collective-permute-start(bf16[1,2,384]{2,1,0:T(2,128)(2,1)} %get-tuple-element.10), channel_id=1, source_target_pairs={{0,1},{1,2},{2,3},{3,4},{4,5},{5,6},{6,7},{7,8},{8,9},{9,10},{10,1... | collective-permute-start | bytes 4616 | tf_op jit(solution)/shard_map/ppermute | solution.py:17
  18.9 1.3 collective-permute-start.4
  20.2 1.8 constant_dynamic-update-slice_fusion.16
  22.9 2.4 %fusion.59 = f32[512,384]{1,0:T(8,128)} fusion(bf16[1,512,384]{2,1,0:T(8,128)(2,1)} %param.11, bf16[5,384,384]{2,1,0:T(8,128)(2,1)} %param.10), kind=kOutput, calls=%fused_computation.91 | convolution fusion | flops 150994944 | bytes 1474560 | tf_op jit(solution)/shard_map/brd,cd->brc/dot_general | solution.py:73
  27.0 1.5 fusion.75
  29.0 2.8 %slice.143 = f32[1,512,384]{2,1,0:T(8,128)} slice(f32[1,1024,384]{2,1,0:T(8,128)S(1)} %multiply_bitcast_fusion), slice={[0:1:1], [1:1024:2], [0:384:1]} | slice | bytes 1572864 | tf_op jit(solution)/shard_map/slice | solution.py:59
  31.7 2.8 %slice.142 = f32[1,512,384]{2,1,0:T(8,128)} slice(f32[1,1024,384]{2,1,0:T(8,128)S(1)} %multiply_bitcast_fusion), slice={[0:1:1], [0:1024:2], [0:384:1]} | slice | bytes 1572864 | tf_op jit(solution)/shard_map/slice | solution.py:59
  34.5 1.9 fusion.29
  37.1 1.3 collective-permute-start.3
  38.3 3.8 %collective-permute-start.2 = (bf16[1,2,384]{2,1,0:T(2,128)(2,1)}, bf16[1,2,384]{2,1,0:T(2,128)(2,1)S(1)}, u32[]{:S(2)}, u32[]{:S(2)}) collective-permute-start(bf16[1,2,384]{2,1,0:T(2,128)(2,1)} %get-tuple-element.13), channel_id=1, source_target_pairs={{0,1},{1,2},{2,3},{3,4},{4,5},{5,6},{6,7},{7,8},{8,9},{9,10},{10,1... | collective-permute-start | bytes 4616 | tf_op jit(solution)/shard_map/ppermute | solution.py:17
  44.1 1.6 multiply_bitcast_fusion.1
  46.2 2.2 %mul.172 = f32[1024,384]{1,0:T(8,128)} reshape(f32[512,2,384]{2,1,0:T(2,128)S(1)} %broadcast_in_dim.2) | data formatting | bytes 3145728 | tf_op jit(solution)/shard_map/mul | solution.py:93
  48.5 3.6 %fusion.6 = f32[60,384]{1,0:T(8,128)S(1)} fusion(f32[1024,384]{1,0:T(8,128)} %mul.172, f32[1024,384]{1,0:T(8,128)S(1)} %fusion.75, f32[1,1024,60]{1,0,2:T(1,128)} %copy-done.8), kind=kOutput, calls=%fused_computation.16 | convolution fusion | flops 290193408 | bytes 3483648 | tf_op jit(solution)/shard_map/blk,blc->kc/dot_general | solution.py:94
  52.7 1.2 fusion.25
  54.0 1.2 fusion.24
  55.2 1.3 fusion.23
  56.5 1.2 fusion.22
  57.8 1.2 fusion.21
  59.0 1.3 copy-done.1
  63.1 136.3 %all-reduce.3.cloned.1.call-done = (f32[5,384,384]{2,1,0:T(8,128)}, f32[15,4,384]{2,1,0:T(4,128)}) async-done(((f32[5,384,384]{2,1,0:T(8,128)}, f32[15,4,384]{2,1,0:T(4,128)}), (f32[5,384,384]{2,1,0:T(8,128)}, f32[15,4,384]{2,1,0:T(4,128)})) %all-reduce.3.cloned.1.call-update) | async-done | bytes 3041296 | tf_op jit(solution)/shard_map/psum | solution.py:102
  199.4 3.7 %copy.40 = f32[5,384,384]{2,1,0:T(8,128)} copy(f32[5,384,384]{2,1,0:T(8,128)} %get-tuple-element.18) | data formatting | bytes 5898240
  (65 shorter events, 11.8 us)
Async XLA Ops:
  7.2 192.2 %all-reduce.3.cloned.1.call-start = ((), (), s32[]{:S(2)}) async-start(), calls=%async_computation | async-start | bytes 6082560 | tf_op jit(solution)/shard_map/psum | solution.py:102
  8.8 16.5 %collective-permute-start.1 = (s32[1,7]{1,0:T(1,128)S(1)}, s32[1,7]{1,0:T(1,128)S(1)}, u32[]{:S(2)}, u32[]{:S(2)}) collective-permute-start(s32[1,7]{1,0:T(1,128)S(1)} %get-tuple-element.14), channel_id=1, source_target_pairs={{1,0},{2,1},{3,2},{4,3},{5,4},{6,5},{7,6},{8,7},{9,8},{10,9},{11,1... | collective-permute-start | bytes 92 | tf_op jit(solution)/shard_map/ppermute | solution.py:20
  10.1 15.2 %collective-permute-start = (s32[1,7]{1,0:T(1,128)S(1)}, s32[1,7]{1,0:T(1,128)S(1)}, u32[]{:S(2)}, u32[]{:S(2)}) collective-permute-start(s32[1,7]{1,0:T(1,128)S(1)} %get-tuple-element.15), channel_id=1, source_target_pairs={{0,1},{1,2},{2,3},{3,4},{4,5},{5,6},{6,7},{7,8},{8,9},{9,10},{10,1... | collective-permute-start | bytes 92 | tf_op jit(solution)/shard_map/ppermute | solution.py:17
  14.4 28.7 %collective-permute-start.5 = (bf16[1,2,384]{2,1,0:T(2,128)(2,1)}, bf16[1,2,384]{2,1,0:T(2,128)(2,1)S(1)}, u32[]{:S(2)}, u32[]{:S(2)}) collective-permute-start(bf16[1,2,384]{2,1,0:T(2,128)(2,1)} %get-tuple-element.10), channel_id=1, source_target_pairs={{0,1},{1,2},{2,3},{3,4},{4,5},{5,6},{6,7},{7,8},{8,9},{9,10},{10,1... | collective-permute-start | bytes 4616 | tf_op jit(solution)/shard_map/ppermute | solution.py:17
  18.9 23.3 %collective-permute-start.4 = (bf16[1,2,384]{2,1,0:T(2,128)(2,1)}, bf16[1,2,384]{2,1,0:T(2,128)(2,1)S(1)}, u32[]{:S(2)}, u32[]{:S(2)}) collective-permute-start(bf16[1,2,384]{2,1,0:T(2,128)(2,1)} %get-tuple-element.11), channel_id=1, source_target_pairs={{1,0},{2,1},{3,2},{4,3},{5,4},{6,5},{7,6},{8,7},{9,8},{10,9},{11,1... | collective-permute-start | bytes 4616 | tf_op jit(solution)/shard_map/ppermute | solution.py:20
  27.0 1.9 copy-start.8
  34.5 7.7 %copy-start.4 = (bf16[1,514,384]{2,1,0:T(8,128)(2,1)S(1)}, bf16[1,514,384]{2,1,0:T(8,128)(2,1)}, u32[]{:S(2)}) copy-start(bf16[1,514,384]{2,1,0:T(8,128)(2,1)} %constant_dynamic-update-slice_fusion.16) | copy-start | bytes 1184260
  34.5 7.7 %copy-start = (bf16[5,384,384]{2,1,0:T(8,128)(2,1)S(1)}, bf16[5,384,384]{2,1,0:T(8,128)(2,1)}, u32[]{:S(2)}) copy-start(bf16[5,384,384]{2,1,0:T(8,128)(2,1)} %param.10) | copy-start | bytes 4423684
  34.5 8.1 %copy-start.5 = (f32[512,384]{1,0:T(8,128)S(1)}, f32[512,384]{1,0:T(8,128)}, u32[]{:S(2)}) copy-start(f32[512,384]{1,0:T(8,128)} %fusion.59) | copy-start | bytes 2359300
  36.4 7.7 %copy-start.6 = (bf16[1,512,384]{2,1,0:T(8,128)(2,1)}, bf16[1,512,384]{2,1,0:T(8,128)(2,1)S(1)}, u32[]{:S(2)}) copy-start(bf16[1,512,384]{2,1,0:T(8,128)(2,1)S(1)} %get-tuple-element.7) | copy-start | bytes 1179652
  37.1 19.5 %collective-permute-start.3 = (bf16[1,2,384]{2,1,0:T(2,128)(2,1)}, bf16[1,2,384]{2,1,0:T(2,128)(2,1)S(1)}, u32[]{:S(2)}, u32[]{:S(2)}) collective-permute-start(bf16[1,2,384]{2,1,0:T(2,128)(2,1)} %get-tuple-element.12), channel_id=1, source_target_pairs={{1,0},{2,1},{3,2},{4,3},{5,4},{6,5},{7,6},{8,7},{9,8},{10,9},{11,1... | collective-permute-start | bytes 4616 | tf_op jit(solution)/shard_map/ppermute | solution.py:20
  38.3 14.4 %collective-permute-start.2 = (bf16[1,2,384]{2,1,0:T(2,128)(2,1)}, bf16[1,2,384]{2,1,0:T(2,128)(2,1)S(1)}, u32[]{:S(2)}, u32[]{:S(2)}) collective-permute-start(bf16[1,2,384]{2,1,0:T(2,128)(2,1)} %get-tuple-element.13), channel_id=1, source_target_pairs={{0,1},{1,2},{2,3},{3,4},{4,5},{5,6},{6,7},{7,8},{8,9},{9,10},{10,1... | collective-permute-start | bytes 4616 | tf_op jit(solution)/shard_map/ppermute | solution.py:17
  42.7 1.0 copy-start.2
  48.5 4.3 %copy-start.3 = (bf16[1,512,384]{2,1,0:T(8,128)(2,1)S(1)}, bf16[1,512,384]{2,1,0:T(8,128)(2,1)}, u32[]{:S(2)}) copy-start(bf16[1,512,384]{2,1,0:T(8,128)(2,1)} %param.11) | copy-start | bytes 1179652
  52.7 2.5 %copy-start.7 = (bf16[1,512,384]{2,1,0:T(8,128)(2,1)S(1)}, bf16[1,512,384]{2,1,0:T(8,128)(2,1)}, u32[]{:S(2)}) copy-start(bf16[1,512,384]{2,1,0:T(8,128)(2,1)} %copy-done.6) | copy-start | bytes 1179652
  59.0 1.4 copy-start.1
  199.4 3.7 %copy-start.9 = (f32[15,4,384]{2,1,0:T(4,128)S(1)}, f32[15,4,384]{2,1,0:T(4,128)}, u32[]{:S(2)}) copy-start(f32[15,4,384]{2,1,0:T(4,128)} %get-tuple-element.19) | copy-start | bytes 276484
Sparse Core Ops, SparseCore 0:
  59.1 140.2 all-reduce.2
where the time goes:
time: 211 us
  waiting for transfers between devices  136 us (64%)
  local copies, waits for them, and re-layouts  21.4 us (10%)
  matrix products  19.3 us (9%)
  starting transfers between devices  15.2 us (7%)
  between operations  14.4 us (7%)
  other arithmetic  3.93 us (2%)
    psum x1, waiting for transfers between devices, per_device(): conv_grad = lax.psum(tap_grads, ('dp', 'context'))  136 us
    ppermute x3, starting transfers between devices, with_halo(): lax.ppermute(lax.slice_in_dim(block, block.shape[dim] - width, None, axis...  11.3 us
    unnamed x37, local copies, waits for them, and re-layouts  9.33 us
    dot_general x5, matrix products, per_device(): jnp.einsum('brc,brd->cd', gated_ext[:, offset:offset + half_rows], cotang...  6.23 us
    slice x2, local copies, waits for them, and re-layouts, per_device(): pooled = (0.5 * (active[:, 0::2] + active[:, 1::2])).astype(jnp.bfloat16)  5.54 us
    dot_general x5, matrix products, per_device(): jnp.einsum('brd,cd->brc', cot_ext[:, 4 - offset:4 - offset + half_rows],...  5.26 us
  transfers between devices with their start and end apart: 7, of which 1 were waited for; matrix products, arithmetic and copies ran while one was open for 16% of the time, Pallas kernels for 0%

commit v1 on v0

v1 whole, which is shorter than its diff:
```python
import functools
import math

import jax
import jax.numpy as jnp
from jax import lax
from jax.experimental import pallas as pl
from jax.experimental.pallas import tpu as pltpu
from jax.sharding import PartitionSpec as P

root_scale = math.sqrt(2.0 / math.pi)
cubic = 0.044715
AXES = ("dp", "context")
TAPS = 5
HALO = 6
LEAD = 16
VMEM = pl.BlockSpec(memory_space=pltpu.VMEM)
SMEM = pl.BlockSpec(memory_space=pltpu.SMEM)
bf16 = jnp.bfloat16
f32 = jnp.float32


def gelu_tanh(value):
    inner = jnp.tanh(value * (root_scale + (root_scale * cubic) * (value * value)))
    half = 0.5 * value
    return half + half * inner


def gelu_slope(value):
    square = value * value
    inner = jnp.tanh(value * (root_scale + (root_scale * cubic) * square))
    rise = (1.0 - inner * inner) * (root_scale + (3.0 * root_scale * cubic) * square)
    return 0.5 + 0.5 * inner + (0.5 * value) * rise


def rounded(value):
    return lax.reduce_precision(value, 8, 7)


def params(limit=48):
    return pltpu.CompilerParams(vmem_limit_bytes=limit * 1024 * 1024)


def first_kernel(rows, lanes, codes, place, positions, amounts, top, bottom, own, near, far):
    length = 2 * rows
    tiles = length // 128
    base = place[0]
    core = place[1]
    x = jnp.concatenate([codes[:, 128 * q : 128 * q + 128] for q in range(tiles)], axis=0)
    spot = (
        base
        + 128 * lax.broadcasted_iota(jnp.int32, x.shape, 0)
        + lax.broadcasted_iota(jnp.int32, x.shape, 1)
    )
    for v in range(positions.shape[1]):
        x = x + jnp.where(spot == positions[0, v], amounts[0, v], 0)
    x = ((x & 3) + 1).astype(f32).astype(bf16)
    source = lax.broadcasted_iota(jnp.int32, (128, 128), 0)
    target = lax.broadcasted_iota(jnp.int32, (128, 128), 1)

    def picked(parity):
        left = (source == 2 * target + parity).astype(f32).astype(bf16)
        right = (source == 2 * (target - 64) + parity).astype(f32).astype(bf16)
        low = jnp.dot(x, left, preferred_element_type=f32)
        high = jnp.dot(x, right, preferred_element_type=f32)
        parts = [low[2 * q : 2 * q + 1] + high[2 * q + 1 : 2 * q + 2] for q in range(tiles // 2)]
        return jnp.concatenate(parts + [jnp.zeros((1, lanes - rows), f32)], axis=1)

    both = jnp.concatenate([picked(0), picked(1), jnp.zeros((6, lanes), f32)], axis=0)
    lane = lax.broadcasted_iota(jnp.int32, both.shape, 1)
    shifted = pltpu.roll(both, HALO, 1)
    last = jnp.where(lane < HALO, pltpu.roll(both, lanes - (rows - HALO), 1), 0.0)
    ahead = (lane >= rows + HALO) & (lane < rows + 2 * HALO)
    first = jnp.where(ahead, pltpu.roll(both, rows + HALO, 1), 0.0)
    blank = jnp.zeros((8, lanes), f32)
    width = top.shape[1]
    pad = jnp.zeros((2, lanes - width), f32)
    rest = jnp.zeros((4, lanes), f32)

    def message(edge, cot):
        cot = jnp.concatenate([cot, pad], axis=1)
        return jnp.concatenate([edge, cot, jnp.zeros((6, lanes), f32)], axis=0)

    first_rows = top[...].astype(f32)[0:2]
    last_rows = bottom[...].astype(f32)[14:16]
    del rest
    head = message(first, first_rows)
    tail = message(last, last_rows)
    own[...] = jnp.concatenate([shifted, blank], axis=0).astype(bf16)
    near[...] = jnp.where(core == 0, tail, head).astype(bf16)
    far[...] = jnp.where(core == 0, head, tail).astype(bf16)


def weight_kernel(weight, out):
    width = weight.shape[2]
    zero = jnp.zeros((1, width), f32)
    taps = weight.shape[0]

    def rows(order):
        return jnp.concatenate(
            [
                zero if k is None else weight[k, a : a + 1, :]
                for a in range(4)
                for k in order
            ],
            axis=0,
        )

    even = [None] + list(range(taps - 2, 0, -2)) + list(range(taps - 1, -1, -2))
    odd = list(range(taps - 1, -1, -2)) + list(range(taps - 2, 0, -2)) + [None]
    full = jnp.concatenate([rows(even), rows(odd)], axis=1)
    high = full.astype(bf16)
    left = full - high.astype(f32)
    middle = left.astype(bf16)
    low = (left - middle.astype(f32)).astype(bf16)
    out[...] = jnp.concatenate([high, middle, low], axis=0)


def one_hot(codes, lanes, shift):
    even = jnp.broadcast_to(codes[0:1], (8, lanes))
    odd = jnp.broadcast_to(codes[1:2], (8, lanes))
    even = pltpu.roll(even, (2 * lanes - 8 + shift) % lanes, 1, stride=1, stride_axis=0)
    odd = pltpu.roll(odd, (2 * lanes - 7 + shift) % lanes, 1, stride=1, stride_axis=0)
    near = jnp.concatenate([even, odd], axis=0)
    return jnp.concatenate([(near == a + 1.0).astype(f32) for a in range(4)], axis=0).astype(bf16)


def conv_kernel(rows, total, place, own, near, far, weight, cot, out, stem, gated):
    lanes = own.shape[1]
    used = rows + 128
    width = cot.shape[1]
    codes = (own[...].astype(f32) + near[...].astype(f32) + far[...].astype(f32))[0:8]
    hot = one_hot(codes, lanes, 0)[:, :used]
    hot = jnp.concatenate([hot, hot, hot], axis=0)
    stem[...] = lax.dot_general(
        weight[...], hot, (((0,), (0,)), ((), ())), preferred_element_type=f32
    )
    spot = place[2] - 2 + lax.broadcasted_iota(jnp.int32, (1, used), 1)
    inside = (spot >= 0) & (spot < total)
    step = 16
    for c in range(0, width, step):
        even = gelu_tanh(stem[c : c + step, :])
        odd = gelu_tanh(stem[width + c : width + c + step, :])
        pooled = (0.5 * (even + odd)).astype(bf16).astype(f32)
        value = jnp.where(inside, gelu_tanh(pooled), 0.0)
        for t in range(TAPS):
            moved = value if t == 0 else pltpu.roll(value, used - t, 1)
            gated[t * width + c : t * width + c + step, :] = moved[:, :rows].astype(bf16)
    out[...] = jnp.dot(gated[...], cot[...], preferred_element_type=f32).astype(bf16)


def back_kernel(
    rows, total, place, own, near, far, weight, conv, cot, d_pooled, stem_part, gated, pooled, stem, ext
):
    lanes = own.shape[1]
    width = cot.shape[1]
    padded = rows + 2 * LEAD
    core = place[1]
    near_v = near[...].astype(f32)
    far_v = far[...].astype(f32)
    codes = (own[...].astype(f32) + near_v + far_v)[0:8]
    hot = one_hot(codes, lanes, LEAD - 2)[:, :padded]
    hot = jnp.concatenate([hot, hot, hot], axis=0)
    stem[...] = lax.dot_general(
        hot, weight[...], (((0,), (0,)), ((), ())), preferred_element_type=f32
    )
    before = jnp.where(core == 0, far_v, near_v)[8:10, :width]
    after = jnp.where(core == 0, near_v, far_v)[8:10, :width]
    gap = jnp.zeros((LEAD - 2, width), f32)
    ext[0:LEAD, :] = jnp.concatenate([gap, before], axis=0).astype(bf16)
    ext[LEAD : LEAD + rows, :] = cot[...]
    ext[LEAD + rows :, :] = jnp.concatenate([after, gap], axis=0).astype(bf16)
    step = 128
    mine = one_hot(codes, lanes, lanes - 2)
    acc = jnp.zeros((64, 2 * width), f32)
    for edge in (0, LEAD + rows):
        act = 0.5 * (
            gelu_tanh(stem[edge : edge + LEAD, :width]) + gelu_tanh(stem[edge : edge + LEAD, width:])
        )
        act = act.astype(bf16).astype(f32)
        spot = place[2] - LEAD + edge + lax.broadcasted_iota(jnp.int32, (LEAD, 1), 0)
        inside = (spot >= 0) & (spot < total)
        gated[edge : edge + LEAD, :] = jnp.where(inside, gelu_tanh(act), 0.0).astype(bf16)
    for r in range(0, rows, step):
        back = jnp.zeros((step, width), f32)
        for t in range(TAPS):
            start = LEAD + 2 - t + r
            back = back + lax.dot_general(
                ext[start : start + step, :],
                conv[t],
                (((1,), (1,)), ((), ())),
                preferred_element_type=f32,
            )
        even = stem[LEAD + r : LEAD + r + step, :width]
        odd = stem[LEAD + r : LEAD + r + step, width:]
        low = (0.5 * (gelu_tanh(even) + gelu_tanh(odd))).astype(bf16)
        value = low.astype(f32)
        pooled[r : r + step, :] = low
        gated[LEAD + r : LEAD + r + step, :] = gelu_tanh(value).astype(bf16)
        grad = cot[r : r + step, :].astype(f32) + back * gelu_slope(value)
        d_pooled[r : r + step, :] = grad.astype(bf16)
        half = 0.5 * grad
        terms = jnp.concatenate([half * gelu_slope(even), half * gelu_slope(odd)], axis=1)
        acc = acc + jnp.dot(mine[:, r : r + step], terms.astype(bf16), preferred_element_type=f32)
    stem_part[...] = acc


def feature_kernel(rows, gated, pooled, conv, out):
    step = 128
    for r in range(0, rows, step):
        acc = pooled[r : r + step, :].astype(f32)
        for t in range(TAPS):
            start = LEAD - 2 + t + r
            acc = acc + jnp.dot(gated[start : start + step, :], conv[t], preferred_element_type=f32)
        out[r : r + step, :] = acc.astype(bf16)


def stem_rows(part, taps, width):
    grid = part.reshape(4, 16, 2 * width)
    even, odd = grid[:, :, :width], grid[:, :, width:]
    place_even = [None] + list(range(taps - 2, 0, -2)) + list(range(taps - 1, -1, -2))
    place_odd = list(range(taps - 1, -1, -2)) + list(range(taps - 2, 0, -2)) + [None]
    return jnp.stack(
        [even[:, place_even.index(k)] + odd[:, place_odd.index(k)] for k in range(taps)], axis=0
    )


def per_device(codes, variant_pos, variant_shift, stem_weight, conv_weight, cotangent):
    n_dp, n_ctx = lax.axis_size("dp"), lax.axis_size("context")
    devices = n_dp * n_ctx
    length = codes.shape[1]
    rows = length // 2
    taps, _, width = stem_weight.shape
    total = rows * n_ctx
    lanes = -(-(rows + 256) // 128) * 128
    ctx = lax.axis_index("context")
    rank = lax.axis_index("dp") * n_ctx + ctx
    core = ctx % 2
    place = jnp.stack([ctx * length, core, ctx * rows]).astype(jnp.int32)
    cot = cotangent[0]

    own, near, far = pl.pallas_call(
        functools.partial(first_kernel, rows, lanes),
        grid=(1,),
        out_shape=[jax.ShapeDtypeStruct((16, lanes), bf16)] * 3,
        in_specs=[
            pl.BlockSpec((1, length), lambda i: (0, 0)),
            SMEM,
            SMEM,
            SMEM,
            pl.BlockSpec((16, width), lambda i: (0, 0)),
            pl.BlockSpec((16, width), lambda i: (rows // 16 - 1, 0)),
        ],
        out_specs=[pl.BlockSpec((16, lanes), lambda i: (0, 0))] * 3,
        compiler_params=params(),
    )(codes, place, variant_pos, variant_shift, cot, cot)

    def swap(value, even_bit, odd_bit):
        pairs = [(i, i ^ (odd_bit if i & 1 else even_bit)) for i in range(devices)]
        return lax.ppermute(value, AXES, pairs)

    def bit(even_bit, odd_bit):
        return (rank // jnp.where(core == 1, odd_bit, even_bit)) % 2

    outward = []
    for d in range(n_dp):
        for c in range(n_ctx):
            other = c + 1 if c & 1 else c - 1
            if 0 <= other < n_ctx:
                outward.append((d * n_ctx + c, d * n_ctx + other))
    near = swap(near, 1, 1)
    far = lax.ppermute(far, AXES, outward)

    weight = pl.pallas_call(
        weight_kernel,
        out_shape=jax.ShapeDtypeStruct((192, 2 * width), bf16),
        in_specs=[VMEM],
        out_specs=VMEM,
        compiler_params=params(),
    )(stem_weight)

    part = pl.pallas_call(
        functools.partial(conv_kernel, rows, total),
        out_shape=jax.ShapeDtypeStruct((TAPS * width, width), bf16),
        in_specs=[SMEM] + [VMEM] * 5,
        out_specs=VMEM,
        scratch_shapes=[
            pltpu.VMEM((2 * width, rows + 128), f32),
            pltpu.VMEM((TAPS * width, rows), bf16),
        ],
        compiler_params=params(),
    )(place, own, near, far, weight, cot)

    padded = rows + 2 * LEAD
    d_pooled, stem_part, gated, pooled = pl.pallas_call(
        functools.partial(back_kernel, rows, total),
        out_shape=[
            jax.ShapeDtypeStruct((rows, width), bf16),
            jax.ShapeDtypeStruct((64, 2 * width), f32),
            jax.ShapeDtypeStruct((padded, width), bf16),
            jax.ShapeDtypeStruct((rows, width), bf16),
        ],
        in_specs=[SMEM] + [VMEM] * 6,
        out_specs=[VMEM] * 4,
        scratch_shapes=[
            pltpu.VMEM((padded, 2 * width), f32),
            pltpu.VMEM((padded, width), bf16),
        ],
        compiler_params=params(),
        cost_estimate=pl.CostEstimate(
            flops=2 * TAPS * rows * width * width, bytes_accessed=4 << 20, transcendentals=0
        ),
    )(place, own, near, far, weight, conv_weight, cot)

    features = pl.pallas_call(
        functools.partial(feature_kernel, rows),
        out_shape=jax.ShapeDtypeStruct((rows, width), bf16),
        in_specs=[VMEM] * 3,
        out_specs=VMEM,
        compiler_params=params(),
        cost_estimate=pl.CostEstimate(
            flops=2 * TAPS * rows * width * width, bytes_accessed=4 << 20, transcendentals=0
        ),
    )(gated, pooled, conv_weight)

    x_bit, y_bit = 2, n_ctx
    split = [(1, 1), (x_bit, y_bit), (y_bit, x_bit)]
    others = [1 << k for k in range(devices.bit_length() - 1) if (1 << k) not in (1, x_bit, y_bit)]
    value = part.astype(f32)
    size = value.shape[0]
    for pair in split:
        size //= 2
        which = bit(*pair)
        low = value.astype(bf16)
        sent = lax.dynamic_slice_in_dim(low, (1 - which) * size, size, 0)
        kept = lax.dynamic_slice_in_dim(low, which * size, size, 0)
        value = kept.astype(f32) + swap(sent, *pair).astype(f32)
    stem_sum = stem_rows(stem_part, taps, width).reshape(4 * taps, width)
    for b in others:
        both = rounded(jnp.concatenate([value, stem_sum], axis=0))
        both = both + swap(both.astype(bf16), b, b).astype(f32)
        value, stem_sum = both[:size], both[size:]
    value = value.astype(bf16)
    for pair in split[::-1]:
        stem_sum = rounded(stem_sum)
        got = swap(jnp.concatenate([value, stem_sum.astype(bf16)], axis=0), *pair)
        stem_sum = stem_sum + got[size:].astype(f32)
        got = got[:size]
        which = bit(*pair)
        value = jnp.where(
            which == 0, jnp.concatenate([value, got], axis=0), jnp.concatenate([got, value], axis=0)
        )
        size *= 2
    conv_grad = value.astype(f32).reshape(TAPS, width, width)
    stem_grad = stem_sum.reshape(taps, 4, width)
    return (features[None], d_pooled[None], conv_grad, stem_grad)


def solution(mesh):
    placed = (P("dp", "context"), P("dp", None), P("dp", None), P(), P(), P("dp", "context", None))
    return jax.shard_map(
        per_device,
        mesh=mesh,
        in_specs=placed,
        out_specs=(P("dp", "context", None), P("dp", "context", None), P(), P()),
        check_vma=False,
    )
```

time: 211 us -> 82.4 us (0.39)
  waiting for transfers between devices: 136 us -> 36 us
  matrix products: 19.3 us -> 0 us
  between operations: 14.4 us -> 1.06 us
  local copies, waits for them, and re-layouts: 21.4 us -> 9.82 us
  Pallas kernels: 0 us -> 10.6 us
  starting transfers between devices: 15.2 us -> 17.9 us
  other arithmetic: 3.93 us -> 6.59 us
    psum x1 -> x0, waiting for transfers between devices: 136 us -> none  [per_device(): conv_grad = lax.psum(tap_grads, ('dp', 'context'))]
    ppermute x6 -> x10, waiting for transfers between devices: 0.02 us -> 36 us  [the longest x9 36 us: swap(): return lax.ppermute(value, AXES, pairs)]
    dot_general x17 -> x0, matrix products: 19.3 us -> none  [the longest x5 6.23 us: per_device(): jnp.einsum('brc,brd->cd', gated_ext[:, offset:offset + half_rows], cotang...]
    pallas_call x0 -> x5, Pallas kernels: none -> 10.6 us  [the longest x1 4.67 us: per_device(): pl.pallas_call(functools.partial(back_kernel, rows, total), out_shape=[ja...]
    slice x5 -> x6, local copies, waits for them, and re-layouts: 7.54 us -> 1.41 us  [the longest x3 1.25 us: per_device(): got = got[:size]]
    ppermute x6 -> x10, starting transfers between devices: 15.2 us -> 17.9 us  [the longest x9 17.2 us: swap(): return lax.ppermute(value, AXES, pairs)]
    mul x1 -> x0, local copies, waits for them, and re-layouts: 2.22 us -> none  [per_device(): dstem = 0.5 * jnp.repeat(dpool, 2, axis=1) * gelu_slope(stem)]
    unnamed x37 -> x22, local copies, waits for them, and re-layouts: 9.33 us -> 7.55 us
  transfers between devices with their start and end apart: 7 -> 10, of which waited for: 1 -> 8; matrix products, arithmetic and copies ran while one was open for 16% -> 0% of each run, Pallas kernels for 0% -> 3%
where the time goes in v1:
time: 82.4 us; the launch traced here: 82 us
  waiting for transfers between devices  36 us (44%)
  starting transfers between devices  17.9 us (22%)
  Pallas kernels  10.6 us (13%)
  local copies, waits for them, and re-layouts  9.82 us (12%)
  other arithmetic  6.59 us (8%)
  between operations  1.06 us (1%)
    ppermute x9, waiting for transfers between devices, swap(): return lax.ppermute(value, AXES, pairs)  36 us
    ppermute x9, starting transfers between devices, swap(): return lax.ppermute(value, AXES, pairs)  17.2 us
    unnamed x22, local copies, waits for them, and re-layouts  7.55 us
    pallas_call x1, Pallas kernels, per_device(): pl.pallas_call(functools.partial(back_kernel, rows, total), out_shape=[ja...  4.67 us
    pallas_call x1, Pallas kernels, per_device(): pl.pallas_call(functools.partial(conv_kernel, rows, total), out_shape=jax...  2.71 us
    pallas_call x1, Pallas kernels, per_device(): pl.pallas_call(functools.partial(feature_kernel, rows), out_shape=jax.Sha...  2.27 us
    convert_element_type x1, other arithmetic, per_device(): conv_grad = value.astype(f32).reshape(TAPS, width, width)  1.81 us
  transfers between devices with their start and end apart: 10, of which 8 were waited for; matrix products, arithmetic and copies ran while one was open for 0% of the time, Pallas kernels for 3%

profile of v1, /device:TPU:0, one launch (start us, length us, event | category | flops | bytes accessed | tf_op | source)
XLA Modules:
  0.0 82.0 jit_solution(9691604114636957206)
XLA Ops:
  0.7 1.0 %copy-done = bf16[1,512,384]{2,1,0:T(8,128)(2,1)S(1)} copy-done((bf16[1,512,384]{2,1,0:T(8,128)(2,1)S(1)}, bf16[1,512,384]{2,1,0:T(8,128)(2,1)}, u32[]{:S(2)}) %copy-start) | copy-done | bytes 393240
  6.9 1.0 %copy-done.1 = bf16[1,512,384]{2,1,0:T(8,128)(2,1)S(1)} copy-done((bf16[1,512,384]{2,1,0:T(8,128)(2,1)S(1)}, bf16[1,512,384]{2,1,0:T(8,128)(2,1)}, u32[]{:S(2)}) %copy-start.1) | copy-done | bytes 393240
  7.9 1.4 %copy-done.6 = bf16[5,384,384]{2,1,0:T(8,128)(2,1)S(1)} copy-done((bf16[5,384,384]{2,1,0:T(8,128)(2,1)S(1)}, bf16[5,384,384]{2,1,0:T(8,128)(2,1)}, u32[]{:S(2)}) %copy-start.6) | copy-done | bytes 1474584
  9.2 4.7 %shard_map.95 = (bf16[512,384]{1,0:T(8,128)(2,1)}, f32[64,768]{1,0:T(8,128)S(1)}, bf16[544,384]{1,0:T(8,128)(2,1)S(1)}, bf16[512,384]{1,0:T(8,128)(2,1)S(1)}) custom-call(s32[3]{0:T(128)S(1)} %pad_add_fusion.place, bf16[16,768]{1,0:T(8,128)(2,1)S(1)} %get-tuple-element.11.own, bf16[16,768]{1,0:T(8,128)(2,1)S(1)} %collective-permute-done.near, ...), custom_call_target="tpu_custom_call" | custom-call | flops 754974720 | bytes 4194304 | tf_op jit(solution)/shard_map/pallas_call | solution.py:295
  14.0 2.7 %shard_map.97 = bf16[1920,384]{1,0:T(8,128)(2,1)S(1)} custom-call(s32[3]{0:T(128)S(1)} %pad_add_fusion.place, bf16[16,768]{1,0:T(8,128)(2,1)S(1)} %get-tuple-element.11.own, bf16[16,768]{1,0:T(8,128)(2,1)S(1)} %collective-permute-done.near, bf16[16,768]{1,0:T(8,128)(2,1)S(1)} %collective-permute-done.1.far, bf16[192,768]{1,0:T(8,128)(2,1)S(1)} %shard_map.94.weight, ...), custom_call_target="tpu_custom_call" | custom-call | tf_op jit(solution)/shard_map/pallas_call | solution.py:282
  16.9 4.3 %collective-permute-start.2 = (bf16[960,384]{1,0:T(8,128)(2,1)S(1)}, bf16[960,384]{1,0:T(8,128)(2,1)S(1)}, u32[]{:S(2)}, u32[]{:S(2)}) collective-permute-start(bf16[960,384]{1,0:T(8,128)(2,1)S(1)} %constant_dynamic-slice_fusion.2), channel_id=1, source_target_pairs={{0,1},{1,0},{2,3},{3,2},{4,5},{5,4},{6,7},{7,6},{8,9},{9,8},{10,11... | collective-permute-start | bytes 2211848 | tf_op jit(solution)/shard_map/ppermute | solution.py:260
  21.3 1.7 %collective-permute-done.2 = bf16[960,384]{1,0:T(8,128)(2,1)S(1)} collective-permute-done((bf16[960,384]{1,0:T(8,128)(2,1)S(1)}, bf16[960,384]{1,0:T(8,128)(2,1)S(1)}, u32[]{:S(2)}, u32[]{:S(2)}) %collective-permute-start.2) | collective-permute-done | bytes 737312 | tf_op jit(solution)/shard_map/ppermute | solution.py:260
  23.2 3.1 %collective-permute-start.3 = (bf16[480,384]{1,0:T(8,128)(2,1)S(1)}, bf16[480,384]{1,0:T(8,128)(2,1)S(1)}, u32[]{:S(2)}, u32[]{:S(2)}) collective-permute-start(bf16[480,384]{1,0:T(8,128)(2,1)S(1)} %constant_dynamic-slice_fusion.1), channel_id=1, source_target_pairs={{0,2},{1,17},{2,0},{3,19},{4,6},{5,21},{6,4},{7,23},{8,10},{9,25},... | collective-permute-start | bytes 1105928 | tf_op jit(solution)/shard_map/ppermute | solution.py:260
  26.3 5.5 %collective-permute-done.3 = bf16[480,384]{1,0:T(8,128)(2,1)S(1)} collective-permute-done((bf16[480,384]{1,0:T(8,128)(2,1)S(1)}, bf16[480,384]{1,0:T(8,128)(2,1)S(1)}, u32[]{:S(2)}, u32[]{:S(2)}) %collective-permute-start.3) | collective-permute-done | bytes 368672 | tf_op jit(solution)/shard_map/ppermute | solution.py:260
  31.9 1.6 %collective-permute-start.4 = (bf16[240,384]{1,0:T(8,128)(2,1)S(1)}, bf16[240,384]{1,0:T(8,128)(2,1)S(1)}, u32[]{:S(2)}, u32[]{:S(2)}) collective-permute-start(bf16[240,384]{1,0:T(8,128)(2,1)S(1)} %constant_dynamic-slice_fusion), channel_id=1, source_target_pairs={{0,16},{1,3},{2,18},{3,1},{4,20},{5,7},{6,22},{7,5},{8,24},{9,11},... | collective-permute-start | bytes 552968 | tf_op jit(solution)/shard_map/ppermute | solution.py:260
  33.5 4.0 %collective-permute-done.4 = bf16[240,384]{1,0:T(8,128)(2,1)S(1)} collective-permute-done((bf16[240,384]{1,0:T(8,128)(2,1)S(1)}, bf16[240,384]{1,0:T(8,128)(2,1)S(1)}, u32[]{:S(2)}, u32[]{:S(2)}) %collective-permute-start.4) | collective-permute-done | bytes 184352 | tf_op jit(solution)/shard_map/ppermute | solution.py:260
  37.6 2.1 %collective-permute-start.5 = (bf16[300,384]{1,0:T(8,128)(2,1)S(1)}, bf16[300,384]{1,0:T(8,128)(2,1)S(1)}, u32[]{:S(2)}, u32[]{:S(2)}) collective-permute-start(bf16[300,384]{1,0:T(8,128)(2,1)S(1)} %fusion), channel_id=1, source_target_pairs={{0,4},{1,5},{2,6},{3,7},{4,0},{5,1},{6,2},{7,3},{8,12},{9,13},{10,... | collective-permute-start | bytes 691208 | tf_op jit(solution)/shard_map/ppermute | solution.py:260
  39.7 4.5 %collective-permute-done.5 = bf16[300,384]{1,0:T(8,128)(2,1)S(1)} collective-permute-done((bf16[300,384]{1,0:T(8,128)(2,1)S(1)}, bf16[300,384]{1,0:T(8,128)(2,1)S(1)}, u32[]{:S(2)}, u32[]{:S(2)}) %collective-permute-start.5) | collective-permute-done | bytes 230432 | tf_op jit(solution)/shard_map/ppermute | solution.py:260
  44.3 2.7 %collective-permute-start.6 = (bf16[300,384]{1,0:T(8,128)(2,1)S(1)}, bf16[300,384]{1,0:T(8,128)(2,1)S(1)}, u32[]{:S(2)}, u32[]{:S(2)}) collective-permute-start(bf16[300,384]{1,0:T(8,128)(2,1)S(1)} %fusion.1), channel_id=1, source_target_pairs={{0,8},{1,9},{2,10},{3,11},{4,12},{5,13},{6,14},{7,15},{8,0},{9,1},... | collective-permute-start | bytes 691208 | tf_op jit(solution)/shard_map/ppermute | solution.py:260
  46.9 8.9 %collective-permute-done.6 = bf16[300,384]{1,0:T(8,128)(2,1)S(1)} collective-permute-done((bf16[300,384]{1,0:T(8,128)(2,1)S(1)}, bf16[300,384]{1,0:T(8,128)(2,1)S(1)}, u32[]{:S(2)}, u32[]{:S(2)}) %collective-permute-start.6) | collective-permute-done | bytes 230432 | tf_op jit(solution)/shard_map/ppermute | solution.py:260
  56.1 1.6 %collective-permute-start.7 = (bf16[300,384]{1,0:T(8,128)(2,1)S(1)}, bf16[300,384]{1,0:T(8,128)(2,1)S(1)}, u32[]{:S(2)}, u32[]{:S(2)}) collective-permute-start(bf16[300,384]{1,0:T(8,128)(2,1)S(1)} %pad_maximum_fusion.2), channel_id=1, source_target_pairs={{0,16},{1,3},{2,18},{3,1},{4,20},{5,7},{6,22},{7,5},{8,24},{9,11},... | collective-permute-start | bytes 691208 | tf_op jit(solution)/shard_map/ppermute | solution.py:260
  57.7 4.5 %collective-permute-done.7 = bf16[300,384]{1,0:T(8,128)(2,1)S(1)} collective-permute-done((bf16[300,384]{1,0:T(8,128)(2,1)S(1)}, bf16[300,384]{1,0:T(8,128)(2,1)S(1)}, u32[]{:S(2)}, u32[]{:S(2)}) %collective-permute-start.7) | collective-permute-done | bytes 230432 | tf_op jit(solution)/shard_map/ppermute | solution.py:260
  63.0 1.5 %collective-permute-start.8 = (bf16[540,384]{1,0:T(8,128)(2,1)S(1)}, bf16[540,384]{1,0:T(8,128)(2,1)S(1)}, u32[]{:S(2)}, u32[]{:S(2)}) collective-permute-start(bf16[540,384]{1,0:T(8,128)(2,1)S(1)} %pad_maximum_fusion.1), channel_id=1, source_target_pairs={{0,2},{1,17},{2,0},{3,19},{4,6},{5,21},{6,4},{7,23},{8,10},{9,25},... | collective-permute-start | bytes 1244168 | tf_op jit(solution)/shard_map/ppermute | solution.py:260
  64.5 6.6 %collective-permute-done.8 = bf16[540,384]{1,0:T(8,128)(2,1)S(1)} collective-permute-done((bf16[540,384]{1,0:T(8,128)(2,1)S(1)}, bf16[540,384]{1,0:T(8,128)(2,1)S(1)}, u32[]{:S(2)}, u32[]{:S(2)}) %collective-permute-start.8) | collective-permute-done | bytes 414752 | tf_op jit(solution)/shard_map/ppermute | solution.py:260
  72.2 1.1 %fusion.3 = bf16[60,384]{1,0:T(8,128)(2,1)S(1)} fusion(bf16[540,384]{1,0:T(8,128)(2,1)} %copy-done.9, bf16[300,384]{1,0:T(8,128)(2,1)} %copy-done.10, f32[300,384]{1,0:T(8,128)} %copy-done.8), kind=kLoop, calls=%fused_computation.20 | loop fusion | flops 184320 | bytes 230400 | tf_op jit(solution)/shard_map/convert_element_type | solution.py:346
  74.3 2.3 %shard_map.96 = bf16[512,384]{1,0:T(8,128)(2,1)} custom-call(bf16[544,384]{1,0:T(8,128)(2,1)S(1)} %get-tuple-element.14.gated, bf16[512,384]{1,0:T(8,128)(2,1)S(1)} %get-tuple-element.15.pooled, bf16[5,384,384]{2,1,0:T(8,128)(2,1)S(1)} %copy-done.7), custom_call_target="tpu_custom_call" | custom-call | flops 754974720 | bytes 4194304 | tf_op jit(solution)/shard_map/pallas_call | solution.py:315
  76.9 1.0 %convert_add_fusion.2 = f32[60,384]{1,0:T(8,128)S(1)} fusion(bf16[1020,384]{1,0:T(8,128)(2,1)} %collective-permute-done.9, bf16[540,384]{1,0:T(8,128)(2,1)} %copy-done.9, bf16[300,384]{1,0:T(8,128)(2,1)} %copy-done.10, f32[300,384]{1,0:T(8,128)} %copy-done.8), kind=kLoop, calls=%fused_computation.16 | loop fusion | flops 207360 | bytes 322560 | tf_op jit(solution)/shard_map/add | solution.py:347
  78.6 1.2 %slice.224 = bf16[960,384]{1,0:T(8,128)(2,1)S(1)} slice(bf16[1020,384]{1,0:T(8,128)(2,1)} %collective-permute-done.9), slice={[0:960], [0:384]} | slice | bytes 1474560 | tf_op jit(solution)/shard_map/slice | solution.py:348
  80.2 1.8 %convert.5 = f32[5,384,384]{2,1,0:T(8,128)} convert(bf16[5,384,384]{2,1,0:T(8,128)(2,1)S(1)} %bitcast.75) | non-fusion elementwise | flops 737280 | bytes 4423680 | tf_op jit(solution)/shard_map/convert_element_type | solution.py:354
  (67 shorter events, 10.3 us)
Async XLA Ops:
  0.7 1.0 %copy-start = (bf16[1,512,384]{2,1,0:T(8,128)(2,1)S(1)}, bf16[1,512,384]{2,1,0:T(8,128)(2,1)}, u32[]{:S(2)}) copy-start(bf16[1,512,384]{2,1,0:T(8,128)(2,1)} %param.11) | copy-start | bytes 1179652
  1.7 0.7 copy-start.3
  2.4 0.7 copy-start.4
  3.1 0.7 copy-start.5
  4.6 2.3 %collective-permute-start = (bf16[16,768]{1,0:T(8,128)(2,1)S(1)}, bf16[16,768]{1,0:T(8,128)(2,1)S(1)}, u32[]{:S(2)}, u32[]{:S(2)}) collective-permute-start(bf16[16,768]{1,0:T(8,128)(2,1)S(1)} %get-tuple-element.12), channel_id=1, source_target_pairs={{0,1},{1,0},{2,3},{3,2},{4,5},{5,4},{6,7},{7,6},{8,9},{9,8},{10,11... | collective-permute-start | bytes 73736 | tf_op jit(solution)/shard_map/ppermute | solution.py:260
  5.0 1.8 %collective-permute-start.1 = (bf16[16,768]{1,0:T(8,128)(2,1)S(1)}, bf16[16,768]{1,0:T(8,128)(2,1)S(1)}, u32[]{:S(2)}, u32[]{:S(2)}) collective-permute-start(bf16[16,768]{1,0:T(8,128)(2,1)S(1)} %get-tuple-element.13), channel_id=1, source_target_pairs={{1,2},{2,1},{3,4},{4,3},{5,6},{6,5},{7,8},{8,7},{9,10},{10,9},{11,... | collective-permute-start | bytes 73736 | tf_op jit(solution)/shard_map/ppermute | solution.py:272
  5.8 0.9 %copy-start.2 = (f32[15,4,384]{2,1,0:T(4,128)S(1)}, f32[15,4,384]{2,1,0:T(4,128)}, u32[]{:S(2)}) copy-start(f32[15,4,384]{2,1,0:T(4,128)} %weight.1) | copy-start | bytes 276484
  6.9 1.0 %copy-start.1 = (bf16[1,512,384]{2,1,0:T(8,128)(2,1)S(1)}, bf16[1,512,384]{2,1,0:T(8,128)(2,1)}, u32[]{:S(2)}) copy-start(bf16[1,512,384]{2,1,0:T(8,128)(2,1)} %param.11) | copy-start | bytes 1179652
  7.9 1.4 %copy-start.6 = (bf16[5,384,384]{2,1,0:T(8,128)(2,1)S(1)}, bf16[5,384,384]{2,1,0:T(8,128)(2,1)}, u32[]{:S(2)}) copy-start(bf16[5,384,384]{2,1,0:T(8,128)(2,1)} %conv.3) | copy-start | bytes 4423684
  16.9 6.1 %collective-permute-start.2 = (bf16[960,384]{1,0:T(8,128)(2,1)S(1)}, bf16[960,384]{1,0:T(8,128)(2,1)S(1)}, u32[]{:S(2)}, u32[]{:S(2)}) collective-permute-start(bf16[960,384]{1,0:T(8,128)(2,1)S(1)} %constant_dynamic-slice_fusion.2), channel_id=1, source_target_pairs={{0,1},{1,0},{2,3},{3,2},{4,5},{5,4},{6,7},{7,6},{8,9},{9,8},{10,11... | collective-permute-start | bytes 2211848 | tf_op jit(solution)/shard_map/ppermute | solution.py:260
  23.2 8.6 %collective-permute-start.3 = (bf16[480,384]{1,0:T(8,128)(2,1)S(1)}, bf16[480,384]{1,0:T(8,128)(2,1)S(1)}, u32[]{:S(2)}, u32[]{:S(2)}) collective-permute-start(bf16[480,384]{1,0:T(8,128)(2,1)S(1)} %constant_dynamic-slice_fusion.1), channel_id=1, source_target_pairs={{0,2},{1,17},{2,0},{3,19},{4,6},{5,21},{6,4},{7,23},{8,10},{9,25},... | collective-permute-start | bytes 1105928 | tf_op jit(solution)/shard_map/ppermute | solution.py:260
  31.9 5.6 %collective-permute-start.4 = (bf16[240,384]{1,0:T(8,128)(2,1)S(1)}, bf16[240,384]{1,0:T(8,128)(2,1)S(1)}, u32[]{:S(2)}, u32[]{:S(2)}) collective-permute-start(bf16[240,384]{1,0:T(8,128)(2,1)S(1)} %constant_dynamic-slice_fusion), channel_id=1, source_target_pairs={{0,16},{1,3},{2,18},{3,1},{4,20},{5,7},{6,22},{7,5},{8,24},{9,11},... | collective-permute-start | bytes 552968 | tf_op jit(solution)/shard_map/ppermute | solution.py:260
  37.6 6.6 %collective-permute-start.5 = (bf16[300,384]{1,0:T(8,128)(2,1)S(1)}, bf16[300,384]{1,0:T(8,128)(2,1)S(1)}, u32[]{:S(2)}, u32[]{:S(2)}) collective-permute-start(bf16[300,384]{1,0:T(8,128)(2,1)S(1)} %fusion), channel_id=1, source_target_pairs={{0,4},{1,5},{2,6},{3,7},{4,0},{5,1},{6,2},{7,3},{8,12},{9,13},{10,... | collective-permute-start | bytes 691208 | tf_op jit(solution)/shard_map/ppermute | solution.py:260
  44.3 11.6 %collective-permute-start.6 = (bf16[300,384]{1,0:T(8,128)(2,1)S(1)}, bf16[300,384]{1,0:T(8,128)(2,1)S(1)}, u32[]{:S(2)}, u32[]{:S(2)}) collective-permute-start(bf16[300,384]{1,0:T(8,128)(2,1)S(1)} %fusion.1), channel_id=1, source_target_pairs={{0,8},{1,9},{2,10},{3,11},{4,12},{5,13},{6,14},{7,15},{8,0},{9,1},... | collective-permute-start | bytes 691208 | tf_op jit(solution)/shard_map/ppermute | solution.py:260
  56.0 7.0 %copy-start.8 = (f32[300,384]{1,0:T(8,128)}, f32[300,384]{1,0:T(8,128)S(1)}, u32[]{:S(2)}) copy-start(f32[300,384]{1,0:T(8,128)S(1)} %convert_add_fusion) | copy-start | bytes 1382404
  56.1 6.1 %collective-permute-start.7 = (bf16[300,384]{1,0:T(8,128)(2,1)S(1)}, bf16[300,384]{1,0:T(8,128)(2,1)S(1)}, u32[]{:S(2)}, u32[]{:S(2)}) collective-permute-start(bf16[300,384]{1,0:T(8,128)(2,1)S(1)} %pad_maximum_fusion.2), channel_id=1, source_target_pairs={{0,16},{1,3},{2,18},{3,1},{4,20},{5,7},{6,22},{7,5},{8,24},{9,11},... | collective-permute-start | bytes 691208 | tf_op jit(solution)/shard_map/ppermute | solution.py:260
  62.2 0.7 copy-start.10
  63.0 8.1 %collective-permute-start.8 = (bf16[540,384]{1,0:T(8,128)(2,1)S(1)}, bf16[540,384]{1,0:T(8,128)(2,1)S(1)}, u32[]{:S(2)}, u32[]{:S(2)}) collective-permute-start(bf16[540,384]{1,0:T(8,128)(2,1)S(1)} %pad_maximum_fusion.1), channel_id=1, source_target_pairs={{0,2},{1,17},{2,0},{3,19},{4,6},{5,21},{6,4},{7,23},{8,10},{9,25},... | collective-permute-start | bytes 1244168 | tf_op jit(solution)/shard_map/ppermute | solution.py:260
  71.1 0.8 copy-start.9
  71.9 2.4 %copy-start.7 = (bf16[5,384,384]{2,1,0:T(8,128)(2,1)S(1)}, bf16[5,384,384]{2,1,0:T(8,128)(2,1)}, u32[]{:S(2)}) copy-start(bf16[5,384,384]{2,1,0:T(8,128)(2,1)} %conv.3) | copy-start | bytes 4423684
  74.3 2.6 %collective-permute-start.9 = (bf16[1020,384]{1,0:T(8,128)(2,1)}, bf16[1020,384]{1,0:T(8,128)(2,1)}, u32[]{:S(2)}, u32[]{:S(2)}) collective-permute-start(bf16[1020,384]{1,0:T(8,128)(2,1)} %pad_maximum_fusion), channel_id=1, source_target_pairs={{0,1},{1,0},{2,3},{3,2},{4,5},{5,4},{6,7},{7,6},{8,9},{9,8},{10,11... | collective-permute-start | bytes 2350088 | tf_op jit(solution)/shard_map/ppermute | solution.py:260

commit v2 on v1

v2 whole, which is shorter than its diff:
```python
import functools
import math

import jax
import jax.numpy as jnp
from jax import lax
from jax.experimental import pallas as pl
from jax.experimental.pallas import tpu as pltpu
from jax.sharding import PartitionSpec as P

root_scale = math.sqrt(2.0 / math.pi)
cubic = 0.044715
AXES = ("dp", "context")
TAPS = 5
HALO = 6
LEAD = 16
VMEM = pl.BlockSpec(memory_space=pltpu.VMEM)
FAR = pl.BlockSpec(memory_space=pltpu.HBM)
bf16 = jnp.bfloat16
f32 = jnp.float32


def gelu_tanh(value):
    inner = jnp.tanh(value * (root_scale + (root_scale * cubic) * (value * value)))
    half = 0.5 * value
    return half + half * inner


def gelu_both(value):
    square = value * value
    inner = jnp.tanh(value * (root_scale + (root_scale * cubic) * square))
    rise = (1.0 - inner * inner) * (root_scale + (3.0 * root_scale * cubic) * square)
    half = 0.5 * value
    return half + half * inner, 0.5 + 0.5 * inner + half * rise


def rounded(value):
    return lax.reduce_precision(value, 8, 7)


def params(limit=24):
    return pltpu.CompilerParams(vmem_limit_bytes=limit * 1024 * 1024)


def after(value, *others):
    return lax.optimization_barrier((value,) + others)[0]


def first_kernel(
    rows, lanes, codes, positions, amounts, cot, own, near, far, msg, base_v, pos_s, amt_s, top, bottom, sems
):
    length = 2 * rows
    tiles = length // 128
    width = cot.shape[1]
    copies = [
        pltpu.make_async_copy(codes, base_v, sems.at[0]),
        pltpu.make_async_copy(positions, pos_s, sems.at[1]),
        pltpu.make_async_copy(amounts, amt_s, sems.at[2]),
        pltpu.make_async_copy(cot.at[pl.ds(0, 16)], top, sems.at[3]),
        pltpu.make_async_copy(cot.at[pl.ds(rows - 16, 16)], bottom, sems.at[4]),
        pltpu.make_async_copy(cot, msg.at[pl.ds(0, rows)], sems.at[5]),
    ]
    for copy in copies:
        copy.start()
    ctx = lax.axis_index("context")
    core = lax.rem(ctx, 2)
    for copy in copies[:5]:
        copy.wait()
    x = jnp.concatenate([base_v[:, 128 * q : 128 * q + 128] for q in range(tiles)], axis=0)
    spot = (
        ctx * length
        + 128 * lax.broadcasted_iota(jnp.int32, x.shape, 0)
        + lax.broadcasted_iota(jnp.int32, x.shape, 1)
    )
    sums = [x] + [jnp.zeros_like(x)] * 3
    for v in range(positions.shape[1]):
        sums[v % 4] = sums[v % 4] + jnp.where(spot == pos_s[0, v], amt_s[0, v], 0)
    x = (sums[0] + sums[1]) + (sums[2] + sums[3])
    x = ((x & 3) + 1).astype(f32).astype(bf16)
    source = lax.broadcasted_iota(jnp.int32, (128, 128), 0)
    target = lax.broadcasted_iota(jnp.int32, (128, 128), 1)

    def picked(parity):
        left = (source == 2 * target + parity).astype(f32).astype(bf16)
        right = (source == 2 * (target - 64) + parity).astype(f32).astype(bf16)
        low = jnp.dot(x, left, preferred_element_type=f32)
        high = jnp.dot(x, right, preferred_element_type=f32)
        parts = [low[2 * q : 2 * q + 1] + high[2 * q + 1 : 2 * q + 2] for q in range(tiles // 2)]
        return jnp.concatenate(parts + [jnp.zeros((1, lanes - rows), f32)], axis=1)

    both = jnp.concatenate([picked(0), picked(1), jnp.zeros((6, lanes), f32)], axis=0)
    lane = lax.broadcasted_iota(jnp.int32, both.shape, 1)
    shifted = pltpu.roll(both, HALO, 1)
    last = jnp.where(lane < HALO, pltpu.roll(both, lanes - (rows - HALO), 1), 0.0)
    ahead = (lane >= rows + HALO) & (lane < rows + 2 * HALO)
    first = jnp.where(ahead, pltpu.roll(both, rows + HALO, 1), 0.0)
    blank = jnp.zeros((8, lanes), f32)
    pad = jnp.zeros((2, lanes - width), f32)

    def message(edge, grads):
        grads = jnp.concatenate([grads, pad], axis=1)
        return jnp.concatenate([edge, grads, jnp.zeros((6, lanes), f32)], axis=0)

    head = message(first, top[...].astype(f32)[0:2])
    tail = message(last, bottom[...].astype(f32)[14:16])
    own[...] = jnp.concatenate([shifted, blank], axis=0).astype(bf16)
    near[...] = jnp.where(core == 0, tail, head).astype(bf16)
    far[...] = jnp.where(core == 0, head, tail).astype(bf16)
    copies[5].wait()


def message_kernel(own, near, whole, msg):
    del whole
    width = msg.shape[1]
    codes = (own[...].astype(f32) + near[...].astype(f32))[0:2]
    blank = jnp.zeros((1, 2 * width - codes.shape[1]), f32)
    lines = []
    for k in range(2):
        line = codes[k : k + 1]
        if blank.shape[1]:
            line = jnp.concatenate([line, blank], axis=1)
        lines += [line[:, :width], line[:, width:]]
    lines.append(jnp.zeros((12, width), f32))
    msg[...] = jnp.concatenate(lines, axis=0).astype(bf16)


def weight_kernel(weight, out, half_out):
    width = weight.shape[2]
    zero = jnp.zeros((1, width), f32)
    even, odd = orders(weight.shape[0])

    def rows(order):
        return jnp.concatenate(
            [
                zero if k is None else weight[k, a : a + 1, :]
                for a in range(4)
                for k in order
            ],
            axis=0,
        )

    def terms(full):
        high = full.astype(bf16)
        left = full - high.astype(f32)
        middle = left.astype(bf16)
        low = (left - middle.astype(f32)).astype(bf16)
        return jnp.concatenate([high, middle, low], axis=0)

    evens, odds = rows(even), rows(odd)
    half = width // 2
    upper = lax.rem(lax.axis_index("dp"), 2) == 1
    out[...] = terms(jnp.concatenate([evens, odds], axis=1))
    mine = [jnp.where(upper, v[:, half:], v[:, :half]) for v in (evens, odds)]
    half_out[...] = terms(jnp.concatenate(mine, axis=1))


def orders(taps):
    even = [None] + list(range(taps - 2, 0, -2)) + list(range(taps - 1, -1, -2))
    odd = list(range(taps - 1, -1, -2)) + list(range(taps - 2, 0, -2)) + [None]
    return even, odd


def one_hot(codes, lanes, shift):
    even = jnp.broadcast_to(codes[0:1], (8, lanes))
    odd = jnp.broadcast_to(codes[1:2], (8, lanes))
    even = pltpu.roll(even, (2 * lanes - 8 + shift) % lanes, 1, stride=1, stride_axis=0)
    odd = pltpu.roll(odd, (2 * lanes - 7 + shift) % lanes, 1, stride=1, stride_axis=0)
    near = jnp.concatenate([even, odd], axis=0)
    return jnp.concatenate([(near == a + 1.0).astype(f32) for a in range(4)], axis=0).astype(bf16)


def shifted_gates(codes, first, total, weight, rows, stem, gated):
    used = rows + 128
    half = weight.shape[1] // 2
    hot = one_hot(codes, codes.shape[1], 0)[:, :used]
    hot = jnp.concatenate([hot, hot, hot], axis=0)
    stem[...] = lax.dot_general(
        weight[...], hot, (((0,), (0,)), ((), ())), preferred_element_type=f32
    )
    spot = first - 2 + lax.broadcasted_iota(jnp.int32, (1, used), 1)
    inside = (spot >= 0) & (spot < total)
    step = 16
    for c in range(0, half, step):
        even = gelu_tanh(stem[c : c + step, :])
        odd = gelu_tanh(stem[half + c : half + c + step, :])
        pooled = (0.5 * (even + odd)).astype(bf16).astype(f32)
        value = jnp.where(inside, gelu_tanh(pooled), 0.0)
        for t in range(TAPS):
            moved = value if t == 0 else pltpu.roll(value, used - t, 1)
            gated[t * half + c : t * half + c + step, :] = moved[:, :rows].astype(bf16)


def own_kernel(rows, total, own, near, far, weight, cot, out, stem, gated, cot_v, sem):
    copy = pltpu.make_async_copy(cot, cot_v, sem)
    copy.start()
    first = lax.axis_index("context") * rows
    codes = (own[...].astype(f32) + near[...].astype(f32) + far[...].astype(f32))[0:8]
    shifted_gates(codes, first, total, weight, rows, stem, gated)
    copy.wait()
    out[...] = jnp.dot(gated[...], cot_v[...], preferred_element_type=f32)


def pair_kernel(rows, total, part, msg, far, weight, sent, kept, stem, gated):
    lanes = far.shape[1]
    ctx = lax.axis_index("context")
    core = lax.rem(ctx, 2)
    extra = msg[rows : rows + 16, :].astype(f32)
    lines = [jnp.concatenate([extra[2 * k : 2 * k + 1], extra[2 * k + 1 : 2 * k + 2]], axis=1) for k in range(2)]
    lines = [line[:, :lanes] for line in lines]
    codes = jnp.concatenate(lines + [jnp.zeros((6, lanes), f32)], axis=0) + far[...].astype(f32)[0:8]
    shifted_gates(codes, ctx * rows, total, weight, rows, stem, gated)
    size = sent.shape[0]
    for which, out in ((1 - core, sent), (core, kept)):
        span = pl.ds(pl.multiple_of(which * size, 16), size)
        value = part[span, :] + jnp.dot(
            gated[span, :], msg[0:rows, :], preferred_element_type=f32
        )
        out[...] = value.astype(out.dtype)


def back_kernel(
    rows, total, own, near, far, weight, conv, cot, d_pooled, stem_part, gated, pooled, stem, ext, back, conv_v, cot_v, sems
):
    copies = [
        pltpu.make_async_copy(cot, cot_v, sems.at[0]),
        pltpu.make_async_copy(conv, conv_v, sems.at[1]),
    ]
    for copy in copies:
        copy.start()
    lanes = own.shape[1]
    width = cot.shape[1]
    padded = rows + 2 * LEAD
    ctx = lax.axis_index("context")
    core = lax.rem(ctx, 2)
    near_v = near[...].astype(f32)
    far_v = far[...].astype(f32)
    codes = (own[...].astype(f32) + near_v + far_v)[0:8]
    hot = one_hot(codes, lanes, LEAD - 2)[:, :padded]
    hot = jnp.concatenate([hot, hot, hot], axis=0)
    stem[...] = lax.dot_general(
        hot, weight[...], (((0,), (0,)), ((), ())), preferred_element_type=f32
    )
    before = jnp.where(core == 0, far_v, near_v)[8:10, :width]
    behind = jnp.where(core == 0, near_v, far_v)[8:10, :width]
    gap = jnp.zeros((LEAD - 2, width), f32)
    ext[0:LEAD, :] = jnp.concatenate([gap, before], axis=0).astype(bf16)
    ext[LEAD + rows :, :] = jnp.concatenate([behind, gap], axis=0).astype(bf16)
    mine = one_hot(codes, lanes, lanes - 2)
    for edge in (0, LEAD + rows):
        act = 0.5 * (
            gelu_tanh(stem[edge : edge + LEAD, :width]) + gelu_tanh(stem[edge : edge + LEAD, width:])
        )
        act = act.astype(bf16).astype(f32)
        spot = ctx * rows - LEAD + edge + lax.broadcasted_iota(jnp.int32, (LEAD, 1), 0)
        inside = (spot >= 0) & (spot < total)
        gated[edge : edge + LEAD, :] = jnp.where(inside, gelu_tanh(act), 0.0).astype(bf16)
    for copy in copies:
        copy.wait()
    ext[LEAD : LEAD + rows, :] = cot_v[...]
    for t in range(TAPS):
        start = LEAD + 2 - t
        term = lax.dot_general(
            ext[start : start + rows, :], conv_v[t], (((1,), (1,)), ((), ())), preferred_element_type=f32
        )
        back[...] = term if t == 0 else back[...] + term
    step = 32
    for r in range(0, rows, step):
        even = stem[LEAD + r : LEAD + r + step, :width]
        odd = stem[LEAD + r : LEAD + r + step, width:]
        even, even_slope = gelu_both(even)
        odd, odd_slope = gelu_both(odd)
        low = (0.5 * (even + odd)).astype(bf16)
        pooled[r : r + step, :] = low
        gate, slope = gelu_both(low.astype(f32))
        gated[LEAD + r : LEAD + r + step, :] = gate.astype(bf16)
        grad = cot_v[r : r + step, :].astype(f32) + back[r : r + step, :] * slope
        d_pooled[r : r + step, :] = grad.astype(bf16)
        half = 0.5 * grad
        stem[LEAD + r : LEAD + r + step, :width] = half * even_slope
        stem[LEAD + r : LEAD + r + step, width:] = half * odd_slope
    grads = jnp.dot(
        mine[:, :rows], stem[LEAD : LEAD + rows, :].astype(bf16), preferred_element_type=f32
    )
    even, odd = orders(stem_part.shape[0] // 4 - 1)
    for k in range(len(even) - 1):
        for a in range(4):
            p, q = 16 * a + even.index(k), 16 * a + odd.index(k)
            stem_part[4 * k + a : 4 * k + a + 1, :] = (
                grads[p : p + 1, :width] + grads[q : q + 1, width:]
            )
    stem_part[stem_part.shape[0] - 4 :, :] = jnp.zeros((4, width), f32)


def feature_kernel(rows, gated, pooled, conv, out, conv_v, sem):
    copy = pltpu.make_async_copy(conv, conv_v, sem)
    copy.start()
    copy.wait()
    acc = pooled[...].astype(f32)
    for t in range(TAPS):
        start = LEAD - 2 + t
        acc = acc + jnp.dot(gated[start : start + rows, :], conv_v[t], preferred_element_type=f32)
    out[...] = acc.astype(bf16)


def place_units(pieces, sizes, offsets, unit, size, bits, out, room, sems):
    copies = []
    for piece, count, offset in zip(pieces, sizes, offsets):
        for p, (x, y, core) in enumerate(bits):
            for u in range(count // unit):
                n = len(copies)
                at = (2 * core + x) * (size // unit) + offset // unit + u
                per_tap = out.shape[0] // (2 * TAPS * unit)
                tap = at // per_tap
                row = (2 * tap + y) * (per_tap * unit) + (at - tap * per_tap) * unit
                room[n * unit : (n + 1) * unit, :] = piece[
                    p * count + u * unit : p * count + (u + 1) * unit, :
                ].astype(f32)
                copy = pltpu.make_async_copy(
                    room.at[pl.ds(n * unit, unit)],
                    out.at[pl.ds(pl.multiple_of(row, 8), unit)],
                    sems.at[n],
                )
                copy.start()
                copies.append(copy)
    for copy in copies:
        copy.wait()


def piece_bits(flip, order_first, order_second):
    ctx = lax.axis_index("context")
    core = lax.rem(ctx, 2)
    x = lax.rem(ctx // 2, 2)
    y = lax.rem(lax.axis_index("dp"), 2)
    x_first = jnp.where(core == 0, order_first, order_second)
    x_first = jnp.where(flip == 1, 1 - x_first, x_first)
    result = []
    for p in range(4):
        one, two = p % 2, p // 2
        dx = jnp.where(x_first == 1, one, two)
        dy = one + two - dx
        result.append((lax.rem(x + dx, 2), lax.rem(y + dy, 2), lax.rem(core + flip, 2)))
    return result


def place_kernel(flip, sizes, offsets, unit, size, left, right, *rest):
    if flip:
        stem, whole, out, stem_out, room, sems = rest
        del whole
        total = stem[...].astype(bf16).astype(f32) + right[right.shape[0] - stem.shape[0] :, :].astype(f32)
        for k in range(stem_out.shape[0]):
            stem_out[k] = total[4 * k : 4 * k + 4, :]
    else:
        out, room, sems = rest
    bits = [piece_bits(flip, 1, 0), piece_bits(flip, 0, 1)]
    copies_at = sizes[0] * 4 // unit
    place_units([left], sizes[:1], offsets[:1], unit, size, bits[0], out, room.at[pl.ds(0, sizes[0] * 4)], sems.at[pl.ds(0, copies_at)])
    place_units([right], sizes[1:], offsets[1:], unit, size, bits[1], out, room.at[pl.ds(sizes[0] * 4, sizes[1] * 4)], sems.at[pl.ds(copies_at, sizes[1] * 4 // unit)])


def per_device(codes, variant_pos, variant_shift, stem_weight, conv_weight, cotangent):
    n_dp, n_ctx = lax.axis_size("dp"), lax.axis_size("context")
    devices = n_dp * n_ctx
    length = codes.shape[1]
    rows = length // 2
    taps, _, width = stem_weight.shape
    half = width // 2
    total = rows * n_ctx
    lanes = -(-(rows + 256) // 128) * 128
    ctx = lax.axis_index("context")
    core = ctx % 2
    cot = cotangent[0]
    x_bit, y_bit = 2, n_ctx

    def swap(value, even_bit, odd_bit=None):
        odd_bit = even_bit if odd_bit is None else odd_bit
        pairs = [(i, i ^ (odd_bit if i & 1 else even_bit)) for i in range(devices)]
        return lax.ppermute(value, AXES, pairs)

    outward = []
    for d in range(n_dp):
        for c in range(n_ctx):
            other = c + 1 if c & 1 else c - 1
            if 0 <= other < n_ctx:
                outward.append((d * n_ctx + c, d * n_ctx + other))

    edge = jax.ShapeDtypeStruct((16, lanes), bf16)
    message = jax.ShapeDtypeStruct((rows + 16, width), bf16)
    own, near, far, msg = pl.pallas_call(
        functools.partial(first_kernel, rows, lanes),
        out_shape=[edge, edge, edge, message],
        in_specs=[FAR] * 4,
        out_specs=[VMEM] * 4,
        scratch_shapes=[
            pltpu.VMEM((1, length), jnp.int32),
            pltpu.SMEM(variant_pos.shape, jnp.int32),
            pltpu.SMEM(variant_pos.shape, jnp.int32),
            pltpu.VMEM((16, width), bf16),
            pltpu.VMEM((16, width), bf16),
            pltpu.SemaphoreType.DMA((6,)),
        ],
        compiler_params=params(),
    )(codes, variant_pos, variant_shift, cot)
    near = swap(near, 1)
    msg = pl.pallas_call(
        message_kernel,
        grid=(1,),
        out_shape=message,
        in_specs=[
            pl.BlockSpec((16, lanes), lambda i: (0, 0)),
            pl.BlockSpec((16, lanes), lambda i: (0, 0)),
            pl.BlockSpec(memory_space=pl.ANY),
        ],
        out_specs=pl.BlockSpec((16, width), lambda i: (rows // 16, 0)),
        input_output_aliases={2: 0},
        compiler_params=params(),
    )(own, near, msg)
    msg = swap(msg, y_bit)
    outer = far
    far = lax.ppermute(outer, AXES, outward)
    pair_far = lax.ppermute(outer, AXES, [(a, b ^ y_bit) for a, b in outward])

    weight, half_weight = pl.pallas_call(
        weight_kernel,
        out_shape=[
            jax.ShapeDtypeStruct((192, 2 * width), bf16),
            jax.ShapeDtypeStruct((192, width), bf16),
        ],
        in_specs=[VMEM],
        out_specs=[VMEM] * 2,
        compiler_params=params(),
    )(stem_weight)

    gates = [
        pltpu.VMEM((width, rows + 128), f32),
        pltpu.VMEM((TAPS * half, rows), bf16),
    ]
    part = pl.pallas_call(
        functools.partial(own_kernel, rows, total),
        out_shape=jax.ShapeDtypeStruct((TAPS * half, width), f32),
        in_specs=[VMEM] * 4 + [FAR],
        out_specs=VMEM,
        scratch_shapes=gates + [pltpu.VMEM((rows, width), bf16), pltpu.SemaphoreType.DMA],
        compiler_params=params(),
    )(own, near, far, half_weight, cot)

    size = TAPS * half // 2
    sent, kept = pl.pallas_call(
        functools.partial(pair_kernel, rows, total),
        out_shape=[
            jax.ShapeDtypeStruct((size, width), bf16),
            jax.ShapeDtypeStruct((size, width), f32),
        ],
        in_specs=[VMEM] * 4,
        out_specs=[VMEM] * 2,
        scratch_shapes=gates,
        compiler_params=params(),
    )(part, msg, pair_far, half_weight)
    value = kept + swap(sent, 1).astype(f32)
    x = ctx // x_bit % 2
    size //= 2
    sent = lax.dynamic_slice_in_dim(value, (1 - x) * size, size, 0).astype(bf16)
    kept = lax.dynamic_slice_in_dim(value, x * size, size, 0)
    value = kept + swap(sent, x_bit).astype(f32)

    padded = rows + 2 * LEAD
    cost = pl.CostEstimate(
        flops=2 * TAPS * rows * width * width, bytes_accessed=4 << 20, transcendentals=0
    )
    d_pooled, stem_part, gated, pooled = pl.pallas_call(
        functools.partial(back_kernel, rows, total),
        out_shape=[
            jax.ShapeDtypeStruct((rows, width), bf16),
            jax.ShapeDtypeStruct((4 * taps + 4, width), f32),
            jax.ShapeDtypeStruct((padded, width), bf16),
            jax.ShapeDtypeStruct((rows, width), bf16),
        ],
        in_specs=[VMEM] * 4 + [FAR] * 2,
        out_specs=[VMEM] * 4,
        scratch_shapes=[
            pltpu.VMEM((padded, 2 * width), f32),
            pltpu.VMEM((padded, width), bf16),
            pltpu.VMEM((rows, width), f32),
            pltpu.VMEM(conv_weight.shape, bf16),
            pltpu.VMEM((rows, width), bf16),
            pltpu.SemaphoreType.DMA((2,)),
        ],
        compiler_params=params(),
        cost_estimate=cost,
    )(after(own, sent), near, far, weight, conv_weight, cot)

    unit = half // 4
    cut = 3 * unit
    left = value[:cut]
    right = jnp.concatenate([value[cut:], stem_part], axis=0)
    others = [1 << k for k in range(devices.bit_length() - 1) if (1 << k) not in (1, x_bit, y_bit)]
    last = None
    for b in others:
        left, right = rounded(left), rounded(right)
        last = left
        left, right = [v + swap(v.astype(bf16), b).astype(f32) for v in (left, right)]
    features = pl.pallas_call(
        functools.partial(feature_kernel, rows),
        out_shape=jax.ShapeDtypeStruct((rows, width), bf16),
        in_specs=[VMEM] * 2 + [FAR],
        out_specs=VMEM,
        scratch_shapes=[pltpu.VMEM(conv_weight.shape, bf16), pltpu.SemaphoreType.DMA],
        compiler_params=params(),
        cost_estimate=cost,
    )(gated, after(pooled, last), conv_weight)

    rest = size - cut
    left = left.astype(bf16)
    stem_sum = right[rest:]
    right = right[:rest].astype(bf16)
    for one, two in ((x_bit, y_bit), (y_bit, x_bit)):
        got = swap(left, one, two)
        left = jnp.concatenate([left, got], axis=0)
        stem_sum = rounded(stem_sum)
        got = swap(jnp.concatenate([right, stem_sum.astype(bf16)], axis=0), two, one)
        stem_sum = stem_sum + got[right.shape[0] :].astype(f32)
        right = jnp.concatenate([right, got[: right.shape[0]]], axis=0)
    got_left = swap(left, 1)
    got_right = swap(jnp.concatenate([right, stem_sum.astype(bf16)], axis=0), 1)

    sizes, offsets = (cut, rest), (0, cut)
    whole = jax.ShapeDtypeStruct((TAPS * width, width), f32)
    room = [pltpu.VMEM((4 * size, width), f32), pltpu.SemaphoreType.DMA((4 * size // unit,))]
    conv_grad = pl.pallas_call(
        functools.partial(place_kernel, 0, sizes, offsets, unit, size),
        out_shape=whole,
        in_specs=[VMEM] * 2,
        out_specs=FAR,
        scratch_shapes=room,
        compiler_params=params(),
        cost_estimate=pl.CostEstimate(flops=0, bytes_accessed=4 << 20, transcendentals=0),
    )(left, right)
    conv_grad, stem_grad = pl.pallas_call(
        functools.partial(place_kernel, 1, sizes, offsets, unit, size),
        out_shape=[whole, jax.ShapeDtypeStruct(stem_weight.shape, f32)],
        in_specs=[VMEM] * 3 + [FAR],
        out_specs=[FAR, VMEM],
        scratch_shapes=room,
        input_output_aliases={3: 0},
        compiler_params=params(),
    )(got_left, got_right, stem_sum, conv_grad)
    conv_grad = conv_grad.reshape(TAPS, width, width)
    return (features[None], d_pooled[None], conv_grad, stem_grad)


def solution(mesh):
    placed = (P("dp", "context"), P("dp", None), P("dp", None), P(), P(), P("dp", "context", None))
    return jax.shard_map(
        per_device,
        mesh=mesh,
        in_specs=placed,
        out_specs=(P("dp", "context", None), P("dp", "context", None), P(), P()),
        check_vma=False,
    )
```

time: 82.4 us -> 68.7 us (0.83)
  waiting for transfers between devices: 36 us -> 23.7 us
  Pallas kernels: 10.6 us -> 15.9 us
  other arithmetic: 6.59 us -> 1.52 us
  local copies, waits for them, and re-layouts: 9.82 us -> 5.8 us
  starting transfers between devices: 17.9 us -> 20.5 us
    ppermute x9 -> x14, waiting for transfers between devices: 36 us -> 23.7 us  [swap(): return lax.ppermute(value, AXES, pairs)]
    pallas_call x3 -> x7, Pallas kernels: 3.62 us -> 8.93 us  [the longest x1 2.64 us: per_device(): pl.pallas_call(functools.partial(place_kernel, 1, sizes, offsets, unit, s...]
    convert_element_type x8, other arithmetic: 3.33 us -> 0.2 us  [the longest x4 0.12 us: per_device(): v.astype(bf16)]
    ppermute x9 -> x14, starting transfers between devices: 17.2 us -> 19.1 us  [swap(): return lax.ppermute(value, AXES, pairs)]
    unnamed x22 -> x20, local copies, waits for them, and re-layouts: 7.55 us -> 5.73 us
    slice x6 -> x4, local copies, waits for them, and re-layouts: 1.41 us -> 0.05 us  [the longest x2 0.03 us: per_device(): right = jnp.concatenate([right, got[:right.shape[0]]], axis=0)]
    concatenate x3 -> x6, other arithmetic: 1.04 us -> 0.18 us  [the longest x2 0.07 us: per_device(): left = jnp.concatenate([left, got], axis=0)]
  transfers between devices with their start and end apart: 10 -> 16, of which waited for: 8 -> 9; matrix products, arithmetic and copies ran while one was open for 0% -> 1% of each run, Pallas kernels for 3% -> 16%
where the time goes in v2:
time: 68.7 us; the launch traced here: 68.4 us
  waiting for transfers between devices  23.7 us (34%)
  starting transfers between devices  20.5 us (30%)
  Pallas kernels  15.9 us (23%)
  local copies, waits for them, and re-layouts  5.8 us (8%)
  other arithmetic  1.52 us (2%)
  between operations  0.96 us (1%)
    ppermute x14, waiting for transfers between devices, swap(): return lax.ppermute(value, AXES, pairs)  23.7 us
    ppermute x14, starting transfers between devices, swap(): return lax.ppermute(value, AXES, pairs)  19.1 us
    unnamed x20, local copies, waits for them, and re-layouts  5.73 us
    pallas_call x1, Pallas kernels, per_device(): pl.pallas_call(functools.partial(back_kernel, rows, total), out_shape=[ja...  4.57 us
    pallas_call x1, Pallas kernels, per_device(): pl.pallas_call(functools.partial(place_kernel, 1, sizes, offsets, unit, s...  2.64 us
    pallas_call x1, Pallas kernels, per_device(): pl.pallas_call(functools.partial(feature_kernel, rows), out_shape=jax.Sha...  2.43 us
    pallas_call x1, Pallas kernels, per_device(): pl.pallas_call(functools.partial(place_kernel, 0, sizes, offsets, unit, s...  1.99 us
    pallas_call x1, Pallas kernels, per_device(): pl.pallas_call(functools.partial(own_kernel, rows, total), out_shape=jax....  1.78 us
  transfers between devices with their start and end apart: 16, of which 9 were waited for; matrix products, arithmetic and copies ran while one was open for 1% of the time, Pallas kernels for 16%

profile of v2, /device:TPU:0, one launch (start us, length us, event | category | flops | bytes accessed | tf_op | source)
XLA Modules:
  0.0 68.4 jit_solution(4140469199792057154)
XLA Ops:
  0.6 1.0 %copy-done = bf16[1,512,384]{2,1,0:T(8,128)(2,1)S(1)} copy-done((bf16[1,512,384]{2,1,0:T(8,128)(2,1)S(1)}, bf16[1,512,384]{2,1,0:T(8,128)(2,1)}, u32[]{:S(2)}) %copy-start) | copy-done | bytes 393240
  5.9 2.9 %collective-permute-start.2 = (bf16[528,384]{1,0:T(8,128)(2,1)S(1)}, bf16[528,384]{1,0:T(8,128)(2,1)S(1)}, u32[]{:S(2)}, u32[]{:S(2)}) collective-permute-start(bf16[528,384]{1,0:T(8,128)(2,1)S(1)} %shard_map.96), channel_id=1, source_target_pairs={{0,16},{1,17},{2,18},{3,19},{4,20},{5,21},{6,22},{7,23},{8,24},{9,... | collective-permute-start | bytes 1216520 | tf_op jit(solution)/shard_map/ppermute | solution.py:377
  12.2 1.8 %shard_map.95.part = f32[960,384]{1,0:T(8,128)S(1)} custom-call(bf16[16,768]{1,0:T(8,128)(2,1)S(1)} %get-tuple-element.27.own, bf16[16,768]{1,0:T(8,128)(2,1)S(1)} %collective-permute-done.near, bf16[16,768]{1,0:T(8,128)(2,1)S(1)} %collective-permute-done.1.far, bf16[192,384]{1,0:T(8,128)(2,1)S(1)} %get-tuple-element.23.weight, bf16[512,384]{1,0:T(8,128)(2,1)S(1)} %bitcast.5), custom_call_target="tpu_custom_call" | custom-call | tf_op jit(solution)/shard_map/pallas_call | solution.py:437
  14.0 4.8 %collective-permute-done.2.msg = bf16[528,384]{1,0:T(8,128)(2,1)S(1)} collective-permute-done((bf16[528,384]{1,0:T(8,128)(2,1)S(1)}, bf16[528,384]{1,0:T(8,128)(2,1)S(1)}, u32[]{:S(2)}, u32[]{:S(2)}) %collective-permute-start.2) | collective-permute-done | bytes 405536 | tf_op jit(solution)/shard_map/ppermute | solution.py:377
  18.8 1.5 %shard_map.97 = (bf16[480,384]{1,0:T(8,128)(2,1)S(1)}, f32[480,384]{1,0:T(8,128)S(1)}) custom-call(f32[960,384]{1,0:T(8,128)S(1)} %shard_map.95.part, bf16[528,384]{1,0:T(8,128)(2,1)S(1)} %collective-permute-done.2.msg, bf16[16,768]{1,0:T(8,128)(2,1)S(1)} %collective-permute-done.3.far, bf16[192,384]{1,0:T(8,128)(2,1)S(1)} %get-tuple-element.23.weight), custom_call_target="tpu_custom_call" | custom-call | tf_op jit(solution)/shard_map/pallas_call | solution.py:447
  20.4 1.8 %collective-permute-done.4 = bf16[480,384]{1,0:T(8,128)(2,1)} collective-permute-done((bf16[480,384]{1,0:T(8,128)(2,1)S(1)}, bf16[480,384]{1,0:T(8,128)(2,1)}, u32[]{:S(2)}, u32[]{:S(2)}) %collective-permute-start.4) | collective-permute-done | bytes 368672 | tf_op jit(solution)/shard_map/ppermute | solution.py:377
  22.1 1.0 %convert_add_fusion = f32[480,384]{1,0:T(8,128)S(1)} fusion(f32[480,384]{1,0:T(8,128)S(1)} %get-tuple-element.25, bf16[480,384]{1,0:T(8,128)(2,1)} %collective-permute-done.4), kind=kLoop, calls=%fused_computation | loop fusion | flops 368640 | bytes 1843200 | tf_op jit(solution)/shard_map/add | solution.py:458
  24.1 1.8 %collective-permute-start.5 = (bf16[240,384]{1,0:T(8,128)(2,1)S(1)}, bf16[240,384]{1,0:T(8,128)(2,1)S(1)}, u32[]{:S(2)}, u32[]{:S(2)}) collective-permute-start(bf16[240,384]{1,0:T(8,128)(2,1)S(1)} %dynamic-slice_convert_fusion), channel_id=1, source_target_pairs={{0,2},{1,3},{2,0},{3,1},{4,6},{5,7},{6,4},{7,5},{8,10},{9,11},{10,... | collective-permute-start | bytes 552968 | tf_op jit(solution)/shard_map/ppermute | solution.py:377
  25.9 4.6 %shard_map.98 = (bf16[512,384]{1,0:T(8,128)(2,1)}, f32[64,384]{1,0:T(8,128)S(1)}, bf16[544,384]{1,0:T(8,128)(2,1)S(1)}, bf16[512,384]{1,0:T(8,128)(2,1)S(1)}) custom-call(bf16[16,768]{1,0:T(8,128)(2,1)S(1)} %get-tuple-element.27.own, bf16[16,768]{1,0:T(8,128)(2,1)S(1)} %collective-permute-done.near, bf16[16,768]{1,0:T(8,128)(2,1)S(1)} %collective-permute-done.1.far, ...), custom_call_target="tpu_custom_call" | custom-call | flops 754974720 | bytes 4194304 | tf_op jit(solution)/shard_map/pallas_call | solution.py:469
  31.1 2.0 %collective-permute-start.6 = (bf16[144,384]{1,0:T(8,128)(2,1)S(1)}, bf16[144,384]{1,0:T(8,128)(2,1)S(1)}, u32[]{:S(2)}, u32[]{:S(2)}) collective-permute-start(bf16[144,384]{1,0:T(8,128)(2,1)S(1)} %fusion), channel_id=1, source_target_pairs={{0,4},{1,5},{2,6},{3,7},{4,0},{5,1},{6,2},{7,3},{8,12},{9,13},{10,... | collective-permute-start | bytes 331784 | tf_op jit(solution)/shard_map/ppermute | solution.py:377
  33.3 3.8 %collective-permute-done.6 = bf16[144,384]{1,0:T(8,128)(2,1)S(1)} collective-permute-done((bf16[144,384]{1,0:T(8,128)(2,1)S(1)}, bf16[144,384]{1,0:T(8,128)(2,1)S(1)}, u32[]{:S(2)}, u32[]{:S(2)}) %collective-permute-start.6) | collective-permute-done | bytes 110624 | tf_op jit(solution)/shard_map/ppermute | solution.py:377
  37.1 3.0 %collective-permute-start.7 = (bf16[144,384]{1,0:T(8,128)(2,1)S(1)}, bf16[144,384]{1,0:T(8,128)(2,1)S(1)}, u32[]{:S(2)}, u32[]{:S(2)}) collective-permute-start(bf16[144,384]{1,0:T(8,128)(2,1)S(1)} %get-tuple-element.38), channel_id=1, source_target_pairs={{0,8},{1,9},{2,10},{3,11},{4,12},{5,13},{6,14},{7,15},{8,0},{9,1},... | collective-permute-start | bytes 331784 | tf_op jit(solution)/shard_map/ppermute | solution.py:377
  40.1 2.6 %collective-permute-start.12 = (bf16[160,384]{1,0:T(8,128)(2,1)S(1)}, bf16[160,384]{1,0:T(8,128)(2,1)S(1)}, u32[]{:S(2)}, u32[]{:S(2)}) collective-permute-start(bf16[160,384]{1,0:T(8,128)(2,1)S(1)} %fusion.2), channel_id=1, source_target_pairs={{0,8},{1,9},{2,10},{3,11},{4,12},{5,13},{6,14},{7,15},{8,0},{9,1},... | collective-permute-start | bytes 368648 | tf_op jit(solution)/shard_map/ppermute | solution.py:377
  42.7 4.9 %collective-permute-done.7 = bf16[144,384]{1,0:T(8,128)(2,1)S(1)} collective-permute-done((bf16[144,384]{1,0:T(8,128)(2,1)S(1)}, bf16[144,384]{1,0:T(8,128)(2,1)S(1)}, u32[]{:S(2)}, u32[]{:S(2)}) %collective-permute-start.7) | collective-permute-done | bytes 110624 | tf_op jit(solution)/shard_map/ppermute | solution.py:377
  47.7 1.6 %collective-permute-start.8 = (bf16[144,384]{1,0:T(8,128)(2,1)S(1)}, bf16[144,384]{1,0:T(8,128)(2,1)S(1)}, u32[]{:S(2)}, u32[]{:S(2)}) collective-permute-start(bf16[144,384]{1,0:T(8,128)(2,1)S(1)} %add_convert_fusion), channel_id=1, source_target_pairs={{0,2},{1,17},{2,0},{3,19},{4,6},{5,21},{6,4},{7,23},{8,10},{9,25},... | collective-permute-start | bytes 331784 | tf_op jit(solution)/shard_map/ppermute | solution.py:377
  49.4 1.3 %collective-permute-start.13 = (bf16[160,384]{1,0:T(8,128)(2,1)S(1)}, bf16[160,384]{1,0:T(8,128)(2,1)S(1)}, u32[]{:S(2)}, u32[]{:S(2)}) collective-permute-start(bf16[160,384]{1,0:T(8,128)(2,1)S(1)} %pad_maximum_fusion.5), channel_id=1, source_target_pairs={{0,16},{1,3},{2,18},{3,1},{4,20},{5,7},{6,22},{7,5},{8,24},{9,11},... | collective-permute-start | bytes 368648 | tf_op jit(solution)/shard_map/ppermute | solution.py:377
  50.7 2.9 %collective-permute-done.8 = bf16[144,384]{1,0:T(8,128)(2,1)S(1)} collective-permute-done((bf16[144,384]{1,0:T(8,128)(2,1)S(1)}, bf16[144,384]{1,0:T(8,128)(2,1)S(1)}, u32[]{:S(2)}, u32[]{:S(2)}) %collective-permute-start.8) | collective-permute-done | bytes 110624 | tf_op jit(solution)/shard_map/ppermute | solution.py:377
  53.7 1.6 %collective-permute-start.9 = (bf16[288,384]{1,0:T(8,128)(2,1)S(1)}, bf16[288,384]{1,0:T(8,128)(2,1)S(1)}, u32[]{:S(2)}, u32[]{:S(2)}) collective-permute-start(bf16[288,384]{1,0:T(8,128)(2,1)S(1)} %pad_maximum_fusion.3), channel_id=1, source_target_pairs={{0,16},{1,3},{2,18},{3,1},{4,20},{5,7},{6,22},{7,5},{8,24},{9,11},... | collective-permute-start | bytes 663560 | tf_op jit(solution)/shard_map/ppermute | solution.py:377
  55.3 1.4 %collective-permute-start.14 = (bf16[256,384]{1,0:T(8,128)(2,1)S(1)}, bf16[256,384]{1,0:T(8,128)(2,1)S(1)}, u32[]{:S(2)}, u32[]{:S(2)}) collective-permute-start(bf16[256,384]{1,0:T(8,128)(2,1)S(1)} %pad_maximum_fusion.4), channel_id=1, source_target_pairs={{0,2},{1,17},{2,0},{3,19},{4,6},{5,21},{6,4},{7,23},{8,10},{9,25},... | collective-permute-start | bytes 589832 | tf_op jit(solution)/shard_map/ppermute | solution.py:377
  56.7 2.9 %collective-permute-done.9 = bf16[288,384]{1,0:T(8,128)(2,1)S(1)} collective-permute-done((bf16[288,384]{1,0:T(8,128)(2,1)S(1)}, bf16[288,384]{1,0:T(8,128)(2,1)S(1)}, u32[]{:S(2)}, u32[]{:S(2)}) %collective-permute-start.9) | collective-permute-done | bytes 221216 | tf_op jit(solution)/shard_map/ppermute | solution.py:377
  59.8 1.3 %collective-permute-done.14 = bf16[256,384]{1,0:T(8,128)(2,1)S(1)} collective-permute-done((bf16[256,384]{1,0:T(8,128)(2,1)S(1)}, bf16[256,384]{1,0:T(8,128)(2,1)S(1)}, u32[]{:S(2)}, u32[]{:S(2)}) %collective-permute-start.14) | collective-permute-done | bytes 196640 | tf_op jit(solution)/shard_map/ppermute | solution.py:377
  61.2 2.4 %shard_map.99 = bf16[512,384]{1,0:T(8,128)(2,1)} custom-call(bf16[544,384]{1,0:T(8,128)(2,1)S(1)} %get-tuple-element.29.gated, bf16[512,384]{1,0:T(8,128)(2,1)S(1)} %get-tuple-element.31.pooled, bf16[5,384,384]{2,1,0:T(8,128)(2,1)S(1)} %copy-done.7), custom_call_target="tpu_custom_call" | custom-call | flops 754974720 | bytes 4194304 | tf_op jit(solution)/shard_map/pallas_call | solution.py:501
  63.7 2.0 %shard_map.100.rest_1_ = f32[1920,384]{1,0:T(8,128)} custom-call(bf16[576,384]{1,0:T(8,128)(2,1)S(1)} %pad_maximum_fusion.left, bf16[384,384]{1,0:T(8,128)(2,1)S(1)} %pad_maximum_fusion.2.right), custom_call_target="tpu_custom_call" | custom-call | bytes 4194304 | tf_op jit(solution)/shard_map/pallas_call | solution.py:528
  65.7 2.6 %shard_map.101 = (f32[1920,384]{1,0:T(8,128)}, f32[15,4,384]{2,1,0:T(4,128)}) custom-call(bf16[576,384]{1,0:T(8,128)(2,1)S(1)} %collective-permute-done.10.left, bf16[448,384]{1,0:T(8,128)(2,1)S(1)} %collective-permute-done.15.right, f32[64,384]{1,0:T(8,128)S(1)} %get-tuple-element.37.rest_0_, ...), custom_call_target="tpu_custom_call", output_to_operand_aliasing={{0}: (3, {})} | custom-call | tf_op jit(solution)/shard_map/pallas_call | solution.py:537
  (59 shorter events, 10.0 us)
Async XLA Ops:
  0.6 1.0 %copy-start = (bf16[1,512,384]{2,1,0:T(8,128)(2,1)S(1)}, bf16[1,512,384]{2,1,0:T(8,128)(2,1)}, u32[]{:S(2)}) copy-start(bf16[1,512,384]{2,1,0:T(8,128)(2,1)} %param.11) | copy-start | bytes 1179652
  1.6 0.7 %copy-start.4 = (s32[1,1024]{1,0:T(1,128)S(1)}, s32[1,1024]{1,0:T(1,128)}, u32[]{:S(2)}) copy-start(s32[1,1024]{1,0:T(1,128)} %codes.1) | copy-start | bytes 12292
  4.5 1.4 %collective-permute-start = (bf16[16,768]{1,0:T(8,128)(2,1)S(1)}, bf16[16,768]{1,0:T(8,128)(2,1)S(1)}, u32[]{:S(2)}, u32[]{:S(2)}) collective-permute-start(bf16[16,768]{1,0:T(8,128)(2,1)S(1)} %get-tuple-element.21), channel_id=1, source_target_pairs={{0,1},{1,0},{2,3},{3,2},{4,5},{5,4},{6,7},{7,6},{8,9},{9,8},{10,11... | collective-permute-start | bytes 73736 | tf_op jit(solution)/shard_map/ppermute | solution.py:377
  5.9 12.9 %collective-permute-start.2 = (bf16[528,384]{1,0:T(8,128)(2,1)S(1)}, bf16[528,384]{1,0:T(8,128)(2,1)S(1)}, u32[]{:S(2)}, u32[]{:S(2)}) collective-permute-start(bf16[528,384]{1,0:T(8,128)(2,1)S(1)} %shard_map.96), channel_id=1, source_target_pairs={{0,16},{1,17},{2,18},{3,19},{4,20},{5,21},{6,22},{7,23},{8,24},{9,... | collective-permute-start | bytes 1216520 | tf_op jit(solution)/shard_map/ppermute | solution.py:377
  8.8 2.4 %collective-permute-start.1 = (bf16[16,768]{1,0:T(8,128)(2,1)S(1)}, bf16[16,768]{1,0:T(8,128)(2,1)S(1)}, u32[]{:S(2)}, u32[]{:S(2)}) collective-permute-start(bf16[16,768]{1,0:T(8,128)(2,1)S(1)} %get-tuple-element.22), channel_id=1, source_target_pairs={{1,2},{2,1},{3,4},{4,3},{5,6},{6,5},{7,8},{8,7},{9,10},{10,9},{11,... | collective-permute-start | bytes 73736 | tf_op jit(solution)/shard_map/ppermute | solution.py:419
  9.5 4.6 %collective-permute-start.3 = (bf16[16,768]{1,0:T(8,128)(2,1)S(1)}, bf16[16,768]{1,0:T(8,128)(2,1)S(1)}, u32[]{:S(2)}, u32[]{:S(2)}) collective-permute-start(bf16[16,768]{1,0:T(8,128)(2,1)S(1)} %get-tuple-element.22), channel_id=1, source_target_pairs={{1,18},{2,17},{3,20},{4,19},{5,22},{6,21},{7,24},{8,23},{9,26},{10... | collective-permute-start | bytes 73736 | tf_op jit(solution)/shard_map/ppermute | solution.py:420
  10.2 0.9 %copy-start.3 = (f32[15,4,384]{2,1,0:T(4,128)S(1)}, f32[15,4,384]{2,1,0:T(4,128)}, u32[]{:S(2)}) copy-start(f32[15,4,384]{2,1,0:T(4,128)} %weight.1) | copy-start | bytes 276484
  11.2 1.0 %copy-start.1 = (bf16[1,512,384]{2,1,0:T(8,128)(2,1)S(1)}, bf16[1,512,384]{2,1,0:T(8,128)(2,1)}, u32[]{:S(2)}) copy-start(bf16[1,512,384]{2,1,0:T(8,128)(2,1)} %param.11) | copy-start | bytes 1179652
  12.2 13.6 %copy-start.2 = (bf16[1,512,384]{2,1,0:T(8,128)(2,1)S(1)}, bf16[1,512,384]{2,1,0:T(8,128)(2,1)}, u32[]{:S(2)}) copy-start(bf16[1,512,384]{2,1,0:T(8,128)(2,1)} %param.11) | copy-start | bytes 1179652
  12.2 13.6 %copy-start.7 = (bf16[5,384,384]{2,1,0:T(8,128)(2,1)S(1)}, bf16[5,384,384]{2,1,0:T(8,128)(2,1)}, u32[]{:S(2)}) copy-start(bf16[5,384,384]{2,1,0:T(8,128)(2,1)} %conv.3) | copy-start | bytes 4423684
  20.3 1.9 %collective-permute-start.4 = (bf16[480,384]{1,0:T(8,128)(2,1)S(1)}, bf16[480,384]{1,0:T(8,128)(2,1)}, u32[]{:S(2)}, u32[]{:S(2)}) collective-permute-start(bf16[480,384]{1,0:T(8,128)(2,1)S(1)} %get-tuple-element.26), channel_id=1, source_target_pairs={{0,1},{1,0},{2,3},{3,2},{4,5},{5,4},{6,7},{7,6},{8,9},{9,8},{10,11... | collective-permute-start | bytes 1105928 | tf_op jit(solution)/shard_map/ppermute | solution.py:377
  23.2 0.9 %copy-start.8 = (f32[480,384]{1,0:T(8,128)}, f32[480,384]{1,0:T(8,128)S(1)}, u32[]{:S(2)}) copy-start(f32[480,384]{1,0:T(8,128)S(1)} %convert_add_fusion) | copy-start | bytes 2211844
  24.1 6.9 %collective-permute-start.5 = (bf16[240,384]{1,0:T(8,128)(2,1)S(1)}, bf16[240,384]{1,0:T(8,128)(2,1)S(1)}, u32[]{:S(2)}, u32[]{:S(2)}) collective-permute-start(bf16[240,384]{1,0:T(8,128)(2,1)S(1)} %dynamic-slice_convert_fusion), channel_id=1, source_target_pairs={{0,2},{1,3},{2,0},{3,1},{4,6},{5,7},{6,4},{7,5},{8,10},{9,11},{10,... | collective-permute-start | bytes 552968 | tf_op jit(solution)/shard_map/ppermute | solution.py:377
  25.9 5.1 %copy-start.9 = (f32[480,384]{1,0:T(8,128)S(1)}, f32[480,384]{1,0:T(8,128)}, u32[]{:S(2)}) copy-start(f32[480,384]{1,0:T(8,128)} %copy-done.8) | copy-start | bytes 2211844
  31.1 5.9 %collective-permute-start.6 = (bf16[144,384]{1,0:T(8,128)(2,1)S(1)}, bf16[144,384]{1,0:T(8,128)(2,1)S(1)}, u32[]{:S(2)}, u32[]{:S(2)}) collective-permute-start(bf16[144,384]{1,0:T(8,128)(2,1)S(1)} %fusion), channel_id=1, source_target_pairs={{0,4},{1,5},{2,6},{3,7},{4,0},{5,1},{6,2},{7,3},{8,12},{9,13},{10,... | collective-permute-start | bytes 331784 | tf_op jit(solution)/shard_map/ppermute | solution.py:377
  33.1 7.0 %collective-permute-start.11 = (bf16[160,384]{1,0:T(8,128)(2,1)S(1)}, bf16[160,384]{1,0:T(8,128)(2,1)S(1)}, u32[]{:S(2)}, u32[]{:S(2)}) collective-permute-start(bf16[160,384]{1,0:T(8,128)(2,1)S(1)} %fusion.1), channel_id=1, source_target_pairs={{0,4},{1,5},{2,6},{3,7},{4,0},{5,1},{6,2},{7,3},{8,12},{9,13},{10,... | collective-permute-start | bytes 368648 | tf_op jit(solution)/shard_map/ppermute | solution.py:377
  37.1 10.6 %collective-permute-start.7 = (bf16[144,384]{1,0:T(8,128)(2,1)S(1)}, bf16[144,384]{1,0:T(8,128)(2,1)S(1)}, u32[]{:S(2)}, u32[]{:S(2)}) collective-permute-start(bf16[144,384]{1,0:T(8,128)(2,1)S(1)} %get-tuple-element.38), channel_id=1, source_target_pairs={{0,8},{1,9},{2,10},{3,11},{4,12},{5,13},{6,14},{7,15},{8,0},{9,1},... | collective-permute-start | bytes 331784 | tf_op jit(solution)/shard_map/ppermute | solution.py:377
  40.1 9.1 %collective-permute-start.12 = (bf16[160,384]{1,0:T(8,128)(2,1)S(1)}, bf16[160,384]{1,0:T(8,128)(2,1)S(1)}, u32[]{:S(2)}, u32[]{:S(2)}) collective-permute-start(bf16[160,384]{1,0:T(8,128)(2,1)S(1)} %fusion.2), channel_id=1, source_target_pairs={{0,8},{1,9},{2,10},{3,11},{4,12},{5,13},{6,14},{7,15},{8,0},{9,1},... | collective-permute-start | bytes 368648 | tf_op jit(solution)/shard_map/ppermute | solution.py:377
  47.7 6.0 %collective-permute-start.8 = (bf16[144,384]{1,0:T(8,128)(2,1)S(1)}, bf16[144,384]{1,0:T(8,128)(2,1)S(1)}, u32[]{:S(2)}, u32[]{:S(2)}) collective-permute-start(bf16[144,384]{1,0:T(8,128)(2,1)S(1)} %add_convert_fusion), channel_id=1, source_target_pairs={{0,2},{1,17},{2,0},{3,19},{4,6},{5,21},{6,4},{7,23},{8,10},{9,25},... | collective-permute-start | bytes 331784 | tf_op jit(solution)/shard_map/ppermute | solution.py:377
  49.4 5.8 %collective-permute-start.13 = (bf16[160,384]{1,0:T(8,128)(2,1)S(1)}, bf16[160,384]{1,0:T(8,128)(2,1)S(1)}, u32[]{:S(2)}, u32[]{:S(2)}) collective-permute-start(bf16[160,384]{1,0:T(8,128)(2,1)S(1)} %pad_maximum_fusion.5), channel_id=1, source_target_pairs={{0,16},{1,3},{2,18},{3,1},{4,20},{5,7},{6,22},{7,5},{8,24},{9,11},... | collective-permute-start | bytes 368648 | tf_op jit(solution)/shard_map/ppermute | solution.py:377
  53.7 6.0 %collective-permute-start.9 = (bf16[288,384]{1,0:T(8,128)(2,1)S(1)}, bf16[288,384]{1,0:T(8,128)(2,1)S(1)}, u32[]{:S(2)}, u32[]{:S(2)}) collective-permute-start(bf16[288,384]{1,0:T(8,128)(2,1)S(1)} %pad_maximum_fusion.3), channel_id=1, source_target_pairs={{0,16},{1,3},{2,18},{3,1},{4,20},{5,7},{6,22},{7,5},{8,24},{9,11},... | collective-permute-start | bytes 663560 | tf_op jit(solution)/shard_map/ppermute | solution.py:377
  55.3 5.7 %collective-permute-start.14 = (bf16[256,384]{1,0:T(8,128)(2,1)S(1)}, bf16[256,384]{1,0:T(8,128)(2,1)S(1)}, u32[]{:S(2)}, u32[]{:S(2)}) collective-permute-start(bf16[256,384]{1,0:T(8,128)(2,1)S(1)} %pad_maximum_fusion.4), channel_id=1, source_target_pairs={{0,2},{1,17},{2,0},{3,19},{4,6},{5,21},{6,4},{7,23},{8,10},{9,25},... | collective-permute-start | bytes 589832 | tf_op jit(solution)/shard_map/ppermute | solution.py:377
  59.7 6.0 %collective-permute-start.10 = (bf16[576,384]{1,0:T(8,128)(2,1)S(1)}, bf16[576,384]{1,0:T(8,128)(2,1)S(1)}, u32[]{:S(2)}, u32[]{:S(2)}) collective-permute-start(bf16[576,384]{1,0:T(8,128)(2,1)S(1)} %pad_maximum_fusion.left), channel_id=1, source_target_pairs={{0,1},{1,0},{2,3},{3,2},{4,5},{5,4},{6,7},{7,6},{8,9},{9,8},{10,11... | collective-permute-start | bytes 1327112 | tf_op jit(solution)/shard_map/ppermute | solution.py:377
  61.2 4.6 %collective-permute-start.15 = (bf16[448,384]{1,0:T(8,128)(2,1)S(1)}, bf16[448,384]{1,0:T(8,128)(2,1)S(1)}, u32[]{:S(2)}, u32[]{:S(2)}) collective-permute-start(bf16[448,384]{1,0:T(8,128)(2,1)S(1)} %pad_maximum_fusion.1), channel_id=1, source_target_pairs={{0,1},{1,0},{2,3},{3,2},{4,5},{5,4},{6,7},{7,6},{8,9},{9,8},{10,11... | collective-permute-start | bytes 1032200 | tf_op jit(solution)/shard_map/ppermute | solution.py:377
  (2 other events, 1.3 us)

commit v3 on v2

v3 whole, which is shorter than its diff:
```python
import functools
import math

import jax
import jax.numpy as jnp
from jax import lax
from jax.experimental import pallas as pl
from jax.experimental.pallas import tpu as pltpu
from jax.sharding import PartitionSpec as P

root_scale = math.sqrt(2.0 / math.pi)
cubic = 0.044715
AXES = ("dp", "context")
TAPS = 5
FIRST = 3
FIRST_LIMIT = 48
HALO = 6
LEAD = 16
VMEM = pl.BlockSpec(memory_space=pltpu.VMEM)
FAR = pl.BlockSpec(memory_space=pltpu.HBM)
bf16 = jnp.bfloat16
f32 = jnp.float32


def gelu_tanh(value):
    inner = jnp.tanh(value * (root_scale + (root_scale * cubic) * (value * value)))
    half = 0.5 * value
    return half + half * inner


def gelu_both(value):
    square = value * value
    inner = jnp.tanh(value * (root_scale + (root_scale * cubic) * square))
    rise = (1.0 - inner * inner) * (root_scale + (3.0 * root_scale * cubic) * square)
    half = 0.5 * value
    return half + half * inner, 0.5 + 0.5 * inner + half * rise


def rounded(value):
    return lax.reduce_precision(value, 8, 7)


def params(limit=24):
    return pltpu.CompilerParams(vmem_limit_bytes=limit * 1024 * 1024)


def together(*values):
    return lax.optimization_barrier(values)


def after(value, *others):
    return together(value, *others)[0]


def first_kernel(
    rows,
    lanes,
    codes,
    positions,
    amounts,
    cot,
    stem_weight,
    own,
    near,
    far,
    weight,
    half_weight,
    base_v,
    pos_s,
    amt_s,
    top,
    bottom,
    weight_v,
    sems,
):
    length = 2 * rows
    tiles = length // 128
    width = cot.shape[1]
    copies = [
        pltpu.make_async_copy(codes, base_v, sems.at[0]),
        pltpu.make_async_copy(positions, pos_s, sems.at[1]),
        pltpu.make_async_copy(amounts, amt_s, sems.at[2]),
        pltpu.make_async_copy(cot.at[pl.ds(0, 16)], top, sems.at[3]),
        pltpu.make_async_copy(cot.at[pl.ds(rows - 16, 16)], bottom, sems.at[4]),
        pltpu.make_async_copy(stem_weight, weight_v, sems.at[5]),
    ]
    for copy in copies:
        copy.start()
    ctx = lax.axis_index("context")
    core = lax.rem(ctx, 2)
    for copy in copies[:5]:
        copy.wait()
    x = jnp.concatenate([base_v[:, 128 * q : 128 * q + 128] for q in range(tiles)], axis=0)
    spot = (
        ctx * length
        + 128 * lax.broadcasted_iota(jnp.int32, x.shape, 0)
        + lax.broadcasted_iota(jnp.int32, x.shape, 1)
    )
    sums = [x] + [jnp.zeros_like(x)] * 3
    for v in range(positions.shape[1]):
        sums[v % 4] = sums[v % 4] + jnp.where(spot == pos_s[0, v], amt_s[0, v], 0)
    x = (sums[0] + sums[1]) + (sums[2] + sums[3])
    x = ((x & 3) + 1).astype(f32).astype(bf16)
    source = lax.broadcasted_iota(jnp.int32, (128, 128), 0)
    target = lax.broadcasted_iota(jnp.int32, (128, 128), 1)

    def picked(parity):
        left = (source == 2 * target + parity).astype(f32).astype(bf16)
        right = (source == 2 * (target - 64) + parity).astype(f32).astype(bf16)
        low = jnp.dot(x, left, preferred_element_type=f32)
        high = jnp.dot(x, right, preferred_element_type=f32)
        parts = [low[2 * q : 2 * q + 1] + high[2 * q + 1 : 2 * q + 2] for q in range(tiles // 2)]
        return jnp.concatenate(parts + [jnp.zeros((1, lanes - rows), f32)], axis=1)

    both = jnp.concatenate([picked(0), picked(1), jnp.zeros((6, lanes), f32)], axis=0)
    lane = lax.broadcasted_iota(jnp.int32, both.shape, 1)
    shifted = pltpu.roll(both, HALO, 1)
    last = jnp.where(lane < HALO, pltpu.roll(both, lanes - (rows - HALO), 1), 0.0)
    ahead = (lane >= rows + HALO) & (lane < rows + 2 * HALO)
    first = jnp.where(ahead, pltpu.roll(both, rows + HALO, 1), 0.0)
    blank = jnp.zeros((8, lanes), f32)
    pad = jnp.zeros((2, lanes - width), f32)

    def message(edge, grads):
        grads = jnp.concatenate([grads, pad], axis=1)
        return jnp.concatenate([edge, grads, jnp.zeros((6, lanes), f32)], axis=0)

    head = message(first, top[...].astype(f32)[0:2])
    tail = message(last, bottom[...].astype(f32)[14:16])
    own[...] = jnp.concatenate([shifted, blank], axis=0).astype(bf16)
    near[...] = jnp.where(core == 0, tail, head).astype(bf16)
    far[...] = jnp.where(core == 0, head, tail).astype(bf16)
    copies[5].wait()
    stem_terms(weight_v, weight, half_weight)


def stem_terms(weight, out, half_out):
    width = weight.shape[2]
    zero = jnp.zeros((1, width), f32)
    even, odd = orders(weight.shape[0])

    def rows(order):
        return jnp.concatenate(
            [
                zero if k is None else weight[k, a : a + 1, :]
                for a in range(4)
                for k in order
            ],
            axis=0,
        )

    def terms(full):
        high = full.astype(bf16)
        left = full - high.astype(f32)
        middle = left.astype(bf16)
        low = (left - middle.astype(f32)).astype(bf16)
        return jnp.concatenate([high, middle, low], axis=0)

    evens, odds = rows(even), rows(odd)
    half = width // 2
    upper = lax.rem(lax.axis_index("dp"), 2) == 1
    out[...] = terms(jnp.concatenate([evens, odds], axis=1))
    mine = [jnp.where(upper, v[:, half:], v[:, :half]) for v in (evens, odds)]
    half_out[...] = terms(jnp.concatenate(mine, axis=1))


def orders(taps):
    even = [None] + list(range(taps - 2, 0, -2)) + list(range(taps - 1, -1, -2))
    odd = list(range(taps - 1, -1, -2)) + list(range(taps - 2, 0, -2)) + [None]
    return even, odd


def one_hot(codes, lanes, shift):
    even = jnp.broadcast_to(codes[0:1], (8, lanes))
    odd = jnp.broadcast_to(codes[1:2], (8, lanes))
    even = pltpu.roll(even, (2 * lanes - 8 + shift) % lanes, 1, stride=1, stride_axis=0)
    odd = pltpu.roll(odd, (2 * lanes - 7 + shift) % lanes, 1, stride=1, stride_axis=0)
    near = jnp.concatenate([even, odd], axis=0)
    return jnp.concatenate([(near == a + 1.0).astype(f32) for a in range(4)], axis=0).astype(bf16)


def shifted_gates(codes, first, total, weight, rows, stem, gated):
    used = rows + 128
    half = weight.shape[1] // 2
    quarter = half // 4
    hot = one_hot(codes, codes.shape[1], 0)[:, :used]
    hot = jnp.concatenate([hot, hot, hot], axis=0)
    stem[...] = lax.dot_general(
        weight[...], hot, (((0,), (0,)), ((), ())), preferred_element_type=f32
    )
    spot = first - 2 + lax.broadcasted_iota(jnp.int32, (1, used), 1)
    inside = (spot >= 0) & (spot < total)
    step = 16
    for c in range(0, half, step):
        even = gelu_tanh(stem[c : c + step, :])
        odd = gelu_tanh(stem[half + c : half + c + step, :])
        pooled = (0.5 * (even + odd)).astype(bf16).astype(f32)
        value = jnp.where(inside, gelu_tanh(pooled), 0.0)
        for t in range(TAPS):
            moved = value if t == 0 else pltpu.roll(value, used - t, 1)
            at = (c // quarter * TAPS + t) * quarter + c % quarter
            gated[at : at + step, :] = moved[:, :rows].astype(bf16)


def own_kernel(rows, total, own, near, far, weight, cot, out, stem, gated, cot_v, sem):
    copy = pltpu.make_async_copy(cot, cot_v, sem)
    copy.start()
    first = lax.axis_index("context") * rows
    codes = (own[...].astype(f32) + near[...].astype(f32) + far[...].astype(f32))[0:8]
    shifted_gates(codes, first, total, weight, rows, stem, gated)
    copy.wait()
    out[...] = jnp.dot(gated[...], cot_v[...], preferred_element_type=f32)


def pair_kernel(rows, total, codes, weight, gated, stem):
    first = lax.axis_index("context") * rows
    shifted_gates(codes[...].astype(f32)[0:8], first, total, weight, rows, stem, gated)


def sum_kernel(part, gated, cot, sent, kept):
    core = lax.rem(lax.axis_index("context"), 2)
    size = sent.shape[0]
    for which, out in ((1 - core, sent), (core, kept)):
        span = pl.ds(pl.multiple_of(which * size, 16), size)
        value = part[span, :] + jnp.dot(gated[span, :], cot[...], preferred_element_type=f32)
        out[...] = value.astype(out.dtype)


def split_kernel(value, got, sent, kept):
    x = lax.rem(lax.axis_index("context") // 2, 2)
    size = sent.shape[0]
    for which, out in ((1 - x, sent), (x, kept)):
        span = pl.ds(pl.multiple_of(which * size, 16), size)
        out[...] = (value[span, :] + got[span, :].astype(f32)).astype(out.dtype)


def back_kernel(rows, conv, cot, back, ext, sem):
    width = cot.shape[1]
    copy = pltpu.make_async_copy(cot, ext.at[pl.ds(LEAD, rows)], sem)
    copy.start()
    blank = jnp.zeros((LEAD, width), bf16)
    ext[0:LEAD, :] = blank
    ext[LEAD + rows :, :] = blank
    copy.wait()
    for t in range(TAPS):
        start = LEAD + 2 - t
        term = turned(ext[start : start + rows, :], conv[t])
        back[...] = term if t == 0 else back[...] + term


def turned(left, right):
    return lax.dot_general(left, right, (((1,), (1,)), ((), ())), preferred_element_type=f32)


def edge_terms(near, far, conv):
    width = conv.shape[1]
    core = lax.rem(lax.axis_index("context"), 2)
    near_v, far_v = near[...].astype(f32), far[...].astype(f32)
    before = jnp.where(core == 0, far_v, near_v)[8:10, :width]
    behind = jnp.where(core == 0, near_v, far_v)[8:10, :width]
    none = jnp.zeros((6, width), f32)
    one = jnp.zeros((1, width), f32)
    top = jnp.concatenate([before, none], axis=0).astype(bf16)
    top_late = jnp.concatenate([before[1:2], one, none], axis=0).astype(bf16)
    end = jnp.concatenate([none, behind], axis=0).astype(bf16)
    end_late = jnp.concatenate([none, one, behind[0:1]], axis=0).astype(bf16)
    first = turned(top, conv[4]) + turned(top_late, conv[3])
    last = turned(end, conv[0]) + turned(end_late, conv[1])
    return first, last


def slope_kernel(
    rows, total, own, near, far, weight, back, conv, cot, d_pooled, stem_part, gated, pooled, stem, cot_v, sem
):
    copy = pltpu.make_async_copy(cot, cot_v, sem)
    copy.start()
    lanes = own.shape[1]
    width = cot.shape[1]
    padded = rows + 2 * LEAD
    codes = (own[...].astype(f32) + near[...].astype(f32) + far[...].astype(f32))[0:8]
    hot = one_hot(codes, lanes, LEAD - 2)[:, :padded]
    hot = jnp.concatenate([hot, hot, hot], axis=0)
    stem[...] = lax.dot_general(
        hot, weight[...], (((0,), (0,)), ((), ())), preferred_element_type=f32
    )
    mine = one_hot(codes, lanes, lanes - 2)
    first = lax.axis_index("context") * rows
    for edge in (0, LEAD + rows):
        act = 0.5 * (
            gelu_tanh(stem[edge : edge + LEAD, :width]) + gelu_tanh(stem[edge : edge + LEAD, width:])
        )
        act = act.astype(bf16).astype(f32)
        spot = first - LEAD + edge + lax.broadcasted_iota(jnp.int32, (LEAD, 1), 0)
        inside = (spot >= 0) & (spot < total)
        gated[edge : edge + LEAD, :] = jnp.where(inside, gelu_tanh(act), 0.0).astype(bf16)
    top, end = edge_terms(near, far, conv)
    none = jnp.zeros((24, width), f32)
    copy.wait()
    step = 32
    for r in range(0, rows, step):
        even = stem[LEAD + r : LEAD + r + step, :width]
        odd = stem[LEAD + r : LEAD + r + step, width:]
        even, even_slope = gelu_both(even)
        odd, odd_slope = gelu_both(odd)
        low = (0.5 * (even + odd)).astype(bf16)
        pooled[r : r + step, :] = low
        gate, slope = gelu_both(low.astype(f32))
        gated[LEAD + r : LEAD + r + step, :] = gate.astype(bf16)
        rise = back[r : r + step, :]
        if r == 0:
            rise = rise + jnp.concatenate([top, none], axis=0)
        if r + step == rows:
            rise = rise + jnp.concatenate([none, end], axis=0)
        grad = cot_v[r : r + step, :].astype(f32) + rise * slope
        d_pooled[r : r + step, :] = grad.astype(bf16)
        half = 0.5 * grad
        stem[LEAD + r : LEAD + r + step, :width] = half * even_slope
        stem[LEAD + r : LEAD + r + step, width:] = half * odd_slope
    grads = jnp.dot(
        mine[:, :rows], stem[LEAD : LEAD + rows, :].astype(bf16), preferred_element_type=f32
    )
    even, odd = orders(stem_part.shape[0] // 4 - 1)
    for k in range(len(even) - 1):
        for a in range(4):
            p, q = 16 * a + even.index(k), 16 * a + odd.index(k)
            stem_part[4 * k + a : 4 * k + a + 1, :] = (
                grads[p : p + 1, :width] + grads[q : q + 1, width:]
            )
    stem_part[stem_part.shape[0] - 4 :, :] = jnp.zeros((4, width), f32)


def feature_kernel(rows, gated, pooled, conv, out):
    acc = pooled[...].astype(f32)
    for t in range(TAPS):
        start = LEAD - 2 + t
        acc = acc + jnp.dot(gated[start : start + rows, :], conv[t], preferred_element_type=f32)
    out[...] = acc.astype(bf16)


def put_pieces(flip, chains, out, room, sems):
    ctx = lax.axis_index("context")
    core = lax.rem(ctx, 2)
    x = lax.rem(ctx // 2, 2)
    y = lax.rem(lax.axis_index("dp"), 2)
    unit = room.shape[1]
    half = out.shape[1] // 2
    from_core = lax.rem(core + flip, 2)
    copies = []
    at = 0
    for chain, (piece, tap, taps) in enumerate(chains):
        x_first = jnp.where(from_core == chain, 1, 0)
        for p in range(4):
            one, two = p % 2, p // 2
            dx = jnp.where(x_first == 1, one, two)
            dy = one + two - dx
            from_x, from_y = lax.rem(x + dx, 2), lax.rem(y + dy, 2)
            channel = from_y * half + (2 * from_core + from_x) * unit
            for t in range(taps):
                low = (p * taps + t) * unit
                room[at + t] = piece[low : low + unit, :].astype(f32)
            copy = pltpu.make_async_copy(
                room.at[pl.ds(at, taps)],
                out.at[pl.ds(tap, taps), pl.ds(pl.multiple_of(channel, 16), unit)],
                sems.at[len(copies)],
            )
            copy.start()
            copies.append(copy)
            at += taps
    return copies


def place_kernel(left, right, out, room, sems):
    for copy in put_pieces(0, ((left, 0, FIRST), (right, FIRST, TAPS - FIRST)), out, room, sems):
        copy.wait()


def last_kernel(left, right, stem, whole, out, stem_out, room, sems):
    del whole
    copies = put_pieces(
        1, ((left, 0, FIRST), (right, FIRST, TAPS - FIRST)), out, room, sems
    )
    core = lax.rem(lax.axis_index("context"), 2)
    mine = stem[...].astype(bf16).astype(f32)
    other = right[right.shape[0] - stem.shape[0] :, :].astype(f32)
    whole_stem = jnp.concatenate(
        [jnp.where(core == 0, mine, other), jnp.where(core == 0, other, mine)], axis=0
    )
    for k in range(stem_out.shape[0]):
        stem_out[k] = whole_stem[4 * k : 4 * k + 4, :]
    for copy in copies:
        copy.wait()


def per_device(codes, variant_pos, variant_shift, stem_weight, conv_weight, cotangent):
    n_dp, n_ctx = lax.axis_size("dp"), lax.axis_size("context")
    devices = n_dp * n_ctx
    length = codes.shape[1]
    rows = length // 2
    taps, _, width = stem_weight.shape
    half = width // 2
    unit = half // 4
    total = rows * n_ctx
    lanes = -(-(rows + 256) // 128) * 128
    core = lax.axis_index("context") % 2
    cot = cotangent[0]
    x_bit, y_bit = 2, n_ctx

    def swap(value, even_bit, odd_bit=None):
        odd_bit = even_bit if odd_bit is None else odd_bit
        pairs = [(i, i ^ (odd_bit if i & 1 else even_bit)) for i in range(devices)]
        return lax.ppermute(value, AXES, pairs)

    def call(kernel, out, operands, scratch=(), **options):
        shapes = [jax.ShapeDtypeStruct(o[0], o[1]) for o in out]
        specs = [o[2] if len(o) > 2 else VMEM for o in out]
        options.setdefault("compiler_params", params())
        return pl.pallas_call(
            kernel,
            out_shape=shapes,
            in_specs=[spec for _, spec in operands],
            out_specs=specs,
            scratch_shapes=list(scratch),
            **options,
        )(*[value for value, _ in operands])

    def near_by(*values):
        return [(value, VMEM) for value in values]

    def far_off(*values):
        return [(pltpu.with_memory_space_constraint(value, pltpu.HBM), FAR) for value in values]

    outward = {}
    for d in range(n_dp):
        for c in range(n_ctx):
            other = c + 1 if c & 1 else c - 1
            if 0 <= other < n_ctx:
                outward[d * n_ctx + c] = d * n_ctx + other

    pair_cot = swap(cot, y_bit)
    dma = pltpu.SemaphoreType.DMA
    edge = ((16, lanes), bf16)
    own, near, far, weight, half_weight = call(
        functools.partial(first_kernel, rows, lanes),
        [edge, edge, edge, ((192, 2 * width), bf16), ((192, width), bf16)],
        far_off(codes, variant_pos, variant_shift, cot, stem_weight),
        [
            pltpu.VMEM((1, length), jnp.int32),
            pltpu.SMEM(variant_pos.shape, jnp.int32),
            pltpu.SMEM(variant_pos.shape, jnp.int32),
            pltpu.VMEM((16, width), bf16),
            pltpu.VMEM((16, width), bf16),
            pltpu.VMEM(stem_weight.shape, f32),
            dma((6,)),
        ],
        compiler_params=params(FIRST_LIMIT),
    )
    near = swap(near, 1)
    cost = pl.CostEstimate(
        flops=2 * TAPS * rows * width * width, bytes_accessed=4 << 20, transcendentals=0
    )
    padded = rows + 2 * LEAD
    (back,) = call(
        functools.partial(back_kernel, rows),
        [((rows, width), f32)],
        near_by(conv_weight) + far_off(after(cot, far)),
        [pltpu.VMEM((padded, width), bf16), dma],
        cost_estimate=cost,
    )
    far = lax.ppermute(far, AXES, list(outward.items()))
    pair_codes = swap(own + near + far, y_bit)
    stem_half = pltpu.VMEM((width, rows + 128), f32)
    gates = ((TAPS * half, rows), bf16)
    (part,) = call(
        functools.partial(own_kernel, rows, total),
        [((TAPS * half, width), f32)],
        near_by(own, near, far, half_weight) + far_off(cot),
        [stem_half, pltpu.VMEM(*gates), pltpu.VMEM((rows, width), bf16), dma],
    )
    (pair_gates,) = call(
        functools.partial(pair_kernel, rows, total),
        [gates],
        near_by(pair_codes, half_weight),
        [stem_half],
    )
    size = TAPS * half // 2
    sent, kept = call(
        sum_kernel, [((size, width), bf16), ((size, width), f32)], near_by(part, pair_gates, pair_cot)
    )
    got = swap(sent, 1)
    size //= 2
    sent, kept = call(
        split_kernel, [((size, width), bf16), ((size, width), f32)], near_by(kept, got)
    )
    got = swap(sent, x_bit)
    d_pooled, stem_part, gated, pooled = call(
        functools.partial(slope_kernel, rows, total),
        [
            ((rows, width), bf16),
            ((4 * taps + 4, width), f32),
            ((padded, width), bf16),
            ((rows, width), bf16),
        ],
        near_by(after(own, sent), near, far, weight, back, conv_weight) + far_off(cot),
        [pltpu.VMEM((padded, 2 * width), f32), pltpu.VMEM((rows, width), bf16), dma],
        cost_estimate=cost,
    )
    value = kept + got.astype(f32)

    few = stem_part.shape[0] // 2
    stem_part = after(stem_part, value)
    stem_got = swap(lax.dynamic_slice_in_dim(stem_part, (1 - core) * few, few, 0).astype(bf16), 1)
    stem_sum = lax.dynamic_slice_in_dim(stem_part, core * few, few, 0) + stem_got.astype(f32)

    cut = FIRST * unit
    rest = size - cut
    left = value[:cut]
    right = jnp.concatenate([value[cut:], stem_sum], axis=0)
    others = [1 << k for k in range(devices.bit_length() - 1) if (1 << k) not in (1, x_bit, y_bit)]
    for k, b in enumerate(others):
        odd_b = others[(k + 1) % len(others)]
        left, right = rounded(left), rounded(right)
        if k == len(others) - 1:
            pooled = after(pooled, right)
        left, right = [v + swap(v.astype(bf16), b, odd_b).astype(f32) for v in (left, right)]
    (features,) = call(
        functools.partial(feature_kernel, rows),
        [((rows, width), bf16)],
        near_by(gated, pooled, conv_weight),
        cost_estimate=cost,
    )
    left, features = together(left, features)
    left = left.astype(bf16)
    stem_sum = right[rest:]
    right = right[:rest].astype(bf16)

    whole = ((TAPS, width, width), f32, FAR)

    for one, two in ((x_bit, y_bit), (y_bit, x_bit)):
        got_left = swap(left, one, two)
        stem_sum = rounded(stem_sum)
        got_right = swap(jnp.concatenate([right, stem_sum.astype(bf16)], axis=0), two, one)
        stem_sum = stem_sum + got_right[right.shape[0] :].astype(f32)
        left = jnp.concatenate([left, got_left], axis=0)
        right = jnp.concatenate([right, got_right[: right.shape[0]]], axis=0)
    got_left = swap(left, 1)
    got_right = swap(jnp.concatenate([right, stem_sum.astype(bf16)], axis=0), 1)
    (conv_grad,) = call(
        place_kernel,
        [whole],
        near_by(left, right),
        [pltpu.VMEM((TAPS * 4, unit, width), f32), dma((8,))],
    )
    conv_grad, stem_grad = call(
        last_kernel,
        [whole, (stem_weight.shape, f32)],
        near_by(got_left, got_right, stem_sum) + far_off(conv_grad),
        [pltpu.VMEM((TAPS * 4, unit, width), f32), dma((8,))],
        input_output_aliases={3: 0},
    )
    return (features[None], d_pooled[None], conv_grad, stem_grad)


def solution(mesh):
    placed = (P("dp", "context"), P("dp", None), P("dp", None), P(), P(), P("dp", "context", None))
    return jax.shard_map(
        per_device,
        mesh=mesh,
        in_specs=placed,
        out_specs=(P("dp", "context", None), P("dp", "context", None), P(), P()),
        check_vma=False,
    )
```

time: 68.7 us -> 54.8 us (0.80)
  waiting for transfers between devices: 23.7 us -> 17.5 us
  local copies, waits for them, and re-layouts: 5.8 us -> 0.07 us
  starting transfers between devices: 20.5 us -> 19.3 us
  other arithmetic: 1.52 us -> 0.46 us
    ppermute x14 -> x16, waiting for transfers between devices: 23.7 us -> 17.5 us  [swap(): return lax.ppermute(value, AXES, pairs)]
    unnamed x20 -> x2, local copies, waits for them, and re-layouts: 5.73 us -> 0.01 us
    add x3 -> x5, other arithmetic: 1.15 us -> 0.14 us  [the longest x2 0.09 us: per_device(): v + swap(v.astype(bf16), b, odd_b).astype(f32)]
    ppermute x14 -> x16, starting transfers between devices: 19.1 us -> 18.7 us  [swap(): return lax.ppermute(value, AXES, pairs)]
    pallas_call x9 -> x10, Pallas kernels: 15.9 us -> 16.3 us  [call(): pl.pallas_call(kernel, out_shape=shapes, in_specs=[spec for _, spec in op...]
  transfers between devices with their start and end apart: 16 -> 17, of which waited for: 9 -> 9; matrix products, arithmetic and copies ran while one was open for 1% -> 1% of each run, Pallas kernels for 16% -> 25%
where the time goes in v3:
time: 54.8 us; the launch traced here: 54.5 us
  starting transfers between devices  19.3 us (35%)
  waiting for transfers between devices  17.5 us (32%)
  Pallas kernels  16.3 us (30%)
  between operations  0.88 us (2%)
    ppermute x16, starting transfers between devices, swap(): return lax.ppermute(value, AXES, pairs)  18.7 us
    ppermute x16, waiting for transfers between devices, swap(): return lax.ppermute(value, AXES, pairs)  17.5 us
    pallas_call x10, Pallas kernels, call(): pl.pallas_call(kernel, out_shape=shapes, in_specs=[spec for _, spec in op...  16.3 us
  transfers between devices with their start and end apart: 17, of which 9 were waited for; matrix products, arithmetic and copies ran while one was open for 1% of the time, Pallas kernels for 25%

profile of v3, /device:TPU:0, one launch (start us, length us, event | category | flops | bytes accessed | tf_op | source)
XLA Modules:
  0.0 54.5 jit_solution(15519130959720675130)
XLA Ops:
  0.6 3.0 %collective-permute-start.3 = (bf16[512,384]{1,0:T(8,128)(2,1)}, bf16[512,384]{1,0:T(8,128)(2,1)S(1)}, u32[]{:S(2)}, u32[]{:S(2)}) collective-permute-start(bf16[512,384]{1,0:T(8,128)(2,1)} %bitcast.3), channel_id=1, source_target_pairs={{0,16},{1,17},{2,18},{3,19},{4,20},{5,21},{6,22},{7,23},{8,24},{9,... | collective-permute-start | bytes 1179656 | tf_op jit(solution)/shard_map/ppermute | solution.py:411
  3.7 1.3 %shard_map.93 = (bf16[16,768]{1,0:T(8,128)(2,1)S(1)}, bf16[16,768]{1,0:T(8,128)(2,1)S(1)}, bf16[16,768]{1,0:T(8,128)(2,1)S(1)}, bf16[192,768]{1,0:T(8,128)(2,1)S(1)}, bf16[192,384]{1,0:T(8,128)(2,1)S(1)}) custom-call(s32[1,1024]{1,0:T(1,128)} %codes.1, s32[1,64]{1,0:T(1,128)} %positions.1, s32[1,64]{1,0:T(1,128)} %amounts.1, bf16[512,384]{1,0:T(8,128)(2,1)} %bitcast.4, ...), custom_call_target="tpu_custom_call" | custom-call | tf_op jit(solution)/shard_map/pallas_call | solution.py:417
  6.4 1.7 %shard_map.94.part = f32[960,384]{1,0:T(8,128)S(1)} custom-call(bf16[16,768]{1,0:T(8,128)(2,1)S(1)} %get-tuple-element.33.own, bf16[16,768]{1,0:T(8,128)(2,1)S(1)} %collective-permute-done.near, bf16[16,768]{1,0:T(8,128)(2,1)S(1)} %collective-permute-done.1.far, bf16[192,384]{1,0:T(8,128)(2,1)S(1)} %get-tuple-element.28.weight, bf16[512,384]{1,0:T(8,128)(2,1)} %bitcast.5), custom_call_target="tpu_custom_call" | custom-call | tf_op jit(solution)/shard_map/pallas_call | solution.py:417
  8.1 5.2 %collective-permute-done.2.codes = bf16[16,768]{1,0:T(8,128)(2,1)S(1)} collective-permute-done((bf16[16,768]{1,0:T(8,128)(2,1)S(1)}, bf16[16,768]{1,0:T(8,128)(2,1)S(1)}, u32[]{:S(2)}, u32[]{:S(2)}) %collective-permute-start.2) | collective-permute-done | bytes 24608 | tf_op jit(solution)/shard_map/ppermute | solution.py:411
  13.3 0.9 %shard_map.95.gated = bf16[960,512]{1,0:T(8,128)(2,1)S(1)} custom-call(bf16[16,768]{1,0:T(8,128)(2,1)S(1)} %collective-permute-done.2.codes, bf16[192,384]{1,0:T(8,128)(2,1)S(1)} %get-tuple-element.28.weight), custom_call_target="tpu_custom_call" | custom-call | tf_op jit(solution)/shard_map/pallas_call | solution.py:417
  14.2 0.7 %shard_map.96 = (bf16[480,384]{1,0:T(8,128)(2,1)S(1)}, f32[480,384]{1,0:T(8,128)S(1)}) custom-call(f32[960,384]{1,0:T(8,128)S(1)} %shard_map.94.part, bf16[960,512]{1,0:T(8,128)(2,1)S(1)} %shard_map.95.gated, bf16[512,384]{1,0:T(8,128)(2,1)S(1)} %collective-permute-done.3.cot), custom_call_target="tpu_custom_call" | custom-call | tf_op jit(solution)/shard_map/pallas_call | solution.py:417
  15.4 1.3 %collective-permute-done.4.got = bf16[480,384]{1,0:T(8,128)(2,1)S(1)} collective-permute-done((bf16[480,384]{1,0:T(8,128)(2,1)S(1)}, bf16[480,384]{1,0:T(8,128)(2,1)S(1)}, u32[]{:S(2)}, u32[]{:S(2)}) %collective-permute-start.4) | collective-permute-done | bytes 368672 | tf_op jit(solution)/shard_map/ppermute | solution.py:411
  16.8 2.3 %collective-permute-start.5 = (bf16[240,384]{1,0:T(8,128)(2,1)S(1)}, bf16[240,384]{1,0:T(8,128)(2,1)S(1)}, u32[]{:S(2)}, u32[]{:S(2)}) collective-permute-start(bf16[240,384]{1,0:T(8,128)(2,1)S(1)} %get-tuple-element.32), channel_id=1, source_target_pairs={{0,2},{1,3},{2,0},{3,1},{4,6},{5,7},{6,4},{7,5},{8,10},{9,11},{10,... | collective-permute-start | bytes 552968 | tf_op jit(solution)/shard_map/ppermute | solution.py:411
  19.1 2.4 %shard_map.98.back = f32[512,384]{1,0:T(8,128)S(1)} custom-call(bf16[5,384,384]{2,1,0:T(8,128)(2,1)S(1)} %copy-done, bf16[512,384]{1,0:T(8,128)(2,1)} %bitcast.6), custom_call_target="tpu_custom_call" | custom-call | flops 754974720 | bytes 4194304 | tf_op jit(solution)/shard_map/pallas_call | solution.py:417
  21.5 4.1 %shard_map.99 = (bf16[512,384]{1,0:T(8,128)(2,1)}, f32[64,384]{1,0:T(8,128)S(1)}, bf16[544,384]{1,0:T(8,128)(2,1)S(1)}, bf16[512,384]{1,0:T(8,128)(2,1)S(1)}) custom-call(bf16[16,768]{1,0:T(8,128)(2,1)S(1)} %get-tuple-element.33.own, bf16[16,768]{1,0:T(8,128)(2,1)S(1)} %collective-permute-done.near, bf16[16,768]{1,0:T(8,128)(2,1)S(1)} %collective-permute-done.1.far, ...), custom_call_target="tpu_custom_call" | custom-call | flops 754974720 | bytes 4194304 | tf_op jit(solution)/shard_map/pallas_call | solution.py:417
  25.7 1.6 %collective-permute-start.6 = (bf16[144,384]{1,0:T(8,128)(2,1)S(1)}, bf16[144,384]{1,0:T(8,128)(2,1)S(1)}, u32[]{:S(2)}, u32[]{:S(2)}) collective-permute-start(bf16[144,384]{1,0:T(8,128)(2,1)S(1)} %fusion), channel_id=1, source_target_pairs={{0,4},{1,9},{2,6},{3,11},{4,0},{5,13},{6,2},{7,15},{8,12},{9,1},{1... | collective-permute-start | bytes 331784 | tf_op jit(solution)/shard_map/ppermute | solution.py:411
  27.4 1.1 %collective-permute-start.9 = (bf16[128,384]{1,0:T(8,128)(2,1)S(1)}, bf16[128,384]{1,0:T(8,128)(2,1)S(1)}, u32[]{:S(2)}, u32[]{:S(2)}) collective-permute-start(bf16[128,384]{1,0:T(8,128)(2,1)S(1)} %fusion.1), channel_id=1, source_target_pairs={{0,4},{1,9},{2,6},{3,11},{4,0},{5,13},{6,2},{7,15},{8,12},{9,1},{1... | collective-permute-start | bytes 294920 | tf_op jit(solution)/shard_map/ppermute | solution.py:411
  28.6 3.2 %collective-permute-done.6 = bf16[144,384]{1,0:T(8,128)(2,1)S(1)} collective-permute-done((bf16[144,384]{1,0:T(8,128)(2,1)S(1)}, bf16[144,384]{1,0:T(8,128)(2,1)S(1)}, u32[]{:S(2)}, u32[]{:S(2)}) %collective-permute-start.6) | collective-permute-done | bytes 110624 | tf_op jit(solution)/shard_map/ppermute | solution.py:411
  31.7 2.1 %collective-permute-start.7 = (bf16[144,384]{1,0:T(8,128)(2,1)S(1)}, bf16[144,384]{1,0:T(8,128)(2,1)S(1)}, u32[]{:S(2)}, u32[]{:S(2)}) collective-permute-start(bf16[144,384]{1,0:T(8,128)(2,1)S(1)} %fusion.2), channel_id=1, source_target_pairs={{0,8},{1,5},{2,10},{3,7},{4,12},{5,1},{6,14},{7,3},{8,0},{9,13},{1... | collective-permute-start | bytes 331784 | tf_op jit(solution)/shard_map/ppermute | solution.py:411
  33.9 2.0 %collective-permute-start.13 = (bf16[128,384]{1,0:T(8,128)(2,1)S(1)}, bf16[128,384]{1,0:T(8,128)(2,1)S(1)}, u32[]{:S(2)}, u32[]{:S(2)}) collective-permute-start(bf16[128,384]{1,0:T(8,128)(2,1)S(1)} %get-tuple-element.48), channel_id=1, source_target_pairs={{0,8},{1,5},{2,10},{3,7},{4,12},{5,1},{6,14},{7,3},{8,0},{9,13},{1... | collective-permute-start | bytes 294920 | tf_op jit(solution)/shard_map/ppermute | solution.py:411
  35.8 2.1 %shard_map.100 = bf16[512,384]{1,0:T(8,128)(2,1)} custom-call(bf16[544,384]{1,0:T(8,128)(2,1)S(1)} %get-tuple-element.36.gated, bf16[512,384]{1,0:T(8,128)(2,1)S(1)} %get-tuple-element.40.pooled, bf16[5,384,384]{2,1,0:T(8,128)(2,1)S(1)} %copy-done), custom_call_target="tpu_custom_call" | custom-call | flops 754974720 | bytes 4194304 | tf_op jit(solution)/shard_map/pallas_call | solution.py:417
  38.1 1.4 %collective-permute-start.10 = (bf16[144,384]{1,0:T(8,128)(2,1)S(1)}, bf16[144,384]{1,0:T(8,128)(2,1)S(1)}, u32[]{:S(2)}, u32[]{:S(2)}) collective-permute-start(bf16[144,384]{1,0:T(8,128)(2,1)S(1)} %convert_add_fusion.1), channel_id=1, source_target_pairs={{0,2},{1,17},{2,0},{3,19},{4,6},{5,21},{6,4},{7,23},{8,10},{9,25},... | collective-permute-start | bytes 331784 | tf_op jit(solution)/shard_map/ppermute | solution.py:411
  40.2 1.1 %collective-permute-start.14 = (bf16[128,384]{1,0:T(8,128)(2,1)S(1)}, bf16[128,384]{1,0:T(8,128)(2,1)S(1)}, u32[]{:S(2)}, u32[]{:S(2)}) collective-permute-start(bf16[128,384]{1,0:T(8,128)(2,1)S(1)} %pad_maximum_fusion.5), channel_id=1, source_target_pairs={{0,16},{1,3},{2,18},{3,1},{4,20},{5,7},{6,22},{7,5},{8,24},{9,11},... | collective-permute-start | bytes 294920 | tf_op jit(solution)/shard_map/ppermute | solution.py:411
  41.3 2.4 %collective-permute-done.10 = bf16[144,384]{1,0:T(8,128)(2,1)S(1)} collective-permute-done((bf16[144,384]{1,0:T(8,128)(2,1)S(1)}, bf16[144,384]{1,0:T(8,128)(2,1)S(1)}, u32[]{:S(2)}, u32[]{:S(2)}) %collective-permute-start.10) | collective-permute-done | bytes 110624 | tf_op jit(solution)/shard_map/ppermute | solution.py:411
  43.7 1.2 %collective-permute-start.11 = (bf16[288,384]{1,0:T(8,128)(2,1)S(1)}, bf16[288,384]{1,0:T(8,128)(2,1)S(1)}, u32[]{:S(2)}, u32[]{:S(2)}) collective-permute-start(bf16[288,384]{1,0:T(8,128)(2,1)S(1)} %pad_maximum_fusion.3), channel_id=1, source_target_pairs={{0,16},{1,3},{2,18},{3,1},{4,20},{5,7},{6,22},{7,5},{8,24},{9,11},... | collective-permute-start | bytes 663560 | tf_op jit(solution)/shard_map/ppermute | solution.py:411
  45.0 1.4 %collective-permute-start.15 = (bf16[224,384]{1,0:T(8,128)(2,1)S(1)}, bf16[224,384]{1,0:T(8,128)(2,1)S(1)}, u32[]{:S(2)}, u32[]{:S(2)}) collective-permute-start(bf16[224,384]{1,0:T(8,128)(2,1)S(1)} %pad_maximum_fusion.4), channel_id=1, source_target_pairs={{0,2},{1,17},{2,0},{3,19},{4,6},{5,21},{6,4},{7,23},{8,10},{9,25},... | collective-permute-start | bytes 516104 | tf_op jit(solution)/shard_map/ppermute | solution.py:411
  46.4 3.9 %collective-permute-done.11 = bf16[288,384]{1,0:T(8,128)(2,1)S(1)} collective-permute-done((bf16[288,384]{1,0:T(8,128)(2,1)S(1)}, bf16[288,384]{1,0:T(8,128)(2,1)S(1)}, u32[]{:S(2)}, u32[]{:S(2)}) %collective-permute-start.11) | collective-permute-done | bytes 221216 | tf_op jit(solution)/shard_map/ppermute | solution.py:411
  51.1 1.2 %shard_map.101.whole = f32[5,384,384]{2,1,0:T(8,128)} custom-call(bf16[576,384]{1,0:T(8,128)(2,1)S(1)} %pad_maximum_fusion.left, bf16[384,384]{1,0:T(8,128)(2,1)S(1)} %pad_maximum_fusion.2.right), custom_call_target="tpu_custom_call" | custom-call | tf_op jit(solution)/shard_map/pallas_call | solution.py:417
  52.7 1.8 %shard_map.102 = (f32[5,384,384]{2,1,0:T(8,128)}, f32[15,4,384]{2,1,0:T(4,128)}) custom-call(bf16[576,384]{1,0:T(8,128)(2,1)S(1)} %collective-permute-done.12.left, bf16[416,384]{1,0:T(8,128)(2,1)S(1)} %collective-permute-done.16.right, f32[32,384]{1,0:T(8,128)S(1)} %get-tuple-element.47.stem, ...), custom_call_target="tpu_custom_call", output_to_operand_aliasing={{0}: (3, {})} | custom-call | tf_op jit(solution)/shard_map/pallas_call | solution.py:417
  (45 shorter events, 4.1 us)
Async XLA Ops:
  0.6 13.5 %collective-permute-start.3 = (bf16[512,384]{1,0:T(8,128)(2,1)}, bf16[512,384]{1,0:T(8,128)(2,1)S(1)}, u32[]{:S(2)}, u32[]{:S(2)}) collective-permute-start(bf16[512,384]{1,0:T(8,128)(2,1)} %bitcast.3), channel_id=1, source_target_pairs={{0,16},{1,17},{2,18},{3,19},{4,20},{5,21},{6,22},{7,23},{8,24},{9,... | collective-permute-start | bytes 1179656 | tf_op jit(solution)/shard_map/ppermute | solution.py:411
  5.0 1.3 %collective-permute-start = (bf16[16,768]{1,0:T(8,128)(2,1)S(1)}, bf16[16,768]{1,0:T(8,128)(2,1)S(1)}, u32[]{:S(2)}, u32[]{:S(2)}) collective-permute-start(bf16[16,768]{1,0:T(8,128)(2,1)S(1)} %get-tuple-element.26), channel_id=1, source_target_pairs={{0,1},{1,0},{2,3},{3,2},{4,5},{5,4},{6,7},{7,6},{8,9},{9,8},{10,11... | collective-permute-start | bytes 73736 | tf_op jit(solution)/shard_map/ppermute | solution.py:411
  5.1 1.2 %collective-permute-start.1 = (bf16[16,768]{1,0:T(8,128)(2,1)S(1)}, bf16[16,768]{1,0:T(8,128)(2,1)S(1)}, u32[]{:S(2)}, u32[]{:S(2)}) collective-permute-start(bf16[16,768]{1,0:T(8,128)(2,1)S(1)} %get-tuple-element.27), channel_id=1, source_target_pairs={{1,2},{2,1},{3,4},{4,3},{5,6},{6,5},{7,8},{8,7},{9,10},{10,9},{11,... | collective-permute-start | bytes 73736 | tf_op jit(solution)/shard_map/ppermute | solution.py:469
  6.3 7.0 %collective-permute-start.2 = (bf16[16,768]{1,0:T(8,128)(2,1)S(1)}, bf16[16,768]{1,0:T(8,128)(2,1)S(1)}, u32[]{:S(2)}, u32[]{:S(2)}) collective-permute-start(bf16[16,768]{1,0:T(8,128)(2,1)S(1)} %add_add_fusion), channel_id=1, source_target_pairs={{0,16},{1,17},{2,18},{3,19},{4,20},{5,21},{6,22},{7,23},{8,24},{9,... | collective-permute-start | bytes 73736 | tf_op jit(solution)/shard_map/ppermute | solution.py:411
  8.1 11.0 %copy-start = (bf16[5,384,384]{2,1,0:T(8,128)(2,1)S(1)}, bf16[5,384,384]{2,1,0:T(8,128)(2,1)}, u32[]{:S(2)}) copy-start(bf16[5,384,384]{2,1,0:T(8,128)(2,1)} %conv.5) | copy-start | bytes 4423684
  14.9 1.8 %collective-permute-start.4 = (bf16[480,384]{1,0:T(8,128)(2,1)S(1)}, bf16[480,384]{1,0:T(8,128)(2,1)S(1)}, u32[]{:S(2)}, u32[]{:S(2)}) collective-permute-start(bf16[480,384]{1,0:T(8,128)(2,1)S(1)} %get-tuple-element.30), channel_id=1, source_target_pairs={{0,1},{1,0},{2,3},{3,2},{4,5},{5,4},{6,7},{7,6},{8,9},{9,8},{10,11... | collective-permute-start | bytes 1105928 | tf_op jit(solution)/shard_map/ppermute | solution.py:411
  16.8 8.8 %collective-permute-start.5 = (bf16[240,384]{1,0:T(8,128)(2,1)S(1)}, bf16[240,384]{1,0:T(8,128)(2,1)S(1)}, u32[]{:S(2)}, u32[]{:S(2)}) collective-permute-start(bf16[240,384]{1,0:T(8,128)(2,1)S(1)} %get-tuple-element.32), channel_id=1, source_target_pairs={{0,2},{1,3},{2,0},{3,1},{4,6},{5,7},{6,4},{7,5},{8,10},{9,11},{10,... | collective-permute-start | bytes 552968 | tf_op jit(solution)/shard_map/ppermute | solution.py:411
  25.6 1.8 %collective-permute-start.8 = (bf16[32,384]{1,0:T(8,128)(2,1)S(1)}, bf16[32,384]{1,0:T(8,128)(2,1)S(1)}, u32[]{:S(2)}, u32[]{:S(2)}) collective-permute-start(bf16[32,384]{1,0:T(8,128)(2,1)S(1)} %dynamic-slice_convert_fusion), channel_id=1, source_target_pairs={{0,1},{1,0},{2,3},{3,2},{4,5},{5,4},{6,7},{7,6},{8,9},{9,8},{10,11... | collective-permute-start | bytes 73736 | tf_op jit(solution)/shard_map/ppermute | solution.py:411
  25.7 6.0 %collective-permute-start.6 = (bf16[144,384]{1,0:T(8,128)(2,1)S(1)}, bf16[144,384]{1,0:T(8,128)(2,1)S(1)}, u32[]{:S(2)}, u32[]{:S(2)}) collective-permute-start(bf16[144,384]{1,0:T(8,128)(2,1)S(1)} %fusion), channel_id=1, source_target_pairs={{0,4},{1,9},{2,6},{3,11},{4,0},{5,13},{6,2},{7,15},{8,12},{9,1},{1... | collective-permute-start | bytes 331784 | tf_op jit(solution)/shard_map/ppermute | solution.py:411
  27.4 6.4 %collective-permute-start.9 = (bf16[128,384]{1,0:T(8,128)(2,1)S(1)}, bf16[128,384]{1,0:T(8,128)(2,1)S(1)}, u32[]{:S(2)}, u32[]{:S(2)}) collective-permute-start(bf16[128,384]{1,0:T(8,128)(2,1)S(1)} %fusion.1), channel_id=1, source_target_pairs={{0,4},{1,9},{2,6},{3,11},{4,0},{5,13},{6,2},{7,15},{8,12},{9,1},{1... | collective-permute-start | bytes 294920 | tf_op jit(solution)/shard_map/ppermute | solution.py:411
  31.7 6.3 %collective-permute-start.7 = (bf16[144,384]{1,0:T(8,128)(2,1)S(1)}, bf16[144,384]{1,0:T(8,128)(2,1)S(1)}, u32[]{:S(2)}, u32[]{:S(2)}) collective-permute-start(bf16[144,384]{1,0:T(8,128)(2,1)S(1)} %fusion.2), channel_id=1, source_target_pairs={{0,8},{1,5},{2,10},{3,7},{4,12},{5,1},{6,14},{7,3},{8,0},{9,13},{1... | collective-permute-start | bytes 331784 | tf_op jit(solution)/shard_map/ppermute | solution.py:411
  33.9 6.2 %collective-permute-start.13 = (bf16[128,384]{1,0:T(8,128)(2,1)S(1)}, bf16[128,384]{1,0:T(8,128)(2,1)S(1)}, u32[]{:S(2)}, u32[]{:S(2)}) collective-permute-start(bf16[128,384]{1,0:T(8,128)(2,1)S(1)} %get-tuple-element.48), channel_id=1, source_target_pairs={{0,8},{1,5},{2,10},{3,7},{4,12},{5,1},{6,14},{7,3},{8,0},{9,13},{1... | collective-permute-start | bytes 294920 | tf_op jit(solution)/shard_map/ppermute | solution.py:411
  38.1 5.6 %collective-permute-start.10 = (bf16[144,384]{1,0:T(8,128)(2,1)S(1)}, bf16[144,384]{1,0:T(8,128)(2,1)S(1)}, u32[]{:S(2)}, u32[]{:S(2)}) collective-permute-start(bf16[144,384]{1,0:T(8,128)(2,1)S(1)} %convert_add_fusion.1), channel_id=1, source_target_pairs={{0,2},{1,17},{2,0},{3,19},{4,6},{5,21},{6,4},{7,23},{8,10},{9,25},... | collective-permute-start | bytes 331784 | tf_op jit(solution)/shard_map/ppermute | solution.py:411
  40.2 4.8 %collective-permute-start.14 = (bf16[128,384]{1,0:T(8,128)(2,1)S(1)}, bf16[128,384]{1,0:T(8,128)(2,1)S(1)}, u32[]{:S(2)}, u32[]{:S(2)}) collective-permute-start(bf16[128,384]{1,0:T(8,128)(2,1)S(1)} %pad_maximum_fusion.5), channel_id=1, source_target_pairs={{0,16},{1,3},{2,18},{3,1},{4,20},{5,7},{6,22},{7,5},{8,24},{9,11},... | collective-permute-start | bytes 294920 | tf_op jit(solution)/shard_map/ppermute | solution.py:411
  43.7 6.6 %collective-permute-start.11 = (bf16[288,384]{1,0:T(8,128)(2,1)S(1)}, bf16[288,384]{1,0:T(8,128)(2,1)S(1)}, u32[]{:S(2)}, u32[]{:S(2)}) collective-permute-start(bf16[288,384]{1,0:T(8,128)(2,1)S(1)} %pad_maximum_fusion.3), channel_id=1, source_target_pairs={{0,16},{1,3},{2,18},{3,1},{4,20},{5,7},{6,22},{7,5},{8,24},{9,11},... | collective-permute-start | bytes 663560 | tf_op jit(solution)/shard_map/ppermute | solution.py:411
  45.0 5.5 %collective-permute-start.15 = (bf16[224,384]{1,0:T(8,128)(2,1)S(1)}, bf16[224,384]{1,0:T(8,128)(2,1)S(1)}, u32[]{:S(2)}, u32[]{:S(2)}) collective-permute-start(bf16[224,384]{1,0:T(8,128)(2,1)S(1)} %pad_maximum_fusion.4), channel_id=1, source_target_pairs={{0,2},{1,17},{2,0},{3,19},{4,6},{5,21},{6,4},{7,23},{8,10},{9,25},... | collective-permute-start | bytes 516104 | tf_op jit(solution)/shard_map/ppermute | solution.py:411
  50.4 2.3 %collective-permute-start.12 = (bf16[576,384]{1,0:T(8,128)(2,1)S(1)}, bf16[576,384]{1,0:T(8,128)(2,1)S(1)}, u32[]{:S(2)}, u32[]{:S(2)}) collective-permute-start(bf16[576,384]{1,0:T(8,128)(2,1)S(1)} %pad_maximum_fusion.left), channel_id=1, source_target_pairs={{0,1},{1,0},{2,3},{3,2},{4,5},{5,4},{6,7},{7,6},{8,9},{9,8},{10,11... | collective-permute-start | bytes 1327112 | tf_op jit(solution)/shard_map/ppermute | solution.py:411
  50.6 2.1 %collective-permute-start.16 = (bf16[416,384]{1,0:T(8,128)(2,1)S(1)}, bf16[416,384]{1,0:T(8,128)(2,1)S(1)}, u32[]{:S(2)}, u32[]{:S(2)}) collective-permute-start(bf16[416,384]{1,0:T(8,128)(2,1)S(1)} %pad_maximum_fusion.1), channel_id=1, source_target_pairs={{0,1},{1,0},{2,3},{3,2},{4,5},{5,4},{6,7},{7,6},{8,9},{9,8},{10,11... | collective-permute-start | bytes 958472 | tf_op jit(solution)/shard_map/ppermute | solution.py:411

commit v4 on v3

--- a/solution.py
+++ b/solution.py
@@ -52,6 +52,14 @@
     return together(value, *others)[0]
 
 
+def holding(kernel, operands, results, kept):
+    def run(*refs):
+        last = operands + kept + results
+        kernel(*refs[:operands], *refs[operands + kept : last], *refs[last + kept :])
+
+    return run
+
+
 def first_kernel(
     rows,
     lanes,
@@ -60,16 +68,17 @@
     amounts,
     cot,
     stem_weight,
+    conv,
     own,
     near,
     far,
     weight,
     half_weight,
+    cot_out,
+    conv_out,
     base_v,
     pos_s,
     amt_s,
-    top,
-    bottom,
     weight_v,
     sems,
 ):
@@ -80,15 +89,15 @@
         pltpu.make_async_copy(codes, base_v, sems.at[0]),
         pltpu.make_async_copy(positions, pos_s, sems.at[1]),
         pltpu.make_async_copy(amounts, amt_s, sems.at[2]),
-        pltpu.make_async_copy(cot.at[pl.ds(0, 16)], top, sems.at[3]),
-        pltpu.make_async_copy(cot.at[pl.ds(rows - 16, 16)], bottom, sems.at[4]),
-        pltpu.make_async_copy(stem_weight, weight_v, sems.at[5]),
+        pltpu.make_async_copy(cot, cot_out, sems.at[3]),
+        pltpu.make_async_copy(stem_weight, weight_v, sems.at[4]),
+        pltpu.make_async_copy(conv, conv_out, sems.at[5]),
     ]
     for copy in copies:
         copy.start()
     ctx = lax.axis_index("context")
     core = lax.rem(ctx, 2)
-    for copy in copies[:5]:
+    for copy in copies[:4]:
         copy.wait()
     x = jnp.concatenate([base_v[:, 128 * q : 128 * q + 128] for q in range(tiles)], axis=0)
     spot = (
@@ -125,13 +134,14 @@
         grads = jnp.concatenate([grads, pad], axis=1)
         return jnp.concatenate([edge, grads, jnp.zeros((6, lanes), f32)], axis=0)
 
-    head = message(first, top[...].astype(f32)[0:2])
-    tail = message(last, bottom[...].astype(f32)[14:16])
+    head = message(first, cot_out[0:16, :].astype(f32)[0:2])
+    tail = message(last, cot_out[rows - 16 : rows, :].astype(f32)[14:16])
     own[...] = jnp.concatenate([shifted, blank], axis=0).astype(bf16)
     near[...] = jnp.where(core == 0, tail, head).astype(bf16)
     far[...] = jnp.where(core == 0, head, tail).astype(bf16)
+    copies[4].wait()
+    stem_terms(weight_v, weight, half_weight)
     copies[5].wait()
-    stem_terms(weight_v, weight, half_weight)
 
 
 def stem_terms(weight, out, half_out):
@@ -202,14 +212,12 @@
             gated[at : at + step, :] = moved[:, :rows].astype(bf16)
 
 
-def own_kernel(rows, total, own, near, far, weight, cot, out, stem, gated, cot_v, sem):
-    copy = pltpu.make_async_copy(cot, cot_v, sem)
-    copy.start()
+def own_kernel(rows, total, own, near, far, weight, conv, cot, out, edges, stem, gated):
     first = lax.axis_index("context") * rows
     codes = (own[...].astype(f32) + near[...].astype(f32) + far[...].astype(f32))[0:8]
     shifted_gates(codes, first, total, weight, rows, stem, gated)
-    copy.wait()
-    out[...] = jnp.dot(gated[...], cot_v[...], preferred_element_type=f32)
+    edges[...] = edge_terms(near, far, conv)
+    out[...] = jnp.dot(gated[...], cot[...], preferred_element_type=f32)
 
 
 def pair_kernel(rows, total, codes, weight, gated, stem):
@@ -226,22 +234,30 @@
         out[...] = value.astype(out.dtype)
 
 
+def place_of():
+    ctx = lax.axis_index("context")
+    return ctx, lax.rem(ctx, 2), lax.rem(lax.axis_index("dp"), 2)
+
+
+def quarter_bit(ctx, core):
+    far = 4 if lax.axis_size("context") % 8 == 0 else 2
+    return jnp.where(core == 0, lax.rem(ctx // 2, 2), lax.rem(ctx // far, 2))
+
+
 def split_kernel(value, got, sent, kept):
-    x = lax.rem(lax.axis_index("context") // 2, 2)
+    x = quarter_bit(*place_of()[:2])
     size = sent.shape[0]
     for which, out in ((1 - x, sent), (x, kept)):
         span = pl.ds(pl.multiple_of(which * size, 16), size)
         out[...] = (value[span, :] + got[span, :].astype(f32)).astype(out.dtype)
 
 
-def back_kernel(rows, conv, cot, back, ext, sem):
+def back_kernel(rows, conv, cot, back, ext):
     width = cot.shape[1]
-    copy = pltpu.make_async_copy(cot, ext.at[pl.ds(LEAD, rows)], sem)
-    copy.start()
     blank = jnp.zeros((LEAD, width), bf16)
     ext[0:LEAD, :] = blank
+    ext[LEAD : LEAD + rows, :] = cot[...]
     ext[LEAD + rows :, :] = blank
-    copy.wait()
     for t in range(TAPS):
         start = LEAD + 2 - t
         term = turned(ext[start : start + rows, :], conv[t])
@@ -266,14 +282,12 @@
     end_late = jnp.concatenate([none, one, behind[0:1]], axis=0).astype(bf16)
     first = turned(top, conv[4]) + turned(top_late, conv[3])
     last = turned(end, conv[0]) + turned(end_late, conv[1])
-    return first, last
+    return jnp.concatenate([first, last], axis=0)
 
 
 def slope_kernel(
-    rows, total, own, near, far, weight, back, conv, cot, d_pooled, stem_part, gated, pooled, stem, cot_v, sem
+    rows, total, own, near, far, weight, back, edges, cot, d_pooled, stem_part, gated, pooled, stem
 ):
-    copy = pltpu.make_async_copy(cot, cot_v, sem)
-    copy.start()
     lanes = own.shape[1]
     width = cot.shape[1]
     padded = rows + 2 * LEAD
@@ -293,9 +307,8 @@
         spot = first - LEAD + edge + lax.broadcasted_iota(jnp.int32, (LEAD, 1), 0)
         inside = (spot >= 0) & (spot < total)
         gated[edge : edge + LEAD, :] = jnp.where(inside, gelu_tanh(act), 0.0).astype(bf16)
-    top, end = edge_terms(near, far, conv)
+    top, end = edges[0:8, :], edges[8:16, :]
     none = jnp.zeros((24, width), f32)
-    copy.wait()
     step = 32
     for r in range(0, rows, step):
         even = stem[LEAD + r : LEAD + r + step, :width]
@@ -311,7 +324,7 @@
             rise = rise + jnp.concatenate([top, none], axis=0)
         if r + step == rows:
             rise = rise + jnp.concatenate([none, end], axis=0)
-        grad = cot_v[r : r + step, :].astype(f32) + rise * slope
+        grad = cot[r : r + step, :].astype(f32) + rise * slope
         d_pooled[r : r + step, :] = grad.astype(bf16)
         half = 0.5 * grad
         stem[LEAD + r : LEAD + r + step, :width] = half * even_slope
@@ -337,26 +350,24 @@
     out[...] = acc.astype(bf16)
 
 
-def put_pieces(flip, chains, out, room, sems):
-    ctx = lax.axis_index("context")
-    core = lax.rem(ctx, 2)
-    x = lax.rem(ctx // 2, 2)
-    y = lax.rem(lax.axis_index("dp"), 2)
+def put_pieces(pieces, out, room, sems):
+    ctx, core, y = place_of()
     unit = room.shape[1]
     half = out.shape[1] // 2
-    from_core = lax.rem(core + flip, 2)
     copies = []
     at = 0
-    for chain, (piece, tap, taps) in enumerate(chains):
-        x_first = jnp.where(from_core == chain, 1, 0)
-        for p in range(4):
+    for piece, chain, flip, ids in pieces:
+        tap, taps = ((0, FIRST), (FIRST, TAPS - FIRST))[chain]
+        from_core = lax.rem(core + flip, 2)
+        q = quarter_bit(ctx, from_core)
+        for k, p in enumerate(ids):
             one, two = p % 2, p // 2
-            dx = jnp.where(x_first == 1, one, two)
-            dy = one + two - dx
-            from_x, from_y = lax.rem(x + dx, 2), lax.rem(y + dy, 2)
-            channel = from_y * half + (2 * from_core + from_x) * unit
+            dq = jnp.where(from_core == chain, one, two)
+            dy = one + two - dq
+            from_q, from_y = lax.rem(q + dq, 2), lax.rem(y + dy, 2)
+            channel = from_y * half + (2 * from_core + from_q) * unit
             for t in range(taps):
-                low = (p * taps + t) * unit
+                low = (k * taps + t) * unit
                 room[at + t] = piece[low : low + unit, :].astype(f32)
             copy = pltpu.make_async_copy(
                 room.at[pl.ds(at, taps)],
@@ -369,24 +380,25 @@
     return copies
 
 
-def place_kernel(left, right, out, room, sems):
-    for copy in put_pieces(0, ((left, 0, FIRST), (right, FIRST, TAPS - FIRST)), out, room, sems):
+def early_kernel(left, right, got_left, got_right, out, room, sems):
+    pieces = [(left, 0, 0), (right, 1, 0), (got_left, 0, 1), (got_right, 1, 1)]
+    for copy in put_pieces([(*piece, (0, 1)) for piece in pieces], out, room, sems):
+        copy.wait()
+
+
+def late_kernel(left, right, whole, out, room, sems):
+    del whole
+    for copy in put_pieces([(left, 0, 0, (2, 3)), (right, 1, 0, (2, 3))], out, room, sems):
         copy.wait()
 
 
 def last_kernel(left, right, stem, whole, out, stem_out, room, sems):
     del whole
-    copies = put_pieces(
-        1, ((left, 0, FIRST), (right, FIRST, TAPS - FIRST)), out, room, sems
-    )
-    core = lax.rem(lax.axis_index("context"), 2)
+    copies = put_pieces([(left, 0, 1, (2, 3)), (right, 1, 1, (2, 3))], out, room, sems)
     mine = stem[...].astype(bf16).astype(f32)
-    other = right[right.shape[0] - stem.shape[0] :, :].astype(f32)
-    whole_stem = jnp.concatenate(
-        [jnp.where(core == 0, mine, other), jnp.where(core == 0, other, mine)], axis=0
-    )
+    total = mine + right[right.shape[0] - stem.shape[0] :, :].astype(f32)
     for k in range(stem_out.shape[0]):
-        stem_out[k] = whole_stem[4 * k : 4 * k + 4, :]
+        stem_out[k] = total[4 * k : 4 * k + 4, :]
     for copy in copies:
         copy.wait()
 
@@ -404,13 +416,21 @@
     core = lax.axis_index("context") % 2
     cot = cotangent[0]
     x_bit, y_bit = 2, n_ctx
+    z_bit = 4 if n_ctx % 8 == 0 else 2
 
     def swap(value, even_bit, odd_bit=None):
         odd_bit = even_bit if odd_bit is None else odd_bit
         pairs = [(i, i ^ (odd_bit if i & 1 else even_bit)) for i in range(devices)]
         return lax.ppermute(value, AXES, pairs)
 
-    def call(kernel, out, operands, scratch=(), **options):
+    def call(kernel, out, operands, scratch=(), keep=(), **options):
+        if keep:
+            options["input_output_aliases"] = {
+                len(operands) + k: len(out) + k for k in range(len(keep))
+            }
+            kernel = holding(kernel, len(operands), len(out), len(keep))
+            operands = list(operands) + near_by(*keep)
+            out = list(out) + [(value.shape, value.dtype) for value in keep]
         shapes = [jax.ShapeDtypeStruct(o[0], o[1]) for o in out]
         specs = [o[2] if len(o) > 2 else VMEM for o in out]
         options.setdefault("compiler_params", params())
@@ -439,16 +459,22 @@
     pair_cot = swap(cot, y_bit)
     dma = pltpu.SemaphoreType.DMA
     edge = ((16, lanes), bf16)
-    own, near, far, weight, half_weight = call(
+    own, near, far, weight, half_weight, cot_v, conv_v = call(
         functools.partial(first_kernel, rows, lanes),
-        [edge, edge, edge, ((192, 2 * width), bf16), ((192, width), bf16)],
-        far_off(codes, variant_pos, variant_shift, cot, stem_weight),
+        [
+            edge,
+            edge,
+            edge,
+            ((192, 2 * width), bf16),
+            ((192, width), bf16),
+            (cot.shape, bf16),
+            (conv_weight.shape, bf16),
+        ],
+        far_off(codes, variant_pos, variant_shift, cot, stem_weight, conv_weight),
         [
             pltpu.VMEM((1, length), jnp.int32),
             pltpu.SMEM(variant_pos.shape, jnp.int32),
             pltpu.SMEM(variant_pos.shape, jnp.int32),
-            pltpu.VMEM((16, width), bf16),
-            pltpu.VMEM((16, width), bf16),
             pltpu.VMEM(stem_weight.shape, f32),
             dma((6,)),
         ],
@@ -462,36 +488,44 @@
     (back,) = call(
         functools.partial(back_kernel, rows),
         [((rows, width), f32)],
-        near_by(conv_weight) + far_off(after(cot, far)),
-        [pltpu.VMEM((padded, width), bf16), dma],
+        near_by(conv_v, cot_v),
+        [pltpu.VMEM((padded, width), bf16)],
         cost_estimate=cost,
     )
     far = lax.ppermute(far, AXES, list(outward.items()))
-    pair_codes = swap(own + near + far, y_bit)
+    pair_codes = swap(after(own + near + far, back), y_bit)
     stem_half = pltpu.VMEM((width, rows + 128), f32)
     gates = ((TAPS * half, rows), bf16)
-    (part,) = call(
+    part, edges, back = call(
         functools.partial(own_kernel, rows, total),
-        [((TAPS * half, width), f32)],
-        near_by(own, near, far, half_weight) + far_off(cot),
-        [stem_half, pltpu.VMEM(*gates), pltpu.VMEM((rows, width), bf16), dma],
-    )
-    (pair_gates,) = call(
+        [((TAPS * half, width), f32), ((16, width), f32)],
+        near_by(own, near, far, half_weight, conv_v, cot_v),
+        [stem_half, pltpu.VMEM(*gates)],
+        keep=[back],
+    )
+    pair_gates, back = call(
         functools.partial(pair_kernel, rows, total),
         [gates],
         near_by(pair_codes, half_weight),
         [stem_half],
+        keep=[back],
     )
     size = TAPS * half // 2
-    sent, kept = call(
-        sum_kernel, [((size, width), bf16), ((size, width), f32)], near_by(part, pair_gates, pair_cot)
+    sent, kept, back = call(
+        sum_kernel,
+        [((size, width), bf16), ((size, width), f32)],
+        near_by(part, pair_gates, pair_cot),
+        keep=[back],
     )
     got = swap(sent, 1)
     size //= 2
-    sent, kept = call(
-        split_kernel, [((size, width), bf16), ((size, width), f32)], near_by(kept, got)
-    )
-    got = swap(sent, x_bit)
+    sent, kept, back = call(
+        split_kernel,
+        [((size, width), bf16), ((size, width), f32)],
+        near_by(kept, got),
+        keep=[back],
+    )
+    got = swap(sent, x_bit, z_bit)
     d_pooled, stem_part, gated, pooled = call(
         functools.partial(slope_kernel, rows, total),
         [
@@ -500,32 +534,29 @@
             ((padded, width), bf16),
             ((rows, width), bf16),
         ],
-        near_by(after(own, sent), near, far, weight, back, conv_weight) + far_off(cot),
-        [pltpu.VMEM((padded, 2 * width), f32), pltpu.VMEM((rows, width), bf16), dma],
+        near_by(after(own, sent), near, far, weight, back, edges, cot_v),
+        [pltpu.VMEM((padded, 2 * width), f32)],
         cost_estimate=cost,
     )
     value = kept + got.astype(f32)
-
-    few = stem_part.shape[0] // 2
-    stem_part = after(stem_part, value)
-    stem_got = swap(lax.dynamic_slice_in_dim(stem_part, (1 - core) * few, few, 0).astype(bf16), 1)
-    stem_sum = lax.dynamic_slice_in_dim(stem_part, core * few, few, 0) + stem_got.astype(f32)
 
     cut = FIRST * unit
     rest = size - cut
     left = value[:cut]
-    right = jnp.concatenate([value[cut:], stem_sum], axis=0)
-    others = [1 << k for k in range(devices.bit_length() - 1) if (1 << k) not in (1, x_bit, y_bit)]
-    for k, b in enumerate(others):
-        odd_b = others[(k + 1) % len(others)]
+    right = jnp.concatenate([value[cut:], stem_part], axis=0)
+    bits = [1 << k for k in range(devices.bit_length() - 1)]
+    even_rest = [b for b in bits if b not in (1, x_bit, y_bit)]
+    odd_rest = [b for b in bits if b not in (1, z_bit, y_bit)]
+    odd_rest = odd_rest[1:] + odd_rest[:1]
+    for k, (b, odd_b) in enumerate(zip(even_rest, odd_rest)):
         left, right = rounded(left), rounded(right)
-        if k == len(others) - 1:
+        if k == len(even_rest) - 1:
             pooled = after(pooled, right)
         left, right = [v + swap(v.astype(bf16), b, odd_b).astype(f32) for v in (left, right)]
     (features,) = call(
         functools.partial(feature_kernel, rows),
         [((rows, width), bf16)],
-        near_by(gated, pooled, conv_weight),
+        near_by(gated, pooled, conv_v),
         cost_estimate=cost,
     )
     left, features = together(left, features)
@@ -535,26 +566,40 @@
 
     whole = ((TAPS, width, width), f32, FAR)
 
-    for one, two in ((x_bit, y_bit), (y_bit, x_bit)):
-        got_left = swap(left, one, two)
-        stem_sum = rounded(stem_sum)
-        got_right = swap(jnp.concatenate([right, stem_sum.astype(bf16)], axis=0), two, one)
-        stem_sum = stem_sum + got_right[right.shape[0] :].astype(f32)
-        left = jnp.concatenate([left, got_left], axis=0)
-        right = jnp.concatenate([right, got_right[: right.shape[0]]], axis=0)
-    got_left = swap(left, 1)
-    got_right = swap(jnp.concatenate([right, stem_sum.astype(bf16)], axis=0), 1)
+    def joined(pieces):
+        return jnp.concatenate([pieces, stem_sum.astype(bf16)], axis=0)
+
+    stem_sum = rounded(stem_sum)
+    got_left, got_right = swap(left, x_bit, y_bit), swap(joined(right), y_bit, z_bit)
+    left = jnp.concatenate([left, got_left], axis=0)
+    stem_sum = stem_sum + got_right[rest:].astype(f32)
+    right = jnp.concatenate([right, got_right[:rest]], axis=0)
+
+    stem_sum = rounded(stem_sum)
+    got_left, got_right = swap(left, y_bit, z_bit), swap(joined(right), x_bit, y_bit)
     (conv_grad,) = call(
-        place_kernel,
+        early_kernel,
         [whole],
-        near_by(left, right),
+        near_by(left, right, swap(left, 1), swap(right, 1)),
         [pltpu.VMEM((TAPS * 4, unit, width), f32), dma((8,))],
+    )
+    stem_sum = stem_sum + got_right[2 * rest :].astype(f32)
+    left, right = got_left, got_right[: 2 * rest]
+    left, conv_grad = together(left, conv_grad)
+    got_left, got_right = swap(left, 1), swap(joined(right), 1)
+    room = [pltpu.VMEM((TAPS * 2, unit, width), f32), dma((4,))]
+    (conv_grad,) = call(
+        late_kernel,
+        [whole],
+        near_by(left, right) + far_off(conv_grad),
+        room,
+        input_output_aliases={2: 0},
     )
     conv_grad, stem_grad = call(
         last_kernel,
         [whole, (stem_weight.shape, f32)],
         near_by(got_left, got_right, stem_sum) + far_off(conv_grad),
-        [pltpu.VMEM((TAPS * 4, unit, width), f32), dma((8,))],
+        room,
         input_output_aliases={3: 0},
     )
     return (features[None], d_pooled[None], conv_grad, stem_grad)

time: 54.8 us -> 53.3 us (0.973)
  Pallas kernels: 16.3 us -> 14.8 us
    pallas_call x10 -> x11, Pallas kernels: 16.3 us -> 14.8 us  [call(): pl.pallas_call(kernel, out_shape=shapes, in_specs=[spec for _, spec in op...]
    ppermute x16 -> x17, starting transfers between devices: 18.7 us -> 18.3 us  [swap(): return lax.ppermute(value, AXES, pairs)]
    ppermute x16 -> x17, waiting for transfers between devices: 17.5 us -> 17.5 us  [swap(): return lax.ppermute(value, AXES, pairs)]
  transfers between devices with their start and end apart: 17 -> 18, of which waited for: 9 -> 11; matrix products, arithmetic and copies ran while one was open for 1% -> 1% of each run, Pallas kernels for 25% -> 24%
where the time goes in v4:
time: 53.3 us; the launch traced here: 52.6 us
  starting transfers between devices  19 us (36%)
  waiting for transfers between devices  17.5 us (33%)
  Pallas kernels  14.8 us (28%)
  between operations  0.85 us (2%)
    ppermute x17, starting transfers between devices, swap(): return lax.ppermute(value, AXES, pairs)  18.3 us
    ppermute x17, waiting for transfers between devices, swap(): return lax.ppermute(value, AXES, pairs)  17.5 us
    pallas_call x11, Pallas kernels, call(): pl.pallas_call(kernel, out_shape=shapes, in_specs=[spec for _, spec in op...  14.8 us
  transfers between devices with their start and end apart: 18, of which 11 were waited for; matrix products, arithmetic and copies ran while one was open for 1% of the time, Pallas kernels for 24%

profile of v4, /device:TPU:0, one launch (start us, length us, event | category | flops | bytes accessed | tf_op | source)
XLA Modules:
  0.0 52.6 jit_solution(3685039452643700208)
XLA Ops:
  0.6 3.0 %collective-permute-start.3 = (bf16[512,384]{1,0:T(8,128)(2,1)}, bf16[512,384]{1,0:T(8,128)(2,1)S(1)}, u32[]{:S(2)}, u32[]{:S(2)}) collective-permute-start(bf16[512,384]{1,0:T(8,128)(2,1)} %bitcast.3), channel_id=1, source_target_pairs={{0,16},{1,17},{2,18},{3,19},{4,20},{5,21},{6,22},{7,23},{8,24},{9,... | collective-permute-start | bytes 1179656 | tf_op jit(solution)/shard_map/ppermute | solution.py:424
  3.7 1.6 %shard_map.93 = (bf16[16,768]{1,0:T(8,128)(2,1)S(1)}, bf16[16,768]{1,0:T(8,128)(2,1)S(1)}, bf16[16,768]{1,0:T(8,128)(2,1)S(1)}, bf16[192,768]{1,0:T(8,128)(2,1)S...) custom-call(s32[1,1024]{1,0:T(1,128)} %codes.1, ...), custom_call_target="tpu_custom_call" | custom-call | tf_op jit(solution)/shard_map/pallas_call | solution.py:437
  6.0 1.4 %shard_map.94.refs_6_ = f32[512,384]{1,0:T(8,128)S(1)} custom-call(bf16[5,384,384]{2,1,0:T(8,128)(2,1)S(1)} %get-tuple-element.39.conv.refs_4_, bf16[512,384]{1,0:T(8,128)(2,1)S(1)} %get-tuple-element.40.cot.refs_5_), custom_call_target="tpu_custom_call" | custom-call | flops 754974720 | bytes 4194304 | tf_op jit(solution)/shard_map/pallas_call | solution.py:437
  7.6 1.4 %shard_map.95 = (f32[960,384]{1,0:T(8,128)S(1)}, f32[16,384]{1,0:T(8,128)S(1)}, f32[512,384]{1,0:T(8,128)S(1)}) custom-call(bf16[16,768]{1,0:T(8,128)(2,1)S(1)} %get-tuple-element.51.refs_0_.own, bf16[16,768]{1,0:T(8,128)(2,1)S(1)} %collective-permute-done.refs_1_.near, ...), custom_call_target="tpu_custom_call", output_to_operand_aliasing={{2}: (6, {})} | custom-call | tf_op jit(solution)/shard_map/pallas_call | solution.py:437
  9.0 4.3 %collective-permute-done.2.refs_0_ = bf16[16,768]{1,0:T(8,128)(2,1)S(1)} collective-permute-done((bf16[16,768]{1,0:T(8,128)(2,1)S(1)}, bf16[16,768]{1,0:T(8,128)(2,1)S(1)}, u32[]{:S(2)}, u32[]{:S(2)}) %collective-permute-start.2) | collective-permute-done | bytes 24608 | tf_op jit(solution)/shard_map/ppermute | solution.py:424
  13.3 0.9 %shard_map.96 = (bf16[960,512]{1,0:T(8,128)(2,1)S(1)}, f32[512,384]{1,0:T(8,128)S(1)}) custom-call(bf16[16,768]{1,0:T(8,128)(2,1)S(1)} %collective-permute-done.2.refs_0_, bf16[192,384]{1,0:T(8,128)(2,1)S(1)} %get-tuple-element.38.refs_3_.refs_1_, f32[512,384]{1,0:T(8,128)S(1)} %get-tuple-element.43.refs_2_), custom_call_target="tpu_custom_call", output_to_operand_aliasing={{1}: (2, {})} | custom-call | tf_op jit(solution)/shard_map/pallas_call | solution.py:437
  14.9 0.8 %collective-permute-start.4 = (bf16[480,384]{1,0:T(8,128)(2,1)S(1)}, bf16[480,384]{1,0:T(8,128)(2,1)S(1)}, u32[]{:S(2)}, u32[]{:S(2)}) collective-permute-start(bf16[480,384]{1,0:T(8,128)(2,1)S(1)} %get-tuple-element.47), channel_id=1, source_target_pairs={{0,1},{1,0},{2,3},{3,2},{4,5},{5,4},{6,7},{7,6},{8,9},{9,8},{10,11... | collective-permute-start | bytes 1105928 | tf_op jit(solution)/shard_map/ppermute | solution.py:424
  15.6 1.3 %collective-permute-done.4.refs_1_ = bf16[480,384]{1,0:T(8,128)(2,1)S(1)} collective-permute-done((bf16[480,384]{1,0:T(8,128)(2,1)S(1)}, bf16[480,384]{1,0:T(8,128)(2,1)S(1)}, u32[]{:S(2)}, u32[]{:S(2)}) %collective-permute-start.4) | collective-permute-done | bytes 368672 | tf_op jit(solution)/shard_map/ppermute | solution.py:424
  17.0 2.3 %collective-permute-start.5 = (bf16[240,384]{1,0:T(8,128)(2,1)S(1)}, bf16[240,384]{1,0:T(8,128)(2,1)S(1)}, u32[]{:S(2)}, u32[]{:S(2)}) collective-permute-start(bf16[240,384]{1,0:T(8,128)(2,1)S(1)} %get-tuple-element.50), channel_id=1, source_target_pairs={{0,2},{1,5},{2,0},{3,7},{4,6},{5,1},{6,4},{7,3},{8,10},{9,13},{10,... | collective-permute-start | bytes 552968 | tf_op jit(solution)/shard_map/ppermute | solution.py:424
  19.3 2.9 %shard_map.99 = (bf16[512,384]{1,0:T(8,128)(2,1)}, f32[64,384]{1,0:T(8,128)S(1)}, bf16[544,384]{1,0:T(8,128)(2,1)S(1)}, bf16[512,384]{1,0:T(8,128)(2,1)S(1)}) custom-call(bf16[16,768]{1,0:T(8,128)(2,1)S(1)} %get-tuple-element.51.refs_0_.own, bf16[16,768]{1,0:T(8,128)(2,1)S(1)} %collective-permute-done.refs_1_.near, ...), custom_call_target="tpu_custom_call" | custom-call | flops 754974720 | bytes 4194304 | tf_op jit(solution)/shard_map/pallas_call | solution.py:437
  22.9 3.1 %collective-permute-start.6 = (bf16[144,384]{1,0:T(8,128)(2,1)S(1)}, bf16[144,384]{1,0:T(8,128)(2,1)S(1)}, u32[]{:S(2)}, u32[]{:S(2)}) collective-permute-start(bf16[144,384]{1,0:T(8,128)(2,1)S(1)} %fusion), channel_id=1, source_target_pairs={{0,4},{1,9},{2,6},{3,11},{4,0},{5,13},{6,2},{7,15},{8,12},{9,1},{1... | collective-permute-start | bytes 331784 | tf_op jit(solution)/shard_map/ppermute | solution.py:424
  26.1 3.4 %collective-permute-done.6 = bf16[144,384]{1,0:T(8,128)(2,1)S(1)} collective-permute-done((bf16[144,384]{1,0:T(8,128)(2,1)S(1)}, bf16[144,384]{1,0:T(8,128)(2,1)S(1)}, u32[]{:S(2)}, u32[]{:S(2)}) %collective-permute-start.6) | collective-permute-done | bytes 110624 | tf_op jit(solution)/shard_map/ppermute | solution.py:424
  29.6 3.0 %collective-permute-start.7 = (bf16[144,384]{1,0:T(8,128)(2,1)S(1)}, bf16[144,384]{1,0:T(8,128)(2,1)S(1)}, u32[]{:S(2)}, u32[]{:S(2)}) collective-permute-start(bf16[144,384]{1,0:T(8,128)(2,1)S(1)} %fusion.2), channel_id=1, source_target_pairs={{0,8},{1,3},{2,10},{3,1},{4,12},{5,7},{6,14},{7,5},{8,0},{9,11},{1... | collective-permute-start | bytes 331784 | tf_op jit(solution)/shard_map/ppermute | solution.py:424
  32.6 2.1 %collective-permute-start.11 = (bf16[160,384]{1,0:T(8,128)(2,1)S(1)}, bf16[160,384]{1,0:T(8,128)(2,1)S(1)}, u32[]{:S(2)}, u32[]{:S(2)}) collective-permute-start(bf16[160,384]{1,0:T(8,128)(2,1)S(1)} %get-tuple-element.68), channel_id=1, source_target_pairs={{0,8},{1,3},{2,10},{3,1},{4,12},{5,7},{6,14},{7,5},{8,0},{9,11},{1... | collective-permute-start | bytes 368648 | tf_op jit(solution)/shard_map/ppermute | solution.py:424
  34.7 2.2 %shard_map.100 = bf16[512,384]{1,0:T(8,128)(2,1)} custom-call(bf16[544,384]{1,0:T(8,128)(2,1)S(1)} %get-tuple-element.55.gated, bf16[512,384]{1,0:T(8,128)(2,1)S(1)} %get-tuple-element.58.pooled, bf16[5,384,384]{2,1,0:T(8,128)(2,1)S(1)} %get-tuple-element.39.conv.refs_4_), custom_call_target="tpu_custom_call" | custom-call | flops 754974720 | bytes 4194304 | tf_op jit(solution)/shard_map/pallas_call | solution.py:437
  37.6 0.9 %collective-permute-done.11 = bf16[160,384]{1,0:T(8,128)(2,1)S(1)} collective-permute-done((bf16[160,384]{1,0:T(8,128)(2,1)S(1)}, bf16[160,384]{1,0:T(8,128)(2,1)S(1)}, u32[]{:S(2)}, u32[]{:S(2)}) %collective-permute-start.11) | collective-permute-done | bytes 122912 | tf_op jit(solution)/shard_map/ppermute | solution.py:424
  39.1 2.6 %collective-permute-done.9 = bf16[144,384]{1,0:T(8,128)(2,1)S(1)} collective-permute-done((bf16[144,384]{1,0:T(8,128)(2,1)S(1)}, bf16[144,384]{1,0:T(8,128)(2,1)S(1)}, u32[]{:S(2)}, u32[]{:S(2)}) %collective-permute-start.9) | collective-permute-done | bytes 110624 | tf_op jit(solution)/shard_map/ppermute | solution.py:424
  42.4 1.1 %collective-permute-done.12 = bf16[160,384]{1,0:T(8,128)(2,1)S(1)} collective-permute-done((bf16[160,384]{1,0:T(8,128)(2,1)S(1)}, bf16[160,384]{1,0:T(8,128)(2,1)S(1)}, u32[]{:S(2)}, u32[]{:S(2)}) %collective-permute-start.12) | collective-permute-done | bytes 122912 | tf_op jit(solution)/shard_map/ppermute | solution.py:424
  45.0 1.0 %collective-permute-done.14.got_right = bf16[192,384]{1,0:T(8,128)(2,1)S(1)} collective-permute-done((bf16[192,384]{1,0:T(8,128)(2,1)S(1)}, bf16[192,384]{1,0:T(8,128)(2,1)S(1)}, u32[]{:S(2)}, u32[]{:S(2)}) %collective-permute-start.14) | collective-permute-done | bytes 147488 | tf_op jit(solution)/shard_map/ppermute | solution.py:424
  46.0 1.2 %shard_map.101.whole = f32[5,384,384]{2,1,0:T(8,128)} custom-call(bf16[288,384]{1,0:T(8,128)(2,1)S(1)} %pad_maximum_fusion.left, bf16[192,384]{1,0:T(8,128)(2,1)S(1)} %pad_maximum_fusion.3.right, bf16[288,384]{1,0:T(8,128)(2,1)S(1)} %collective-permute-done.13.got_left, bf16[192,384]{1,0:T(8,128)(2,1)S(1)} %collective-permute-done.14.got_right), custom_call_target="tpu_custom_call" | custom-call | tf_op jit(solution)/shard_map/pallas_call | solution.py:437
  47.2 1.1 %collective-permute-done.10.left = bf16[288,384]{1,0:T(8,128)(2,1)S(1)} collective-permute-done((bf16[288,384]{1,0:T(8,128)(2,1)S(1)}, bf16[288,384]{1,0:T(8,128)(2,1)S(1)}, u32[]{:S(2)}, u32[]{:S(2)}) %collective-permute-start.10) | collective-permute-done | bytes 221216 | tf_op jit(solution)/shard_map/ppermute | solution.py:424
  48.3 0.9 %collective-permute-done.16 = bf16[256,384]{1,0:T(8,128)(2,1)S(1)} collective-permute-done((bf16[256,384]{1,0:T(8,128)(2,1)S(1)}, bf16[256,384]{1,0:T(8,128)(2,1)S(1)}, u32[]{:S(2)}, u32[]{:S(2)}) %collective-permute-start.16) | collective-permute-done | bytes 196640 | tf_op jit(solution)/shard_map/ppermute | solution.py:424
  49.9 0.9 %shard_map.102.whole = f32[5,384,384]{2,1,0:T(8,128)} custom-call(bf16[288,384]{1,0:T(8,128)(2,1)S(1)} %collective-permute-done.10.left, bf16[192,384]{1,0:T(8,128)(2,1)S(1)} %slice.39.right, f32[5,384,384]{2,1,0:T(8,128)} %shard_map.101.whole), custom_call_target="tpu_custom_call", output_to_operand_aliasing={{}: (2, {})} | custom-call | tf_op jit(solution)/shard_map/pallas_call | solution.py:437
  51.0 1.6 %shard_map.103 = (f32[5,384,384]{2,1,0:T(8,128)}, f32[15,4,384]{2,1,0:T(4,128)}) custom-call(bf16[288,384]{1,0:T(8,128)(2,1)S(1)} %collective-permute-done.15.left, bf16[256,384]{1,0:T(8,128)(2,1)S(1)} %collective-permute-done.17.right, f32[64,384]{1,0:T(8,128)S(1)} %get-tuple-element.67.stem, ...), custom_call_target="tpu_custom_call", output_to_operand_aliasing={{0}: (3, {})} | custom-call | tf_op jit(solution)/shard_map/pallas_call | solution.py:437
  (43 shorter events, 6.7 us)
Async XLA Ops:
  0.6 13.5 %collective-permute-start.3 = (bf16[512,384]{1,0:T(8,128)(2,1)}, bf16[512,384]{1,0:T(8,128)(2,1)S(1)}, u32[]{:S(2)}, u32[]{:S(2)}) collective-permute-start(bf16[512,384]{1,0:T(8,128)(2,1)} %bitcast.3), channel_id=1, source_target_pairs={{0,16},{1,17},{2,18},{3,19},{4,20},{5,21},{6,22},{7,23},{8,24},{9,... | collective-permute-start | bytes 1179656 | tf_op jit(solution)/shard_map/ppermute | solution.py:424
  5.3 2.2 %collective-permute-start = (bf16[16,768]{1,0:T(8,128)(2,1)S(1)}, bf16[16,768]{1,0:T(8,128)(2,1)S(1)}, u32[]{:S(2)}, u32[]{:S(2)}) collective-permute-start(bf16[16,768]{1,0:T(8,128)(2,1)S(1)} %get-tuple-element.36), channel_id=1, source_target_pairs={{0,1},{1,0},{2,3},{3,2},{4,5},{5,4},{6,7},{7,6},{8,9},{9,8},{10,11... | collective-permute-start | bytes 73736 | tf_op jit(solution)/shard_map/ppermute | solution.py:424
  5.4 2.1 %collective-permute-start.1 = (bf16[16,768]{1,0:T(8,128)(2,1)S(1)}, bf16[16,768]{1,0:T(8,128)(2,1)S(1)}, u32[]{:S(2)}, u32[]{:S(2)}) collective-permute-start(bf16[16,768]{1,0:T(8,128)(2,1)S(1)} %get-tuple-element.37), channel_id=1, source_target_pairs={{1,2},{2,1},{3,4},{4,3},{5,6},{6,5},{7,8},{8,7},{9,10},{10,9},{11,... | collective-permute-start | bytes 73736 | tf_op jit(solution)/shard_map/ppermute | solution.py:495
  7.5 5.8 %collective-permute-start.2 = (bf16[16,768]{1,0:T(8,128)(2,1)S(1)}, bf16[16,768]{1,0:T(8,128)(2,1)S(1)}, u32[]{:S(2)}, u32[]{:S(2)}) collective-permute-start(bf16[16,768]{1,0:T(8,128)(2,1)S(1)} %add_add_fusion), channel_id=1, source_target_pairs={{0,16},{1,17},{2,18},{3,19},{4,20},{5,21},{6,22},{7,23},{8,24},{9,... | collective-permute-start | bytes 73736 | tf_op jit(solution)/shard_map/ppermute | solution.py:424
  14.9 2.1 %collective-permute-start.4 = (bf16[480,384]{1,0:T(8,128)(2,1)S(1)}, bf16[480,384]{1,0:T(8,128)(2,1)S(1)}, u32[]{:S(2)}, u32[]{:S(2)}) collective-permute-start(bf16[480,384]{1,0:T(8,128)(2,1)S(1)} %get-tuple-element.47), channel_id=1, source_target_pairs={{0,1},{1,0},{2,3},{3,2},{4,5},{5,4},{6,7},{7,6},{8,9},{9,8},{10,11... | collective-permute-start | bytes 1105928 | tf_op jit(solution)/shard_map/ppermute | solution.py:424
  17.0 5.8 %collective-permute-start.5 = (bf16[240,384]{1,0:T(8,128)(2,1)S(1)}, bf16[240,384]{1,0:T(8,128)(2,1)S(1)}, u32[]{:S(2)}, u32[]{:S(2)}) collective-permute-start(bf16[240,384]{1,0:T(8,128)(2,1)S(1)} %get-tuple-element.50), channel_id=1, source_target_pairs={{0,2},{1,5},{2,0},{3,7},{4,6},{5,1},{6,4},{7,3},{8,10},{9,13},{10,... | collective-permute-start | bytes 552968 | tf_op jit(solution)/shard_map/ppermute | solution.py:424
  22.9 6.6 %collective-permute-start.6 = (bf16[144,384]{1,0:T(8,128)(2,1)S(1)}, bf16[144,384]{1,0:T(8,128)(2,1)S(1)}, u32[]{:S(2)}, u32[]{:S(2)}) collective-permute-start(bf16[144,384]{1,0:T(8,128)(2,1)S(1)} %fusion), channel_id=1, source_target_pairs={{0,4},{1,9},{2,6},{3,11},{4,0},{5,13},{6,2},{7,15},{8,12},{9,1},{1... | collective-permute-start | bytes 331784 | tf_op jit(solution)/shard_map/ppermute | solution.py:424
  26.1 6.5 %collective-permute-start.8 = (bf16[160,384]{1,0:T(8,128)(2,1)S(1)}, bf16[160,384]{1,0:T(8,128)(2,1)S(1)}, u32[]{:S(2)}, u32[]{:S(2)}) collective-permute-start(bf16[160,384]{1,0:T(8,128)(2,1)S(1)} %fusion.1), channel_id=1, source_target_pairs={{0,4},{1,9},{2,6},{3,11},{4,0},{5,13},{6,2},{7,15},{8,12},{9,1},{1... | collective-permute-start | bytes 368648 | tf_op jit(solution)/shard_map/ppermute | solution.py:424
  29.6 7.3 %collective-permute-start.7 = (bf16[144,384]{1,0:T(8,128)(2,1)S(1)}, bf16[144,384]{1,0:T(8,128)(2,1)S(1)}, u32[]{:S(2)}, u32[]{:S(2)}) collective-permute-start(bf16[144,384]{1,0:T(8,128)(2,1)S(1)} %fusion.2), channel_id=1, source_target_pairs={{0,8},{1,3},{2,10},{3,1},{4,12},{5,7},{6,14},{7,5},{8,0},{9,11},{1... | collective-permute-start | bytes 331784 | tf_op jit(solution)/shard_map/ppermute | solution.py:424
  32.6 5.8 %collective-permute-start.11 = (bf16[160,384]{1,0:T(8,128)(2,1)S(1)}, bf16[160,384]{1,0:T(8,128)(2,1)S(1)}, u32[]{:S(2)}, u32[]{:S(2)}) collective-permute-start(bf16[160,384]{1,0:T(8,128)(2,1)S(1)} %get-tuple-element.68), channel_id=1, source_target_pairs={{0,8},{1,3},{2,10},{3,1},{4,12},{5,7},{6,14},{7,5},{8,0},{9,11},{1... | collective-permute-start | bytes 368648 | tf_op jit(solution)/shard_map/ppermute | solution.py:424
  36.9 4.8 %collective-permute-start.9 = (bf16[144,384]{1,0:T(8,128)(2,1)S(1)}, bf16[144,384]{1,0:T(8,128)(2,1)S(1)}, u32[]{:S(2)}, u32[]{:S(2)}) collective-permute-start(bf16[144,384]{1,0:T(8,128)(2,1)S(1)} %convert_add_fusion.2), channel_id=1, source_target_pairs={{0,2},{1,17},{2,0},{3,19},{4,6},{5,21},{6,4},{7,23},{8,10},{9,25},... | collective-permute-start | bytes 331784 | tf_op jit(solution)/shard_map/ppermute | solution.py:424
  38.5 4.9 %collective-permute-start.12 = (bf16[160,384]{1,0:T(8,128)(2,1)S(1)}, bf16[160,384]{1,0:T(8,128)(2,1)S(1)}, u32[]{:S(2)}, u32[]{:S(2)}) collective-permute-start(bf16[160,384]{1,0:T(8,128)(2,1)S(1)} %pad_maximum_fusion.4), channel_id=1, source_target_pairs={{0,16},{1,5},{2,18},{3,7},{4,20},{5,1},{6,22},{7,3},{8,24},{9,13},... | collective-permute-start | bytes 368648 | tf_op jit(solution)/shard_map/ppermute | solution.py:424
  41.8 4.2 %collective-permute-start.13 = (bf16[288,384]{1,0:T(8,128)(2,1)S(1)}, bf16[288,384]{1,0:T(8,128)(2,1)S(1)}, u32[]{:S(2)}, u32[]{:S(2)}) collective-permute-start(bf16[288,384]{1,0:T(8,128)(2,1)S(1)} %pad_maximum_fusion.left), channel_id=1, source_target_pairs={{0,1},{1,0},{2,3},{3,2},{4,5},{5,4},{6,7},{7,6},{8,9},{9,8},{10,11... | collective-permute-start | bytes 663560 | tf_op jit(solution)/shard_map/ppermute | solution.py:424
  41.8 6.5 %collective-permute-start.10 = (bf16[288,384]{1,0:T(8,128)(2,1)S(1)}, bf16[288,384]{1,0:T(8,128)(2,1)S(1)}, u32[]{:S(2)}, u32[]{:S(2)}) collective-permute-start(bf16[288,384]{1,0:T(8,128)(2,1)S(1)} %pad_maximum_fusion.left), channel_id=1, source_target_pairs={{0,16},{1,5},{2,18},{3,7},{4,20},{5,1},{6,22},{7,3},{8,24},{9,13},... | collective-permute-start | bytes 663560 | tf_op jit(solution)/shard_map/ppermute | solution.py:424
  43.6 5.7 %collective-permute-start.16 = (bf16[256,384]{1,0:T(8,128)(2,1)S(1)}, bf16[256,384]{1,0:T(8,128)(2,1)S(1)}, u32[]{:S(2)}, u32[]{:S(2)}) collective-permute-start(bf16[256,384]{1,0:T(8,128)(2,1)S(1)} %pad_maximum_fusion.1), channel_id=1, source_target_pairs={{0,2},{1,17},{2,0},{3,19},{4,6},{5,21},{6,4},{7,23},{8,10},{9,25},... | collective-permute-start | bytes 589832 | tf_op jit(solution)/shard_map/ppermute | solution.py:424
  44.2 1.8 %collective-permute-start.14 = (bf16[192,384]{1,0:T(8,128)(2,1)S(1)}, bf16[192,384]{1,0:T(8,128)(2,1)S(1)}, u32[]{:S(2)}, u32[]{:S(2)}) collective-permute-start(bf16[192,384]{1,0:T(8,128)(2,1)S(1)} %pad_maximum_fusion.3.right), channel_id=1, source_target_pairs={{0,1},{1,0},{2,3},{3,2},{4,5},{5,4},{6,7},{7,6},{8,9},{9,8},{10,11... | collective-permute-start | bytes 442376 | tf_op jit(solution)/shard_map/ppermute | solution.py:424
  48.3 2.6 %collective-permute-start.15 = (bf16[288,384]{1,0:T(8,128)(2,1)S(1)}, bf16[288,384]{1,0:T(8,128)(2,1)S(1)}, u32[]{:S(2)}, u32[]{:S(2)}) collective-permute-start(bf16[288,384]{1,0:T(8,128)(2,1)S(1)} %collective-permute-done.10.left), channel_id=1, source_target_pairs={{0,1},{1,0},{2,3},{3,2},{4,5},{5,4},{6,7},{7,6},{8,9},{9,8},{10,11... | collective-permute-start | bytes 663560 | tf_op jit(solution)/shard_map/ppermute | solution.py:424
  49.4 1.6 %collective-permute-start.17 = (bf16[256,384]{1,0:T(8,128)(2,1)S(1)}, bf16[256,384]{1,0:T(8,128)(2,1)S(1)}, u32[]{:S(2)}, u32[]{:S(2)}) collective-permute-start(bf16[256,384]{1,0:T(8,128)(2,1)S(1)} %pad_maximum_fusion.2), channel_id=1, source_target_pairs={{0,1},{1,0},{2,3},{3,2},{4,5},{5,4},{6,7},{7,6},{8,9},{9,8},{10,11... | collective-permute-start | bytes 589832 | tf_op jit(solution)/shard_map/ppermute | solution.py:424

commit v5 on v4

--- a/solution.py
+++ b/solution.py
@@ -67,19 +67,14 @@
     positions,
     amounts,
     cot,
-    stem_weight,
-    conv,
     own,
     near,
     far,
-    weight,
-    half_weight,
-    cot_out,
-    conv_out,
     base_v,
     pos_s,
     amt_s,
-    weight_v,
+    top,
+    bottom,
     sems,
 ):
     length = 2 * rows
@@ -89,15 +84,14 @@
         pltpu.make_async_copy(codes, base_v, sems.at[0]),
         pltpu.make_async_copy(positions, pos_s, sems.at[1]),
         pltpu.make_async_copy(amounts, amt_s, sems.at[2]),
-        pltpu.make_async_copy(cot, cot_out, sems.at[3]),
-        pltpu.make_async_copy(stem_weight, weight_v, sems.at[4]),
-        pltpu.make_async_copy(conv, conv_out, sems.at[5]),
+        pltpu.make_async_copy(cot.at[pl.ds(0, 16)], top, sems.at[3]),
+        pltpu.make_async_copy(cot.at[pl.ds(rows - 16, 16)], bottom, sems.at[4]),
     ]
     for copy in copies:
         copy.start()
     ctx = lax.axis_index("context")
     core = lax.rem(ctx, 2)
-    for copy in copies[:4]:
+    for copy in copies:
         copy.wait()
     x = jnp.concatenate([base_v[:, 128 * q : 128 * q + 128] for q in range(tiles)], axis=0)
     spot = (
@@ -134,14 +128,28 @@
         grads = jnp.concatenate([grads, pad], axis=1)
         return jnp.concatenate([edge, grads, jnp.zeros((6, lanes), f32)], axis=0)
 
-    head = message(first, cot_out[0:16, :].astype(f32)[0:2])
-    tail = message(last, cot_out[rows - 16 : rows, :].astype(f32)[14:16])
+    head = message(first, top[...].astype(f32)[0:2])
+    tail = message(last, bottom[...].astype(f32)[14:16])
     own[...] = jnp.concatenate([shifted, blank], axis=0).astype(bf16)
     near[...] = jnp.where(core == 0, tail, head).astype(bf16)
     far[...] = jnp.where(core == 0, head, tail).astype(bf16)
-    copies[4].wait()
+
+
+def second_kernel(
+    cot, stem_weight, conv, near, weight, half_weight, cot_out, conv_out, weight_v, sems
+):
+    del near
+    copies = [
+        pltpu.make_async_copy(stem_weight, weight_v, sems.at[0]),
+        pltpu.make_async_copy(cot, cot_out, sems.at[1]),
+        pltpu.make_async_copy(conv, conv_out, sems.at[2]),
+    ]
+    for copy in copies:
+        copy.start()
+    copies[0].wait()
     stem_terms(weight_v, weight, half_weight)
-    copies[5].wait()
+    for copy in copies[1:]:
+        copy.wait()
 
 
 def stem_terms(weight, out, half_out):
@@ -361,10 +369,7 @@
         from_core = lax.rem(core + flip, 2)
         q = quarter_bit(ctx, from_core)
         for k, p in enumerate(ids):
-            one, two = p % 2, p // 2
-            dq = jnp.where(from_core == chain, one, two)
-            dy = one + two - dq
-            from_q, from_y = lax.rem(q + dq, 2), lax.rem(y + dy, 2)
+            from_q, from_y = lax.rem(q + p // 2, 2), lax.rem(y + p % 2, 2)
             channel = from_y * half + (2 * from_core + from_q) * unit
             for t in range(taps):
                 low = (k * taps + t) * unit
@@ -386,21 +391,24 @@
         copy.wait()
 
 
-def late_kernel(left, right, whole, out, room, sems):
+def late_kernel(left, right, got_left, whole, out, room, sems):
     del whole
-    for copy in put_pieces([(left, 0, 0, (2, 3)), (right, 1, 0, (2, 3))], out, room, sems):
+    pieces = [(left, 0, 0, (2, 3)), (right, 1, 0, (2, 3)), (got_left, 0, 1, (2, 3))]
+    for copy in put_pieces(pieces, out, room, sems):
         copy.wait()
 
 
-def last_kernel(left, right, stem, whole, out, stem_out, room, sems):
+def last_kernel(right, stem, whole, out, stem_out, room, sems, stem_v, stem_sem):
     del whole
-    copies = put_pieces([(left, 0, 1, (2, 3)), (right, 1, 1, (2, 3))], out, room, sems)
     mine = stem[...].astype(bf16).astype(f32)
     total = mine + right[right.shape[0] - stem.shape[0] :, :].astype(f32)
     for k in range(stem_out.shape[0]):
-        stem_out[k] = total[4 * k : 4 * k + 4, :]
-    for copy in copies:
-        copy.wait()
+        stem_v[k] = total[4 * k : 4 * k + 4, :]
+    copy = pltpu.make_async_copy(stem_v, stem_out, stem_sem)
+    copy.start()
+    copies = put_pieces([(right, 1, 1, (2, 3))], out, room, sems)
+    for done in [*copies, copy]:
+        done.wait()
 
 
 def per_device(codes, variant_pos, variant_shift, stem_weight, conv_weight, cotangent):
@@ -459,26 +467,30 @@
     pair_cot = swap(cot, y_bit)
     dma = pltpu.SemaphoreType.DMA
     edge = ((16, lanes), bf16)
-    own, near, far, weight, half_weight, cot_v, conv_v = call(
+    own, near, far = call(
         functools.partial(first_kernel, rows, lanes),
+        [edge, edge, edge],
+        far_off(codes, variant_pos, variant_shift, cot),
         [
-            edge,
-            edge,
-            edge,
+            pltpu.VMEM((1, length), jnp.int32),
+            pltpu.SMEM(variant_pos.shape, jnp.int32),
+            pltpu.SMEM(variant_pos.shape, jnp.int32),
+            pltpu.VMEM((16, width), bf16),
+            pltpu.VMEM((16, width), bf16),
+            dma((5,)),
+        ],
+        compiler_params=params(FIRST_LIMIT),
+    )
+    weight, half_weight, cot_v, conv_v = call(
+        second_kernel,
+        [
             ((192, 2 * width), bf16),
             ((192, width), bf16),
             (cot.shape, bf16),
             (conv_weight.shape, bf16),
         ],
-        far_off(codes, variant_pos, variant_shift, cot, stem_weight, conv_weight),
-        [
-            pltpu.VMEM((1, length), jnp.int32),
-            pltpu.SMEM(variant_pos.shape, jnp.int32),
-            pltpu.SMEM(variant_pos.shape, jnp.int32),
-            pltpu.VMEM(stem_weight.shape, f32),
-            dma((6,)),
-        ],
-        compiler_params=params(FIRST_LIMIT),
+        far_off(cot, stem_weight, conv_weight) + near_by(near),
+        [pltpu.VMEM(stem_weight.shape, f32), dma((3,))],
     )
     near = swap(near, 1)
     cost = pl.CostEstimate(
@@ -493,7 +505,7 @@
         cost_estimate=cost,
     )
     far = lax.ppermute(far, AXES, list(outward.items()))
-    pair_codes = swap(after(own + near + far, back), y_bit)
+    pair_codes = swap(own + near + far, y_bit)
     stem_half = pltpu.VMEM((width, rows + 128), f32)
     gates = ((TAPS * half, rows), bf16)
     part, edges, back = call(
@@ -550,8 +562,8 @@
     odd_rest = odd_rest[1:] + odd_rest[:1]
     for k, (b, odd_b) in enumerate(zip(even_rest, odd_rest)):
         left, right = rounded(left), rounded(right)
-        if k == len(even_rest) - 1:
-            pooled = after(pooled, right)
+        if k == 0:
+            pooled = after(pooled, right.astype(bf16))
         left, right = [v + swap(v.astype(bf16), b, odd_b).astype(f32) for v in (left, right)]
     (features,) = call(
         functools.partial(feature_kernel, rows),
@@ -570,13 +582,13 @@
         return jnp.concatenate([pieces, stem_sum.astype(bf16)], axis=0)
 
     stem_sum = rounded(stem_sum)
-    got_left, got_right = swap(left, x_bit, y_bit), swap(joined(right), y_bit, z_bit)
+    got_left, got_right = swap(left, y_bit), swap(joined(right), y_bit)
     left = jnp.concatenate([left, got_left], axis=0)
     stem_sum = stem_sum + got_right[rest:].astype(f32)
     right = jnp.concatenate([right, got_right[:rest]], axis=0)
 
     stem_sum = rounded(stem_sum)
-    got_left, got_right = swap(left, y_bit, z_bit), swap(joined(right), x_bit, y_bit)
+    got_left, got_right = swap(left, x_bit, z_bit), swap(joined(right), x_bit, z_bit)
     (conv_grad,) = call(
         early_kernel,
         [whole],
@@ -587,20 +599,24 @@
     left, right = got_left, got_right[: 2 * rest]
     left, conv_grad = together(left, conv_grad)
     got_left, got_right = swap(left, 1), swap(joined(right), 1)
-    room = [pltpu.VMEM((TAPS * 2, unit, width), f32), dma((4,))]
     (conv_grad,) = call(
         late_kernel,
         [whole],
-        near_by(left, right) + far_off(conv_grad),
-        room,
-        input_output_aliases={2: 0},
+        near_by(left, right, got_left) + far_off(conv_grad),
+        [pltpu.VMEM((2 * (TAPS + FIRST), unit, width), f32), dma((6,))],
+        input_output_aliases={3: 0},
     )
     conv_grad, stem_grad = call(
         last_kernel,
-        [whole, (stem_weight.shape, f32)],
-        near_by(got_left, got_right, stem_sum) + far_off(conv_grad),
-        room,
-        input_output_aliases={3: 0},
+        [whole, (stem_weight.shape, f32, FAR)],
+        near_by(got_right, stem_sum) + far_off(conv_grad),
+        [
+            pltpu.VMEM((2 * (TAPS - FIRST), unit, width), f32),
+            dma((2,)),
+            pltpu.VMEM(stem_weight.shape, f32),
+            dma,
+        ],
+        input_output_aliases={2: 0},
     )
     return (features[None], d_pooled[None], conv_grad, stem_grad)
 

time: 53.3 us -> 52.1 us (0.977)
  waiting for transfers between devices: 17.5 us -> 13.6 us
  starting transfers between devices: 19 us -> 20.9 us
    ppermute x17, waiting for transfers between devices: 17.5 us -> 13.6 us  [swap(): return lax.ppermute(value, AXES, pairs)]
    ppermute x17, starting transfers between devices: 18.3 us -> 20.2 us  [swap(): return lax.ppermute(value, AXES, pairs)]
    pallas_call x11 -> x12, Pallas kernels: 14.8 us -> 15.3 us  [call(): pl.pallas_call(kernel, out_shape=shapes, in_specs=[spec for _, spec in op...]
  transfers between devices with their start and end apart: 18 -> 18, of which waited for: 11 -> 11; matrix products, arithmetic and copies ran while one was open for 1% -> 1% of each run, Pallas kernels for 24% -> 27%
where the time goes in v5:
time: 52.1 us; the launch traced here: 51.2 us
  starting transfers between devices  20.9 us (40%)
  Pallas kernels  15.3 us (29%)
  waiting for transfers between devices  13.6 us (26%)
  between operations  0.89 us (2%)
    ppermute x17, starting transfers between devices, swap(): return lax.ppermute(value, AXES, pairs)  20.2 us
    pallas_call x12, Pallas kernels, call(): pl.pallas_call(kernel, out_shape=shapes, in_specs=[spec for _, spec in op...  15.3 us
    ppermute x17, waiting for transfers between devices, swap(): return lax.ppermute(value, AXES, pairs)  13.6 us
  transfers between devices with their start and end apart: 18, of which 11 were waited for; matrix products, arithmetic and copies ran while one was open for 1% of the time, Pallas kernels for 27%

profile of v5, /device:TPU:0, one launch (start us, length us, event | category | flops | bytes accessed | tf_op | source)
XLA Modules:
  0.0 51.2 jit_solution(6486784283376494985)
XLA Ops:
  0.6 3.0 %collective-permute-start.3 = (bf16[512,384]{1,0:T(8,128)(2,1)}, bf16[512,384]{1,0:T(8,128)(2,1)S(1)}, u32[]{:S(2)}, u32[]{:S(2)}) collective-permute-start(bf16[512,384]{1,0:T(8,128)(2,1)} %bitcast.3), channel_id=1, source_target_pairs={{0,16},{1,17},{2,18},{3,19},{4,20},{5,21},{6,22},{7,23},{8,24},{9,... | collective-permute-start | bytes 1179656 | tf_op jit(solution)/shard_map/ppermute | solution.py:432
  3.7 1.1 %shard_map.93 = (bf16[16,768]{1,0:T(8,128)(2,1)S(1)}, bf16[16,768]{1,0:T(8,128)(2,1)S(1)}, bf16[16,768]{1,0:T(8,128)(2,1)S(1)}) custom-call(s32[1,1024]{1,0:T(1,128)} %codes.1, s32[1,64]{1,0:T(1,128)} %positions.1, s32[1,64]{1,0:T(1,128)} %amounts.1, bf16[512,384]{1,0:T(8,128)(2,1)} %bitcast.4), custom_call_target="tpu_custom_call" | custom-call | tf_op jit(solution)/shard_map/pallas_call | solution.py:445
  5.5 2.9 %collective-permute-start = (bf16[16,768]{1,0:T(8,128)(2,1)S(1)}, bf16[16,768]{1,0:T(8,128)(2,1)S(1)}, u32[]{:S(2)}, u32[]{:S(2)}) collective-permute-start(bf16[16,768]{1,0:T(8,128)(2,1)S(1)} %get-tuple-element.35.near), channel_id=1, source_target_pairs={{0,1},{1,0},{2,3},{3,2},{4,5},{5,4},{6,7},{7,6},{8,9},{9,8},{10,11... | collective-permute-start | bytes 73736 | tf_op jit(solution)/shard_map/ppermute | solution.py:432
  8.4 1.6 %shard_map.94 = (bf16[192,768]{1,0:T(8,128)(2,1)S(1)}, bf16[192,384]{1,0:T(8,128)(2,1)S(1)}, bf16[512,384]{1,0:T(8,128)(2,1)S(1)}, bf16[5,384,384]{2,1,0:T(8,128)(2,1)S(1)}) custom-call(bf16[512,384]{1,0:T(8,128)(2,1)} %bitcast.5, f32[15,4,384]{2,1,0:T(4,128)} %stem_weight.1, bf16[5,384,384]{2,1,0:T(8,128)(2,1)} %conv.1, ...), custom_call_target="tpu_custom_call" | custom-call | tf_op jit(solution)/shard_map/pallas_call | solution.py:445
  10.6 1.4 %shard_map.95.refs_6_ = f32[512,384]{1,0:T(8,128)S(1)} custom-call(bf16[5,384,384]{2,1,0:T(8,128)(2,1)S(1)} %get-tuple-element.38.conv.refs_4_, bf16[512,384]{1,0:T(8,128)(2,1)S(1)} %get-tuple-element.39.cot.refs_5_), custom_call_target="tpu_custom_call" | custom-call | flops 754974720 | bytes 4194304 | tf_op jit(solution)/shard_map/pallas_call | solution.py:445
  12.0 1.4 %shard_map.96 = (f32[960,384]{1,0:T(8,128)S(1)}, f32[16,384]{1,0:T(8,128)S(1)}, f32[512,384]{1,0:T(8,128)S(1)}) custom-call(bf16[16,768]{1,0:T(8,128)(2,1)S(1)} %get-tuple-element.49.refs_0_.own, bf16[16,768]{1,0:T(8,128)(2,1)S(1)} %collective-permute-done.refs_1_.near, ...), custom_call_target="tpu_custom_call", output_to_operand_aliasing={{2}: (6, {})} | custom-call | tf_op jit(solution)/shard_map/pallas_call | solution.py:445
  13.9 0.9 %shard_map.97 = (bf16[960,512]{1,0:T(8,128)(2,1)S(1)}, f32[512,384]{1,0:T(8,128)S(1)}) custom-call(bf16[16,768]{1,0:T(8,128)(2,1)S(1)} %collective-permute-done.2.refs_0_, bf16[192,384]{1,0:T(8,128)(2,1)S(1)} %get-tuple-element.37.refs_3_.refs_1_, f32[512,384]{1,0:T(8,128)S(1)} %get-tuple-element.41.refs_2_), custom_call_target="tpu_custom_call", output_to_operand_aliasing={{1}: (2, {})} | custom-call | tf_op jit(solution)/shard_map/pallas_call | solution.py:445
  15.6 1.7 %collective-permute-done.4.refs_1_ = bf16[480,384]{1,0:T(8,128)(2,1)S(1)} collective-permute-done((bf16[480,384]{1,0:T(8,128)(2,1)S(1)}, bf16[480,384]{1,0:T(8,128)(2,1)S(1)}, u32[]{:S(2)}, u32[]{:S(2)}) %collective-permute-start.4) | collective-permute-done | bytes 368672 | tf_op jit(solution)/shard_map/ppermute | solution.py:432
  17.3 1.6 %collective-permute-start.5 = (bf16[240,384]{1,0:T(8,128)(2,1)S(1)}, bf16[240,384]{1,0:T(8,128)(2,1)S(1)}, u32[]{:S(2)}, u32[]{:S(2)}) collective-permute-start(bf16[240,384]{1,0:T(8,128)(2,1)S(1)} %get-tuple-element.48), channel_id=1, source_target_pairs={{0,2},{1,5},{2,0},{3,7},{4,6},{5,1},{6,4},{7,3},{8,10},{9,13},{10,... | collective-permute-start | bytes 552968 | tf_op jit(solution)/shard_map/ppermute | solution.py:432
  18.9 2.9 %shard_map.100 = (bf16[512,384]{1,0:T(8,128)(2,1)}, f32[64,384]{1,0:T(8,128)S(1)}, bf16[544,384]{1,0:T(8,128)(2,1)S(1)}, bf16[512,384]{1,0:T(8,128)(2,1)S(1)}) custom-call(bf16[16,768]{1,0:T(8,128)(2,1)S(1)} %get-tuple-element.49.refs_0_.own, bf16[16,768]{1,0:T(8,128)(2,1)S(1)} %collective-permute-done.refs_1_.near, ...), custom_call_target="tpu_custom_call" | custom-call | flops 754974720 | bytes 4194304 | tf_op jit(solution)/shard_map/pallas_call | solution.py:445
  21.8 1.1 %collective-permute-done.5 = bf16[240,384]{1,0:T(8,128)(2,1)S(1)} collective-permute-done((bf16[240,384]{1,0:T(8,128)(2,1)S(1)}, bf16[240,384]{1,0:T(8,128)(2,1)S(1)}, u32[]{:S(2)}, u32[]{:S(2)}) %collective-permute-start.5) | collective-permute-done | bytes 184352 | tf_op jit(solution)/shard_map/ppermute | solution.py:432
  23.0 2.5 %collective-permute-start.6 = (bf16[144,384]{1,0:T(8,128)(2,1)S(1)}, bf16[144,384]{1,0:T(8,128)(2,1)S(1)}, u32[]{:S(2)}, u32[]{:S(2)}) collective-permute-start(bf16[144,384]{1,0:T(8,128)(2,1)S(1)} %fusion), channel_id=1, source_target_pairs={{0,4},{1,9},{2,6},{3,11},{4,0},{5,13},{6,2},{7,15},{8,12},{9,1},{1... | collective-permute-start | bytes 331784 | tf_op jit(solution)/shard_map/ppermute | solution.py:432
  25.6 2.1 %shard_map.101 = bf16[512,384]{1,0:T(8,128)(2,1)} custom-call(bf16[544,384]{1,0:T(8,128)(2,1)S(1)} %get-tuple-element.53.gated, bf16[512,384]{1,0:T(8,128)(2,1)S(1)} %get-tuple-element.56.pooled, bf16[5,384,384]{2,1,0:T(8,128)(2,1)S(1)} %get-tuple-element.38.conv.refs_4_), custom_call_target="tpu_custom_call" | custom-call | flops 754974720 | bytes 4194304 | tf_op jit(solution)/shard_map/pallas_call | solution.py:445
  27.8 1.2 %collective-permute-done.6 = bf16[144,384]{1,0:T(8,128)(2,1)S(1)} collective-permute-done((bf16[144,384]{1,0:T(8,128)(2,1)S(1)}, bf16[144,384]{1,0:T(8,128)(2,1)S(1)}, u32[]{:S(2)}, u32[]{:S(2)}) %collective-permute-start.6) | collective-permute-done | bytes 110624 | tf_op jit(solution)/shard_map/ppermute | solution.py:432
  29.0 3.0 %collective-permute-start.7 = (bf16[144,384]{1,0:T(8,128)(2,1)S(1)}, bf16[144,384]{1,0:T(8,128)(2,1)S(1)}, u32[]{:S(2)}, u32[]{:S(2)}) collective-permute-start(bf16[144,384]{1,0:T(8,128)(2,1)S(1)} %fusion.2), channel_id=1, source_target_pairs={{0,8},{1,3},{2,10},{3,1},{4,12},{5,7},{6,14},{7,5},{8,0},{9,11},{1... | collective-permute-start | bytes 331784 | tf_op jit(solution)/shard_map/ppermute | solution.py:432
  32.1 2.1 %collective-permute-start.9 = (bf16[160,384]{1,0:T(8,128)(2,1)S(1)}, bf16[160,384]{1,0:T(8,128)(2,1)S(1)}, u32[]{:S(2)}, u32[]{:S(2)}) collective-permute-start(bf16[160,384]{1,0:T(8,128)(2,1)S(1)} %fusion.3), channel_id=1, source_target_pairs={{0,8},{1,3},{2,10},{3,1},{4,12},{5,7},{6,14},{7,5},{8,0},{9,11},{1... | collective-permute-start | bytes 368648 | tf_op jit(solution)/shard_map/ppermute | solution.py:432
  34.8 1.1 %collective-permute-start.13 = (bf16[144,384]{1,0:T(8,128)(2,1)S(1)}, bf16[144,384]{1,0:T(8,128)(2,1)S(1)}, u32[]{:S(2)}, u32[]{:S(2)}) collective-permute-start(bf16[144,384]{1,0:T(8,128)(2,1)S(1)} %convert_add_fusion.2), channel_id=1, source_target_pairs={{0,16},{1,17},{2,18},{3,19},{4,20},{5,21},{6,22},{7,23},{8,24},{9,... | collective-permute-start | bytes 331784 | tf_op jit(solution)/shard_map/ppermute | solution.py:432
  35.9 2.0 %collective-permute-done.9 = bf16[160,384]{1,0:T(8,128)(2,1)S(1)} collective-permute-done((bf16[160,384]{1,0:T(8,128)(2,1)S(1)}, bf16[160,384]{1,0:T(8,128)(2,1)S(1)}, u32[]{:S(2)}, u32[]{:S(2)}) %collective-permute-start.9) | collective-permute-done | bytes 122912 | tf_op jit(solution)/shard_map/ppermute | solution.py:432
  38.0 1.1 %collective-permute-start.10 = (bf16[160,384]{1,0:T(8,128)(2,1)S(1)}, bf16[160,384]{1,0:T(8,128)(2,1)S(1)}, u32[]{:S(2)}, u32[]{:S(2)}) collective-permute-start(bf16[160,384]{1,0:T(8,128)(2,1)S(1)} %pad_maximum_fusion.4), channel_id=1, source_target_pairs={{0,16},{1,17},{2,18},{3,19},{4,20},{5,21},{6,22},{7,23},{8,24},{9,... | collective-permute-start | bytes 368648 | tf_op jit(solution)/shard_map/ppermute | solution.py:432
  41.0 2.0 %collective-permute-done.10 = bf16[160,384]{1,0:T(8,128)(2,1)S(1)} collective-permute-done((bf16[160,384]{1,0:T(8,128)(2,1)S(1)}, bf16[160,384]{1,0:T(8,128)(2,1)S(1)}, u32[]{:S(2)}, u32[]{:S(2)}) %collective-permute-start.10) | collective-permute-done | bytes 122912 | tf_op jit(solution)/shard_map/ppermute | solution.py:432
  44.0 1.4 %collective-permute-done.16.got_right = bf16[192,384]{1,0:T(8,128)(2,1)S(1)} collective-permute-done((bf16[192,384]{1,0:T(8,128)(2,1)S(1)}, bf16[192,384]{1,0:T(8,128)(2,1)S(1)}, u32[]{:S(2)}, u32[]{:S(2)}) %collective-permute-start.16) | collective-permute-done | bytes 147488 | tf_op jit(solution)/shard_map/ppermute | solution.py:432
  45.4 1.2 %shard_map.102.whole = f32[5,384,384]{2,1,0:T(8,128)} custom-call(bf16[288,384]{1,0:T(8,128)(2,1)S(1)} %pad_maximum_fusion.left, bf16[192,384]{1,0:T(8,128)(2,1)S(1)} %pad_maximum_fusion.3.right, bf16[288,384]{1,0:T(8,128)(2,1)S(1)} %collective-permute-done.15.got_left, bf16[192,384]{1,0:T(8,128)(2,1)S(1)} %collective-permute-done.16.got_right), custom_call_target="tpu_custom_call" | custom-call | tf_op jit(solution)/shard_map/pallas_call | solution.py:445
  46.8 2.0 %collective-permute-done.11 = bf16[256,384]{1,0:T(8,128)(2,1)S(1)} collective-permute-done((bf16[256,384]{1,0:T(8,128)(2,1)S(1)}, bf16[256,384]{1,0:T(8,128)(2,1)S(1)}, u32[]{:S(2)}, u32[]{:S(2)}) %collective-permute-start.11) | collective-permute-done | bytes 196640 | tf_op jit(solution)/shard_map/ppermute | solution.py:432
  49.0 1.1 %shard_map.103.whole = f32[5,384,384]{2,1,0:T(8,128)} custom-call(bf16[288,384]{1,0:T(8,128)(2,1)S(1)} %collective-permute-done.14.left, bf16[192,384]{1,0:T(8,128)(2,1)S(1)} %slice.39.right, bf16[288,384]{1,0:T(8,128)(2,1)S(1)} %collective-permute-done.17.got_left, f32[5,384,384]{2,1,0:T(8,128)} %shard_map.102.whole), custom_call_target="tpu_custom_call", output_to_operand_aliasing={{}: (3, {})} | custom-call | tf_op jit(solution)/shard_map/pallas_call | solution.py:445
  (44 shorter events, 7.9 us)
Async XLA Ops:
  0.6 14.2 %collective-permute-start.3 = (bf16[512,384]{1,0:T(8,128)(2,1)}, bf16[512,384]{1,0:T(8,128)(2,1)S(1)}, u32[]{:S(2)}, u32[]{:S(2)}) collective-permute-start(bf16[512,384]{1,0:T(8,128)(2,1)} %bitcast.3), channel_id=1, source_target_pairs={{0,16},{1,17},{2,18},{3,19},{4,20},{5,21},{6,22},{7,23},{8,24},{9,... | collective-permute-start | bytes 1179656 | tf_op jit(solution)/shard_map/ppermute | solution.py:432
  4.8 5.2 %collective-permute-start.1 = (bf16[16,768]{1,0:T(8,128)(2,1)S(1)}, bf16[16,768]{1,0:T(8,128)(2,1)S(1)}, u32[]{:S(2)}, u32[]{:S(2)}) collective-permute-start(bf16[16,768]{1,0:T(8,128)(2,1)S(1)} %get-tuple-element.36), channel_id=1, source_target_pairs={{1,2},{2,1},{3,4},{4,3},{5,6},{6,5},{7,8},{8,7},{9,10},{10,9},{11,... | collective-permute-start | bytes 73736 | tf_op jit(solution)/shard_map/ppermute | solution.py:507
  5.5 4.5 %collective-permute-start = (bf16[16,768]{1,0:T(8,128)(2,1)S(1)}, bf16[16,768]{1,0:T(8,128)(2,1)S(1)}, u32[]{:S(2)}, u32[]{:S(2)}) collective-permute-start(bf16[16,768]{1,0:T(8,128)(2,1)S(1)} %get-tuple-element.35.near), channel_id=1, source_target_pairs={{0,1},{1,0},{2,3},{3,2},{4,5},{5,4},{6,7},{7,6},{8,9},{9,8},{10,11... | collective-permute-start | bytes 73736 | tf_op jit(solution)/shard_map/ppermute | solution.py:432
  10.0 3.9 %collective-permute-start.2 = (bf16[16,768]{1,0:T(8,128)(2,1)S(1)}, bf16[16,768]{1,0:T(8,128)(2,1)S(1)}, u32[]{:S(2)}, u32[]{:S(2)}) collective-permute-start(bf16[16,768]{1,0:T(8,128)(2,1)S(1)} %add_add_fusion), channel_id=1, source_target_pairs={{0,16},{1,17},{2,18},{3,19},{4,20},{5,21},{6,22},{7,23},{8,24},{9,... | collective-permute-start | bytes 73736 | tf_op jit(solution)/shard_map/ppermute | solution.py:432
  15.5 1.8 %collective-permute-start.4 = (bf16[480,384]{1,0:T(8,128)(2,1)S(1)}, bf16[480,384]{1,0:T(8,128)(2,1)S(1)}, u32[]{:S(2)}, u32[]{:S(2)}) collective-permute-start(bf16[480,384]{1,0:T(8,128)(2,1)S(1)} %get-tuple-element.45), channel_id=1, source_target_pairs={{0,1},{1,0},{2,3},{3,2},{4,5},{5,4},{6,7},{7,6},{8,9},{9,8},{10,11... | collective-permute-start | bytes 1105928 | tf_op jit(solution)/shard_map/ppermute | solution.py:432
  17.3 5.6 %collective-permute-start.5 = (bf16[240,384]{1,0:T(8,128)(2,1)S(1)}, bf16[240,384]{1,0:T(8,128)(2,1)S(1)}, u32[]{:S(2)}, u32[]{:S(2)}) collective-permute-start(bf16[240,384]{1,0:T(8,128)(2,1)S(1)} %get-tuple-element.48), channel_id=1, source_target_pairs={{0,2},{1,5},{2,0},{3,7},{4,6},{5,1},{6,4},{7,3},{8,10},{9,13},{10,... | collective-permute-start | bytes 552968 | tf_op jit(solution)/shard_map/ppermute | solution.py:432
  23.0 6.0 %collective-permute-start.6 = (bf16[144,384]{1,0:T(8,128)(2,1)S(1)}, bf16[144,384]{1,0:T(8,128)(2,1)S(1)}, u32[]{:S(2)}, u32[]{:S(2)}) collective-permute-start(bf16[144,384]{1,0:T(8,128)(2,1)S(1)} %fusion), channel_id=1, source_target_pairs={{0,4},{1,9},{2,6},{3,11},{4,0},{5,13},{6,2},{7,15},{8,12},{9,1},{1... | collective-permute-start | bytes 331784 | tf_op jit(solution)/shard_map/ppermute | solution.py:432
  25.5 6.5 %collective-permute-start.8 = (bf16[160,384]{1,0:T(8,128)(2,1)S(1)}, bf16[160,384]{1,0:T(8,128)(2,1)S(1)}, u32[]{:S(2)}, u32[]{:S(2)}) collective-permute-start(bf16[160,384]{1,0:T(8,128)(2,1)S(1)} %fusion.1), channel_id=1, source_target_pairs={{0,4},{1,9},{2,6},{3,11},{4,0},{5,13},{6,2},{7,15},{8,12},{9,1},{1... | collective-permute-start | bytes 368648 | tf_op jit(solution)/shard_map/ppermute | solution.py:432
  29.0 5.7 %collective-permute-start.7 = (bf16[144,384]{1,0:T(8,128)(2,1)S(1)}, bf16[144,384]{1,0:T(8,128)(2,1)S(1)}, u32[]{:S(2)}, u32[]{:S(2)}) collective-permute-start(bf16[144,384]{1,0:T(8,128)(2,1)S(1)} %fusion.2), channel_id=1, source_target_pairs={{0,8},{1,3},{2,10},{3,1},{4,12},{5,7},{6,14},{7,5},{8,0},{9,11},{1... | collective-permute-start | bytes 331784 | tf_op jit(solution)/shard_map/ppermute | solution.py:432
  32.1 5.8 %collective-permute-start.9 = (bf16[160,384]{1,0:T(8,128)(2,1)S(1)}, bf16[160,384]{1,0:T(8,128)(2,1)S(1)}, u32[]{:S(2)}, u32[]{:S(2)}) collective-permute-start(bf16[160,384]{1,0:T(8,128)(2,1)S(1)} %fusion.3), channel_id=1, source_target_pairs={{0,8},{1,3},{2,10},{3,1},{4,12},{5,7},{6,14},{7,5},{8,0},{9,11},{1... | collective-permute-start | bytes 368648 | tf_op jit(solution)/shard_map/ppermute | solution.py:432
  34.8 5.2 %collective-permute-start.13 = (bf16[144,384]{1,0:T(8,128)(2,1)S(1)}, bf16[144,384]{1,0:T(8,128)(2,1)S(1)}, u32[]{:S(2)}, u32[]{:S(2)}) collective-permute-start(bf16[144,384]{1,0:T(8,128)(2,1)S(1)} %convert_add_fusion.2), channel_id=1, source_target_pairs={{0,16},{1,17},{2,18},{3,19},{4,20},{5,21},{6,22},{7,23},{8,24},{9,... | collective-permute-start | bytes 331784 | tf_op jit(solution)/shard_map/ppermute | solution.py:432
  38.0 4.9 %collective-permute-start.10 = (bf16[160,384]{1,0:T(8,128)(2,1)S(1)}, bf16[160,384]{1,0:T(8,128)(2,1)S(1)}, u32[]{:S(2)}, u32[]{:S(2)}) collective-permute-start(bf16[160,384]{1,0:T(8,128)(2,1)S(1)} %pad_maximum_fusion.4), channel_id=1, source_target_pairs={{0,16},{1,17},{2,18},{3,19},{4,20},{5,21},{6,22},{7,23},{8,24},{9,... | collective-permute-start | bytes 368648 | tf_op jit(solution)/shard_map/ppermute | solution.py:432
  40.0 5.3 %collective-permute-start.15 = (bf16[288,384]{1,0:T(8,128)(2,1)S(1)}, bf16[288,384]{1,0:T(8,128)(2,1)S(1)}, u32[]{:S(2)}, u32[]{:S(2)}) collective-permute-start(bf16[288,384]{1,0:T(8,128)(2,1)S(1)} %pad_maximum_fusion.left), channel_id=1, source_target_pairs={{0,1},{1,0},{2,3},{3,2},{4,5},{5,4},{6,7},{7,6},{8,9},{9,8},{10,11... | collective-permute-start | bytes 663560 | tf_op jit(solution)/shard_map/ppermute | solution.py:432
  40.1 6.5 %collective-permute-start.14 = (bf16[288,384]{1,0:T(8,128)(2,1)S(1)}, bf16[288,384]{1,0:T(8,128)(2,1)S(1)}, u32[]{:S(2)}, u32[]{:S(2)}) collective-permute-start(bf16[288,384]{1,0:T(8,128)(2,1)S(1)} %pad_maximum_fusion.left), channel_id=1, source_target_pairs={{0,2},{1,5},{2,0},{3,7},{4,6},{5,1},{6,4},{7,3},{8,10},{9,13},{10,... | collective-permute-start | bytes 663560 | tf_op jit(solution)/shard_map/ppermute | solution.py:432
  43.1 5.7 %collective-permute-start.11 = (bf16[256,384]{1,0:T(8,128)(2,1)S(1)}, bf16[256,384]{1,0:T(8,128)(2,1)S(1)}, u32[]{:S(2)}, u32[]{:S(2)}) collective-permute-start(bf16[256,384]{1,0:T(8,128)(2,1)S(1)} %pad_maximum_fusion.1), channel_id=1, source_target_pairs={{0,2},{1,5},{2,0},{3,7},{4,6},{5,1},{6,4},{7,3},{8,10},{9,13},{10,... | collective-permute-start | bytes 589832 | tf_op jit(solution)/shard_map/ppermute | solution.py:432
  43.9 1.4 %collective-permute-start.16 = (bf16[192,384]{1,0:T(8,128)(2,1)S(1)}, bf16[192,384]{1,0:T(8,128)(2,1)S(1)}, u32[]{:S(2)}, u32[]{:S(2)}) collective-permute-start(bf16[192,384]{1,0:T(8,128)(2,1)S(1)} %pad_maximum_fusion.3.right), channel_id=1, source_target_pairs={{0,1},{1,0},{2,3},{3,2},{4,5},{5,4},{6,7},{7,6},{8,9},{9,8},{10,11... | collective-permute-start | bytes 442376 | tf_op jit(solution)/shard_map/ppermute | solution.py:432
  46.6 2.4 %collective-permute-start.17 = (bf16[288,384]{1,0:T(8,128)(2,1)S(1)}, bf16[288,384]{1,0:T(8,128)(2,1)S(1)}, u32[]{:S(2)}, u32[]{:S(2)}) collective-permute-start(bf16[288,384]{1,0:T(8,128)(2,1)S(1)} %collective-permute-done.14.left), channel_id=1, source_target_pairs={{0,1},{1,0},{2,3},{3,2},{4,5},{5,4},{6,7},{7,6},{8,9},{9,8},{10,11... | collective-permute-start | bytes 663560 | tf_op jit(solution)/shard_map/ppermute | solution.py:432
  48.9 1.5 %collective-permute-start.12 = (bf16[256,384]{1,0:T(8,128)(2,1)S(1)}, bf16[256,384]{1,0:T(8,128)(2,1)S(1)}, u32[]{:S(2)}, u32[]{:S(2)}) collective-permute-start(bf16[256,384]{1,0:T(8,128)(2,1)S(1)} %pad_maximum_fusion.2), channel_id=1, source_target_pairs={{0,1},{1,0},{2,3},{3,2},{4,5},{5,4},{6,7},{7,6},{8,9},{9,8},{10,11... | collective-permute-start | bytes 589832 | tf_op jit(solution)/shard_map/ppermute | solution.py:432

commit v6 on v5

--- a/solution.py
+++ b/solution.py
@@ -249,7 +249,7 @@
 
 def quarter_bit(ctx, core):
     far = 4 if lax.axis_size("context") % 8 == 0 else 2
-    return jnp.where(core == 0, lax.rem(ctx // 2, 2), lax.rem(ctx // far, 2))
+    return jnp.where(core == 0, lax.rem(ctx // far, 2), lax.rem(ctx // 2, 2))
 
 
 def split_kernel(value, got, sent, kept):
@@ -369,7 +369,9 @@
         from_core = lax.rem(core + flip, 2)
         q = quarter_bit(ctx, from_core)
         for k, p in enumerate(ids):
-            from_q, from_y = lax.rem(q + p // 2, 2), lax.rem(y + p % 2, 2)
+            dq = jnp.where(from_core == 0, p % 2, p // 2)
+            dy = jnp.where(from_core == 0, p // 2, p % 2)
+            from_q, from_y = lax.rem(q + dq, 2), lax.rem(y + dy, 2)
             channel = from_y * half + (2 * from_core + from_q) * unit
             for t in range(taps):
                 low = (k * taps + t) * unit
@@ -423,8 +425,8 @@
     lanes = -(-(rows + 256) // 128) * 128
     core = lax.axis_index("context") % 2
     cot = cotangent[0]
-    x_bit, y_bit = 2, n_ctx
-    z_bit = 4 if n_ctx % 8 == 0 else 2
+    z_bit, y_bit = 2, n_ctx
+    x_bit = 4 if n_ctx % 8 == 0 else 2
 
     def swap(value, even_bit, odd_bit=None):
         odd_bit = even_bit if odd_bit is None else odd_bit
@@ -497,39 +499,37 @@
         flops=2 * TAPS * rows * width * width, bytes_accessed=4 << 20, transcendentals=0
     )
     padded = rows + 2 * LEAD
-    (back,) = call(
-        functools.partial(back_kernel, rows),
-        [((rows, width), f32)],
-        near_by(conv_v, cot_v),
-        [pltpu.VMEM((padded, width), bf16)],
-        cost_estimate=cost,
-    )
     far = lax.ppermute(far, AXES, list(outward.items()))
     pair_codes = swap(own + near + far, y_bit)
     stem_half = pltpu.VMEM((width, rows + 128), f32)
     gates = ((TAPS * half, rows), bf16)
-    part, edges, back = call(
+    part, edges = call(
         functools.partial(own_kernel, rows, total),
         [((TAPS * half, width), f32), ((16, width), f32)],
         near_by(own, near, far, half_weight, conv_v, cot_v),
         [stem_half, pltpu.VMEM(*gates)],
-        keep=[back],
-    )
-    pair_gates, back = call(
+    )
+    (pair_gates,) = call(
         functools.partial(pair_kernel, rows, total),
         [gates],
         near_by(pair_codes, half_weight),
         [stem_half],
-        keep=[back],
     )
     size = TAPS * half // 2
-    sent, kept, back = call(
+    sent, kept = call(
         sum_kernel,
         [((size, width), bf16), ((size, width), f32)],
         near_by(part, pair_gates, pair_cot),
-        keep=[back],
     )
     got = swap(sent, 1)
+    (back,) = call(
+        functools.partial(back_kernel, rows),
+        [((rows, width), f32)],
+        near_by(conv_v, after(cot_v, sent)),
+        [pltpu.VMEM((padded, width), bf16)],
+        cost_estimate=cost,
+    )
+    got, back = lax.optimization_barrier((got, back))
     size //= 2
     sent, kept, back = call(
         split_kernel,
@@ -582,13 +582,13 @@
         return jnp.concatenate([pieces, stem_sum.astype(bf16)], axis=0)
 
     stem_sum = rounded(stem_sum)
-    got_left, got_right = swap(left, y_bit), swap(joined(right), y_bit)
+    got_left, got_right = swap(left, x_bit, y_bit), swap(joined(right), x_bit, y_bit)
     left = jnp.concatenate([left, got_left], axis=0)
     stem_sum = stem_sum + got_right[rest:].astype(f32)
     right = jnp.concatenate([right, got_right[:rest]], axis=0)
 
     stem_sum = rounded(stem_sum)
-    got_left, got_right = swap(left, x_bit, z_bit), swap(joined(right), x_bit, z_bit)
+    got_left, got_right = swap(left, y_bit, z_bit), swap(joined(right), y_bit, z_bit)
     (conv_grad,) = call(
         early_kernel,
         [whole],

time: 52.1 us -> 51.3 us (0.985); the launches traced: 51.2 us -> 51.1 us
  waiting for transfers between devices: 13.6 us -> 10.7 us
  starting transfers between devices: 20.9 us -> 23.7 us
    ppermute x17, waiting for transfers between devices: 13.6 us -> 10.7 us  [swap(): return lax.ppermute(value, AXES, pairs)]
    ppermute x17, starting transfers between devices: 20.2 us -> 23 us  [swap(): return lax.ppermute(value, AXES, pairs)]
where the time goes in v6:
time: 51.3 us; the launch traced here: 51.1 us
  starting transfers between devices  23.7 us (46%)
  Pallas kernels  15.3 us (30%)
  waiting for transfers between devices  10.7 us (21%)
  between operations  0.87 us (2%)
    ppermute x17, starting transfers between devices, swap(): return lax.ppermute(value, AXES, pairs)  23 us
    pallas_call x12, Pallas kernels, call(): pl.pallas_call(kernel, out_shape=shapes, in_specs=[spec for _, spec in op...  15.3 us
    ppermute x17, waiting for transfers between devices, swap(): return lax.ppermute(value, AXES, pairs)  10.7 us
  transfers between devices with their start and end apart: 18, of which 11 were waited for; matrix products, arithmetic and copies ran while one was open for 1% of the time, Pallas kernels for 27%

profile of v6, /device:TPU:0, one launch (start us, length us, event | category | flops | bytes accessed | tf_op | source)
XLA Modules:
  0.0 51.1 jit_solution(2351413125855733492)
XLA Ops:
  0.6 3.0 %collective-permute-start.3 = (bf16[512,384]{1,0:T(8,128)(2,1)}, bf16[512,384]{1,0:T(8,128)(2,1)S(1)}, u32[]{:S(2)}, u32[]{:S(2)}) collective-permute-start(bf16[512,384]{1,0:T(8,128)(2,1)} %bitcast.3), channel_id=1, source_target_pairs={{0,16},{1,17},{2,18},{3,19},{4,20},{5,21},{6,22},{7,23},{8,24},{9,... | collective-permute-start | bytes 1179656 | tf_op jit(solution)/shard_map/ppermute | solution.py:434
  3.7 1.1 %shard_map.93 = (bf16[16,768]{1,0:T(8,128)(2,1)S(1)}, bf16[16,768]{1,0:T(8,128)(2,1)S(1)}, bf16[16,768]{1,0:T(8,128)(2,1)S(1)}) custom-call(s32[1,1024]{1,0:T(1,128)} %codes.1, s32[1,64]{1,0:T(1,128)} %positions.1, s32[1,64]{1,0:T(1,128)} %amounts.1, bf16[512,384]{1,0:T(8,128)(2,1)} %bitcast.4), custom_call_target="tpu_custom_call" | custom-call | tf_op jit(solution)/shard_map/pallas_call | solution.py:447
  5.5 2.9 %collective-permute-start = (bf16[16,768]{1,0:T(8,128)(2,1)S(1)}, bf16[16,768]{1,0:T(8,128)(2,1)S(1)}, u32[]{:S(2)}, u32[]{:S(2)}) collective-permute-start(bf16[16,768]{1,0:T(8,128)(2,1)S(1)} %get-tuple-element.34.near), channel_id=1, source_target_pairs={{0,1},{1,0},{2,3},{3,2},{4,5},{5,4},{6,7},{7,6},{8,9},{9,8},{10,11... | collective-permute-start | bytes 73736 | tf_op jit(solution)/shard_map/ppermute | solution.py:434
  9.7 1.6 %shard_map.94 = (bf16[192,768]{1,0:T(8,128)(2,1)S(1)}, bf16[192,384]{1,0:T(8,128)(2,1)S(1)}, bf16[512,384]{1,0:T(8,128)(2,1)S(1)}, bf16[5,384,384]{2,1,0:T(8,128)(2,1)S(1)}) custom-call(bf16[512,384]{1,0:T(8,128)(2,1)} %bitcast.5, f32[15,4,384]{2,1,0:T(4,128)} %stem_weight.1, bf16[5,384,384]{2,1,0:T(8,128)(2,1)} %conv.1, ...), custom_call_target="tpu_custom_call" | custom-call | tf_op jit(solution)/shard_map/pallas_call | solution.py:447
  11.3 1.4 %shard_map.95 = (f32[960,384]{1,0:T(8,128)S(1)}, f32[16,384]{1,0:T(8,128)S(1)}) custom-call(bf16[16,768]{1,0:T(8,128)(2,1)S(1)} %get-tuple-element.47.own, bf16[16,768]{1,0:T(8,128)(2,1)S(1)} %collective-permute-done.near, bf16[16,768]{1,0:T(8,128)(2,1)S(1)} %collective-permute-done.1.far, bf16[192,384]{1,0:T(8,128)(2,1)S(1)} %get-tuple-element.36.weight, ...), custom_call_target="tpu_custom_call" | custom-call | tf_op jit(solution)/shard_map/pallas_call | solution.py:447
  13.5 0.9 %shard_map.96.gated = bf16[960,512]{1,0:T(8,128)(2,1)S(1)} custom-call(bf16[16,768]{1,0:T(8,128)(2,1)S(1)} %collective-permute-done.2.codes, bf16[192,384]{1,0:T(8,128)(2,1)S(1)} %get-tuple-element.36.weight), custom_call_target="tpu_custom_call" | custom-call | tf_op jit(solution)/shard_map/pallas_call | solution.py:447
  15.2 1.4 %shard_map.98.refs_2_ = f32[512,384]{1,0:T(8,128)S(1)} custom-call(bf16[5,384,384]{2,1,0:T(8,128)(2,1)S(1)} %get-tuple-element.37.conv, bf16[512,384]{1,0:T(8,128)(2,1)S(1)} %get-tuple-element.42.cot), custom_call_target="tpu_custom_call" | custom-call | flops 754974720 | bytes 4194304 | tf_op jit(solution)/shard_map/pallas_call | solution.py:447
  16.9 2.9 %collective-permute-start.5 = (bf16[240,384]{1,0:T(8,128)(2,1)S(1)}, bf16[240,384]{1,0:T(8,128)(2,1)S(1)}, u32[]{:S(2)}, u32[]{:S(2)}) collective-permute-start(bf16[240,384]{1,0:T(8,128)(2,1)S(1)} %get-tuple-element.46), channel_id=1, source_target_pairs={{0,4},{1,3},{2,6},{3,1},{4,0},{5,7},{6,2},{7,5},{8,12},{9,11},{10,... | collective-permute-start | bytes 552968 | tf_op jit(solution)/shard_map/ppermute | solution.py:434
  19.8 2.9 %shard_map.100 = (bf16[512,384]{1,0:T(8,128)(2,1)}, f32[64,384]{1,0:T(8,128)S(1)}, bf16[544,384]{1,0:T(8,128)(2,1)S(1)}, bf16[512,384]{1,0:T(8,128)(2,1)S(1)}) custom-call(bf16[16,768]{1,0:T(8,128)(2,1)S(1)} %get-tuple-element.47.own, bf16[16,768]{1,0:T(8,128)(2,1)S(1)} %collective-permute-done.near, bf16[16,768]{1,0:T(8,128)(2,1)S(1)} %collective-permute-done.1.far, ...), custom_call_target="tpu_custom_call" | custom-call | flops 754974720 | bytes 4194304 | tf_op jit(solution)/shard_map/pallas_call | solution.py:447
  23.4 1.1 %collective-permute-start.6 = (bf16[144,384]{1,0:T(8,128)(2,1)S(1)}, bf16[144,384]{1,0:T(8,128)(2,1)S(1)}, u32[]{:S(2)}, u32[]{:S(2)}) collective-permute-start(bf16[144,384]{1,0:T(8,128)(2,1)S(1)} %fusion), channel_id=1, source_target_pairs={{0,2},{1,9},{2,0},{3,11},{4,6},{5,13},{6,4},{7,15},{8,10},{9,1},{1... | collective-permute-start | bytes 331784 | tf_op jit(solution)/shard_map/ppermute | solution.py:434
  24.5 1.1 %collective-permute-start.8 = (bf16[160,384]{1,0:T(8,128)(2,1)S(1)}, bf16[160,384]{1,0:T(8,128)(2,1)S(1)}, u32[]{:S(2)}, u32[]{:S(2)}) collective-permute-start(bf16[160,384]{1,0:T(8,128)(2,1)S(1)} %fusion.1), channel_id=1, source_target_pairs={{0,2},{1,9},{2,0},{3,11},{4,6},{5,13},{6,4},{7,15},{8,10},{9,1},{1... | collective-permute-start | bytes 368648 | tf_op jit(solution)/shard_map/ppermute | solution.py:434
  25.6 2.1 %shard_map.101 = bf16[512,384]{1,0:T(8,128)(2,1)} custom-call(bf16[544,384]{1,0:T(8,128)(2,1)S(1)} %get-tuple-element.51.gated, bf16[512,384]{1,0:T(8,128)(2,1)S(1)} %get-tuple-element.54.pooled, bf16[5,384,384]{2,1,0:T(8,128)(2,1)S(1)} %get-tuple-element.37.conv), custom_call_target="tpu_custom_call" | custom-call | flops 754974720 | bytes 4194304 | tf_op jit(solution)/shard_map/pallas_call | solution.py:447
  28.3 3.1 %collective-permute-start.7 = (bf16[144,384]{1,0:T(8,128)(2,1)S(1)}, bf16[144,384]{1,0:T(8,128)(2,1)S(1)}, u32[]{:S(2)}, u32[]{:S(2)}) collective-permute-start(bf16[144,384]{1,0:T(8,128)(2,1)S(1)} %fusion.2), channel_id=1, source_target_pairs={{0,8},{1,5},{2,10},{3,7},{4,12},{5,1},{6,14},{7,3},{8,0},{9,13},{1... | collective-permute-start | bytes 331784 | tf_op jit(solution)/shard_map/ppermute | solution.py:434
  31.4 1.3 %collective-permute-start.9 = (bf16[160,384]{1,0:T(8,128)(2,1)S(1)}, bf16[160,384]{1,0:T(8,128)(2,1)S(1)}, u32[]{:S(2)}, u32[]{:S(2)}) collective-permute-start(bf16[160,384]{1,0:T(8,128)(2,1)S(1)} %fusion.3), channel_id=1, source_target_pairs={{0,8},{1,5},{2,10},{3,7},{4,12},{5,1},{6,14},{7,3},{8,0},{9,13},{1... | collective-permute-start | bytes 368648 | tf_op jit(solution)/shard_map/ppermute | solution.py:434
  32.7 2.1 %collective-permute-done.7 = bf16[144,384]{1,0:T(8,128)(2,1)S(1)} collective-permute-done((bf16[144,384]{1,0:T(8,128)(2,1)S(1)}, bf16[144,384]{1,0:T(8,128)(2,1)S(1)}, u32[]{:S(2)}, u32[]{:S(2)}) %collective-permute-start.7) | collective-permute-done | bytes 110624 | tf_op jit(solution)/shard_map/ppermute | solution.py:434
  34.9 2.0 %collective-permute-start.13 = (bf16[144,384]{1,0:T(8,128)(2,1)S(1)}, bf16[144,384]{1,0:T(8,128)(2,1)S(1)}, u32[]{:S(2)}, u32[]{:S(2)}) collective-permute-start(bf16[144,384]{1,0:T(8,128)(2,1)S(1)} %convert_add_fusion.2), channel_id=1, source_target_pairs={{0,4},{1,17},{2,6},{3,19},{4,0},{5,21},{6,2},{7,23},{8,12},{9,25},... | collective-permute-start | bytes 331784 | tf_op jit(solution)/shard_map/ppermute | solution.py:434
  37.8 2.2 %collective-permute-start.10 = (bf16[160,384]{1,0:T(8,128)(2,1)S(1)}, bf16[160,384]{1,0:T(8,128)(2,1)S(1)}, u32[]{:S(2)}, u32[]{:S(2)}) collective-permute-start(bf16[160,384]{1,0:T(8,128)(2,1)S(1)} %pad_maximum_fusion.4), channel_id=1, source_target_pairs={{0,4},{1,17},{2,6},{3,19},{4,0},{5,21},{6,2},{7,23},{8,12},{9,25},... | collective-permute-start | bytes 368648 | tf_op jit(solution)/shard_map/ppermute | solution.py:434
  40.1 1.3 %collective-permute-start.14 = (bf16[288,384]{1,0:T(8,128)(2,1)S(1)}, bf16[288,384]{1,0:T(8,128)(2,1)S(1)}, u32[]{:S(2)}, u32[]{:S(2)}) collective-permute-start(bf16[288,384]{1,0:T(8,128)(2,1)S(1)} %pad_maximum_fusion.left), channel_id=1, source_target_pairs={{0,16},{1,3},{2,18},{3,1},{4,20},{5,7},{6,22},{7,5},{8,24},{9,11},... | collective-permute-start | bytes 663560 | tf_op jit(solution)/shard_map/ppermute | solution.py:434
  41.4 1.5 %collective-permute-done.10 = bf16[160,384]{1,0:T(8,128)(2,1)S(1)} collective-permute-done((bf16[160,384]{1,0:T(8,128)(2,1)S(1)}, bf16[160,384]{1,0:T(8,128)(2,1)S(1)}, u32[]{:S(2)}, u32[]{:S(2)}) %collective-permute-start.10) | collective-permute-done | bytes 122912 | tf_op jit(solution)/shard_map/ppermute | solution.py:434
  42.9 1.3 %collective-permute-start.11 = (bf16[256,384]{1,0:T(8,128)(2,1)S(1)}, bf16[256,384]{1,0:T(8,128)(2,1)S(1)}, u32[]{:S(2)}, u32[]{:S(2)}) collective-permute-start(bf16[256,384]{1,0:T(8,128)(2,1)S(1)} %pad_maximum_fusion.1), channel_id=1, source_target_pairs={{0,16},{1,3},{2,18},{3,1},{4,20},{5,7},{6,22},{7,5},{8,24},{9,11},... | collective-permute-start | bytes 589832 | tf_op jit(solution)/shard_map/ppermute | solution.py:434
  44.3 1.4 %collective-permute-done.16.got_right = bf16[192,384]{1,0:T(8,128)(2,1)S(1)} collective-permute-done((bf16[192,384]{1,0:T(8,128)(2,1)S(1)}, bf16[192,384]{1,0:T(8,128)(2,1)S(1)}, u32[]{:S(2)}, u32[]{:S(2)}) %collective-permute-start.16) | collective-permute-done | bytes 147488 | tf_op jit(solution)/shard_map/ppermute | solution.py:434
  45.7 1.2 %shard_map.102.whole = f32[5,384,384]{2,1,0:T(8,128)} custom-call(bf16[288,384]{1,0:T(8,128)(2,1)S(1)} %pad_maximum_fusion.left, bf16[192,384]{1,0:T(8,128)(2,1)S(1)} %pad_maximum_fusion.3.right, bf16[288,384]{1,0:T(8,128)(2,1)S(1)} %collective-permute-done.15.got_left, bf16[192,384]{1,0:T(8,128)(2,1)S(1)} %collective-permute-done.16.got_right), custom_call_target="tpu_custom_call" | custom-call | tf_op jit(solution)/shard_map/pallas_call | solution.py:447
  47.1 1.6 %collective-permute-done.11 = bf16[256,384]{1,0:T(8,128)(2,1)S(1)} collective-permute-done((bf16[256,384]{1,0:T(8,128)(2,1)S(1)}, bf16[256,384]{1,0:T(8,128)(2,1)S(1)}, u32[]{:S(2)}, u32[]{:S(2)}) %collective-permute-start.11) | collective-permute-done | bytes 196640 | tf_op jit(solution)/shard_map/ppermute | solution.py:434
  48.9 1.1 %shard_map.103.whole = f32[5,384,384]{2,1,0:T(8,128)} custom-call(bf16[288,384]{1,0:T(8,128)(2,1)S(1)} %collective-permute-done.14.left, bf16[192,384]{1,0:T(8,128)(2,1)S(1)} %slice.39.right, bf16[288,384]{1,0:T(8,128)(2,1)S(1)} %collective-permute-done.17.got_left, f32[5,384,384]{2,1,0:T(8,128)} %shard_map.102.whole), custom_call_target="tpu_custom_call", output_to_operand_aliasing={{}: (3, {})} | custom-call | tf_op jit(solution)/shard_map/pallas_call | solution.py:447
  (44 shorter events, 7.9 us)
Async XLA Ops:
  0.6 13.8 %collective-permute-start.3 = (bf16[512,384]{1,0:T(8,128)(2,1)}, bf16[512,384]{1,0:T(8,128)(2,1)S(1)}, u32[]{:S(2)}, u32[]{:S(2)}) collective-permute-start(bf16[512,384]{1,0:T(8,128)(2,1)} %bitcast.3), channel_id=1, source_target_pairs={{0,16},{1,17},{2,18},{3,19},{4,20},{5,21},{6,22},{7,23},{8,24},{9,... | collective-permute-start | bytes 1179656 | tf_op jit(solution)/shard_map/ppermute | solution.py:434
  4.8 3.6 %collective-permute-start.1 = (bf16[16,768]{1,0:T(8,128)(2,1)S(1)}, bf16[16,768]{1,0:T(8,128)(2,1)S(1)}, u32[]{:S(2)}, u32[]{:S(2)}) collective-permute-start(bf16[16,768]{1,0:T(8,128)(2,1)S(1)} %get-tuple-element.35), channel_id=1, source_target_pairs={{1,2},{2,1},{3,4},{4,3},{5,6},{6,5},{7,8},{8,7},{9,10},{10,9},{11,... | collective-permute-start | bytes 73736 | tf_op jit(solution)/shard_map/ppermute | solution.py:502
  5.5 3.8 %collective-permute-start = (bf16[16,768]{1,0:T(8,128)(2,1)S(1)}, bf16[16,768]{1,0:T(8,128)(2,1)S(1)}, u32[]{:S(2)}, u32[]{:S(2)}) collective-permute-start(bf16[16,768]{1,0:T(8,128)(2,1)S(1)} %get-tuple-element.34.near), channel_id=1, source_target_pairs={{0,1},{1,0},{2,3},{3,2},{4,5},{5,4},{6,7},{7,6},{8,9},{9,8},{10,11... | collective-permute-start | bytes 73736 | tf_op jit(solution)/shard_map/ppermute | solution.py:434
  9.2 4.3 %collective-permute-start.2 = (bf16[16,768]{1,0:T(8,128)(2,1)S(1)}, bf16[16,768]{1,0:T(8,128)(2,1)S(1)}, u32[]{:S(2)}, u32[]{:S(2)}) collective-permute-start(bf16[16,768]{1,0:T(8,128)(2,1)S(1)} %add_add_fusion), channel_id=1, source_target_pairs={{0,16},{1,17},{2,18},{3,19},{4,20},{5,21},{6,22},{7,23},{8,24},{9,... | collective-permute-start | bytes 73736 | tf_op jit(solution)/shard_map/ppermute | solution.py:434
  15.1 1.8 %collective-permute-start.4 = (bf16[480,384]{1,0:T(8,128)(2,1)S(1)}, bf16[480,384]{1,0:T(8,128)(2,1)S(1)}, u32[]{:S(2)}, u32[]{:S(2)}) collective-permute-start(bf16[480,384]{1,0:T(8,128)(2,1)S(1)} %get-tuple-element.41), channel_id=1, source_target_pairs={{0,1},{1,0},{2,3},{3,2},{4,5},{5,4},{6,7},{7,6},{8,9},{9,8},{10,11... | collective-permute-start | bytes 1105928 | tf_op jit(solution)/shard_map/ppermute | solution.py:434
  16.9 6.4 %collective-permute-start.5 = (bf16[240,384]{1,0:T(8,128)(2,1)S(1)}, bf16[240,384]{1,0:T(8,128)(2,1)S(1)}, u32[]{:S(2)}, u32[]{:S(2)}) collective-permute-start(bf16[240,384]{1,0:T(8,128)(2,1)S(1)} %get-tuple-element.46), channel_id=1, source_target_pairs={{0,4},{1,3},{2,6},{3,1},{4,0},{5,7},{6,2},{7,5},{8,12},{9,11},{10,... | collective-permute-start | bytes 552968 | tf_op jit(solution)/shard_map/ppermute | solution.py:434
  23.4 4.8 %collective-permute-start.6 = (bf16[144,384]{1,0:T(8,128)(2,1)S(1)}, bf16[144,384]{1,0:T(8,128)(2,1)S(1)}, u32[]{:S(2)}, u32[]{:S(2)}) collective-permute-start(bf16[144,384]{1,0:T(8,128)(2,1)S(1)} %fusion), channel_id=1, source_target_pairs={{0,2},{1,9},{2,0},{3,11},{4,6},{5,13},{6,4},{7,15},{8,10},{9,1},{1... | collective-permute-start | bytes 331784 | tf_op jit(solution)/shard_map/ppermute | solution.py:434
  24.5 6.8 %collective-permute-start.8 = (bf16[160,384]{1,0:T(8,128)(2,1)S(1)}, bf16[160,384]{1,0:T(8,128)(2,1)S(1)}, u32[]{:S(2)}, u32[]{:S(2)}) collective-permute-start(bf16[160,384]{1,0:T(8,128)(2,1)S(1)} %fusion.1), channel_id=1, source_target_pairs={{0,2},{1,9},{2,0},{3,11},{4,6},{5,13},{6,4},{7,15},{8,10},{9,1},{1... | collective-permute-start | bytes 368648 | tf_op jit(solution)/shard_map/ppermute | solution.py:434
  28.3 6.5 %collective-permute-start.7 = (bf16[144,384]{1,0:T(8,128)(2,1)S(1)}, bf16[144,384]{1,0:T(8,128)(2,1)S(1)}, u32[]{:S(2)}, u32[]{:S(2)}) collective-permute-start(bf16[144,384]{1,0:T(8,128)(2,1)S(1)} %fusion.2), channel_id=1, source_target_pairs={{0,8},{1,5},{2,10},{3,7},{4,12},{5,1},{6,14},{7,3},{8,0},{9,13},{1... | collective-permute-start | bytes 331784 | tf_op jit(solution)/shard_map/ppermute | solution.py:434
  31.4 6.3 %collective-permute-start.9 = (bf16[160,384]{1,0:T(8,128)(2,1)S(1)}, bf16[160,384]{1,0:T(8,128)(2,1)S(1)}, u32[]{:S(2)}, u32[]{:S(2)}) collective-permute-start(bf16[160,384]{1,0:T(8,128)(2,1)S(1)} %fusion.3), channel_id=1, source_target_pairs={{0,8},{1,5},{2,10},{3,7},{4,12},{5,1},{6,14},{7,3},{8,0},{9,13},{1... | collective-permute-start | bytes 368648 | tf_op jit(solution)/shard_map/ppermute | solution.py:434
  34.9 5.1 %collective-permute-start.13 = (bf16[144,384]{1,0:T(8,128)(2,1)S(1)}, bf16[144,384]{1,0:T(8,128)(2,1)S(1)}, u32[]{:S(2)}, u32[]{:S(2)}) collective-permute-start(bf16[144,384]{1,0:T(8,128)(2,1)S(1)} %convert_add_fusion.2), channel_id=1, source_target_pairs={{0,4},{1,17},{2,6},{3,19},{4,0},{5,21},{6,2},{7,23},{8,12},{9,25},... | collective-permute-start | bytes 331784 | tf_op jit(solution)/shard_map/ppermute | solution.py:434
  37.8 5.0 %collective-permute-start.10 = (bf16[160,384]{1,0:T(8,128)(2,1)S(1)}, bf16[160,384]{1,0:T(8,128)(2,1)S(1)}, u32[]{:S(2)}, u32[]{:S(2)}) collective-permute-start(bf16[160,384]{1,0:T(8,128)(2,1)S(1)} %pad_maximum_fusion.4), channel_id=1, source_target_pairs={{0,4},{1,17},{2,6},{3,19},{4,0},{5,21},{6,2},{7,23},{8,12},{9,25},... | collective-permute-start | bytes 368648 | tf_op jit(solution)/shard_map/ppermute | solution.py:434
  40.0 5.6 %collective-permute-start.15 = (bf16[288,384]{1,0:T(8,128)(2,1)S(1)}, bf16[288,384]{1,0:T(8,128)(2,1)S(1)}, u32[]{:S(2)}, u32[]{:S(2)}) collective-permute-start(bf16[288,384]{1,0:T(8,128)(2,1)S(1)} %pad_maximum_fusion.left), channel_id=1, source_target_pairs={{0,1},{1,0},{2,3},{3,2},{4,5},{5,4},{6,7},{7,6},{8,9},{9,8},{10,11... | collective-permute-start | bytes 663560 | tf_op jit(solution)/shard_map/ppermute | solution.py:434
  40.1 6.8 %collective-permute-start.14 = (bf16[288,384]{1,0:T(8,128)(2,1)S(1)}, bf16[288,384]{1,0:T(8,128)(2,1)S(1)}, u32[]{:S(2)}, u32[]{:S(2)}) collective-permute-start(bf16[288,384]{1,0:T(8,128)(2,1)S(1)} %pad_maximum_fusion.left), channel_id=1, source_target_pairs={{0,16},{1,3},{2,18},{3,1},{4,20},{5,7},{6,22},{7,5},{8,24},{9,11},... | collective-permute-start | bytes 663560 | tf_op jit(solution)/shard_map/ppermute | solution.py:434
  42.9 5.7 %collective-permute-start.11 = (bf16[256,384]{1,0:T(8,128)(2,1)S(1)}, bf16[256,384]{1,0:T(8,128)(2,1)S(1)}, u32[]{:S(2)}, u32[]{:S(2)}) collective-permute-start(bf16[256,384]{1,0:T(8,128)(2,1)S(1)} %pad_maximum_fusion.1), channel_id=1, source_target_pairs={{0,16},{1,3},{2,18},{3,1},{4,20},{5,7},{6,22},{7,5},{8,24},{9,11},... | collective-permute-start | bytes 589832 | tf_op jit(solution)/shard_map/ppermute | solution.py:434
  44.2 1.4 %collective-permute-start.16 = (bf16[192,384]{1,0:T(8,128)(2,1)S(1)}, bf16[192,384]{1,0:T(8,128)(2,1)S(1)}, u32[]{:S(2)}, u32[]{:S(2)}) collective-permute-start(bf16[192,384]{1,0:T(8,128)(2,1)S(1)} %pad_maximum_fusion.3.right), channel_id=1, source_target_pairs={{0,1},{1,0},{2,3},{3,2},{4,5},{5,4},{6,7},{7,6},{8,9},{9,8},{10,11... | collective-permute-start | bytes 442376 | tf_op jit(solution)/shard_map/ppermute | solution.py:434
  46.9 2.0 %collective-permute-start.17 = (bf16[288,384]{1,0:T(8,128)(2,1)S(1)}, bf16[288,384]{1,0:T(8,128)(2,1)S(1)}, u32[]{:S(2)}, u32[]{:S(2)}) collective-permute-start(bf16[288,384]{1,0:T(8,128)(2,1)S(1)} %collective-permute-done.14.left), channel_id=1, source_target_pairs={{0,1},{1,0},{2,3},{3,2},{4,5},{5,4},{6,7},{7,6},{8,9},{9,8},{10,11... | collective-permute-start | bytes 663560 | tf_op jit(solution)/shard_map/ppermute | solution.py:434
  48.8 1.5 %collective-permute-start.12 = (bf16[256,384]{1,0:T(8,128)(2,1)S(1)}, bf16[256,384]{1,0:T(8,128)(2,1)S(1)}, u32[]{:S(2)}, u32[]{:S(2)}) collective-permute-start(bf16[256,384]{1,0:T(8,128)(2,1)S(1)} %pad_maximum_fusion.2), channel_id=1, source_target_pairs={{0,1},{1,0},{2,3},{3,2},{4,5},{5,4},{6,7},{7,6},{8,9},{9,8},{10,11... | collective-permute-start | bytes 589832 | tf_op jit(solution)/shard_map/ppermute | solution.py:434

commit v7 on v6

--- a/solution.py
+++ b/solution.py
@@ -233,13 +233,13 @@
     shifted_gates(codes[...].astype(f32)[0:8], first, total, weight, rows, stem, gated)
 
 
-def sum_kernel(part, gated, cot, sent, kept):
+def sum_kernel(other, part, gated, cot, out):
     core = lax.rem(lax.axis_index("context"), 2)
-    size = sent.shape[0]
-    for which, out in ((1 - core, sent), (core, kept)):
-        span = pl.ds(pl.multiple_of(which * size, 16), size)
-        value = part[span, :] + jnp.dot(gated[span, :], cot[...], preferred_element_type=f32)
-        out[...] = value.astype(out.dtype)
+    which = 1 - core if other else core
+    size = out.shape[0]
+    span = pl.ds(pl.multiple_of(which * size, 16), size)
+    value = part[span, :] + jnp.dot(gated[span, :], cot[...], preferred_element_type=f32)
+    out[...] = value.astype(out.dtype)
 
 
 def place_of():
@@ -423,7 +423,6 @@
     unit = half // 4
     total = rows * n_ctx
     lanes = -(-(rows + 256) // 128) * 128
-    core = lax.axis_index("context") % 2
     cot = cotangent[0]
     z_bit, y_bit = 2, n_ctx
     x_bit = 4 if n_ctx % 8 == 0 else 2
@@ -516,12 +515,17 @@
         [stem_half],
     )
     size = TAPS * half // 2
-    sent, kept = call(
-        sum_kernel,
-        [((size, width), bf16), ((size, width), f32)],
+    (sent,) = call(
+        functools.partial(sum_kernel, True),
+        [((size, width), bf16)],
         near_by(part, pair_gates, pair_cot),
     )
     got = swap(sent, 1)
+    (kept,) = call(
+        functools.partial(sum_kernel, False),
+        [((size, width), f32)],
+        near_by(after(part, sent), pair_gates, pair_cot),
+    )
     (back,) = call(
         functools.partial(back_kernel, rows),
         [((rows, width), f32)],

time: 51.3 us -> 51.2 us (level)
    pallas_call x12 -> x13, Pallas kernels: 15.3 us -> 15.4 us  [call(): pl.pallas_call(kernel, out_shape=shapes, in_specs=[spec for _, spec in op...]
  transfers between devices with their start and end apart: 18 -> 18, of which waited for: 11 -> 10; matrix products, arithmetic and copies ran while one was open for 1% -> 1% of each run, Pallas kernels for 27% -> 28%
where the time goes in v7:
time: 51.2 us; the launch traced here: 51 us
  starting transfers between devices  23.6 us (46%)
  Pallas kernels  15.4 us (30%)
  waiting for transfers between devices  10.6 us (21%)
  between operations  0.88 us (2%)
    ppermute x17, starting transfers between devices, swap(): return lax.ppermute(value, AXES, pairs)  22.9 us
    pallas_call x13, Pallas kernels, call(): pl.pallas_call(kernel, out_shape=shapes, in_specs=[spec for _, spec in op...  15.4 us
    ppermute x17, waiting for transfers between devices, swap(): return lax.ppermute(value, AXES, pairs)  10.6 us
  transfers between devices with their start and end apart: 18, of which 10 were waited for; matrix products, arithmetic and copies ran while one was open for 1% of the time, Pallas kernels for 28%

profile of v7, /device:TPU:0, one launch (start us, length us, event | category | flops | bytes accessed | tf_op | source)
XLA Modules:
  0.0 51.0 jit_solution(5697500254198182693)
XLA Ops:
  0.6 3.0 %collective-permute-start.3 = (bf16[512,384]{1,0:T(8,128)(2,1)}, bf16[512,384]{1,0:T(8,128)(2,1)S(1)}, u32[]{:S(2)}, u32[]{:S(2)}) collective-permute-start(bf16[512,384]{1,0:T(8,128)(2,1)} %bitcast.3), channel_id=1, source_target_pairs={{0,16},{1,17},{2,18},{3,19},{4,20},{5,21},{6,22},{7,23},{8,24},{9,... | collective-permute-start | bytes 1179656 | tf_op jit(solution)/shard_map/ppermute | solution.py:433
  3.7 1.1 %shard_map.93 = (bf16[16,768]{1,0:T(8,128)(2,1)S(1)}, bf16[16,768]{1,0:T(8,128)(2,1)S(1)}, bf16[16,768]{1,0:T(8,128)(2,1)S(1)}) custom-call(s32[1,1024]{1,0:T(1,128)} %codes.1, s32[1,64]{1,0:T(1,128)} %positions.1, s32[1,64]{1,0:T(1,128)} %amounts.1, bf16[512,384]{1,0:T(8,128)(2,1)} %bitcast.4), custom_call_target="tpu_custom_call" | custom-call | tf_op jit(solution)/shard_map/pallas_call | solution.py:446
  5.5 2.9 %collective-permute-start = (bf16[16,768]{1,0:T(8,128)(2,1)S(1)}, bf16[16,768]{1,0:T(8,128)(2,1)S(1)}, u32[]{:S(2)}, u32[]{:S(2)}) collective-permute-start(bf16[16,768]{1,0:T(8,128)(2,1)S(1)} %get-tuple-element.33.near), channel_id=1, source_target_pairs={{0,1},{1,0},{2,3},{3,2},{4,5},{5,4},{6,7},{7,6},{8,9},{9,8},{10,11... | collective-permute-start | bytes 73736 | tf_op jit(solution)/shard_map/ppermute | solution.py:433
  9.7 1.6 %shard_map.94 = (bf16[192,768]{1,0:T(8,128)(2,1)S(1)}, bf16[192,384]{1,0:T(8,128)(2,1)S(1)}, bf16[512,384]{1,0:T(8,128)(2,1)S(1)}, bf16[5,384,384]{2,1,0:T(8,128)(2,1)S(1)}) custom-call(bf16[512,384]{1,0:T(8,128)(2,1)} %bitcast.5, f32[15,4,384]{2,1,0:T(4,128)} %stem_weight.1, bf16[5,384,384]{2,1,0:T(8,128)(2,1)} %conv.1, ...), custom_call_target="tpu_custom_call" | custom-call | tf_op jit(solution)/shard_map/pallas_call | solution.py:446
  11.3 1.4 %shard_map.95 = (f32[960,384]{1,0:T(8,128)S(1)}, f32[16,384]{1,0:T(8,128)S(1)}) custom-call(bf16[16,768]{1,0:T(8,128)(2,1)S(1)} %get-tuple-element.45.own, bf16[16,768]{1,0:T(8,128)(2,1)S(1)} %collective-permute-done.near, bf16[16,768]{1,0:T(8,128)(2,1)S(1)} %collective-permute-done.1.far, bf16[192,384]{1,0:T(8,128)(2,1)S(1)} %get-tuple-element.35.weight, ...), custom_call_target="tpu_custom_call" | custom-call | tf_op jit(solution)/shard_map/pallas_call | solution.py:446
  15.4 1.4 %shard_map.99.refs_2_ = f32[512,384]{1,0:T(8,128)S(1)} custom-call(bf16[5,384,384]{2,1,0:T(8,128)(2,1)S(1)} %get-tuple-element.36.conv, bf16[512,384]{1,0:T(8,128)(2,1)S(1)} %get-tuple-element.40.cot), custom_call_target="tpu_custom_call" | custom-call | flops 754974720 | bytes 4194304 | tf_op jit(solution)/shard_map/pallas_call | solution.py:446
  16.9 2.9 %collective-permute-start.5 = (bf16[240,384]{1,0:T(8,128)(2,1)S(1)}, bf16[240,384]{1,0:T(8,128)(2,1)S(1)}, u32[]{:S(2)}, u32[]{:S(2)}) collective-permute-start(bf16[240,384]{1,0:T(8,128)(2,1)S(1)} %get-tuple-element.44), channel_id=1, source_target_pairs={{0,4},{1,3},{2,6},{3,1},{4,0},{5,7},{6,2},{7,5},{8,12},{9,11},{10,... | collective-permute-start | bytes 552968 | tf_op jit(solution)/shard_map/ppermute | solution.py:433
  19.7 2.9 %shard_map.101 = (bf16[512,384]{1,0:T(8,128)(2,1)}, f32[64,384]{1,0:T(8,128)S(1)}, bf16[544,384]{1,0:T(8,128)(2,1)S(1)}, bf16[512,384]{1,0:T(8,128)(2,1)S(1)}) custom-call(bf16[16,768]{1,0:T(8,128)(2,1)S(1)} %get-tuple-element.45.own, bf16[16,768]{1,0:T(8,128)(2,1)S(1)} %collective-permute-done.near, bf16[16,768]{1,0:T(8,128)(2,1)S(1)} %collective-permute-done.1.far, ...), custom_call_target="tpu_custom_call" | custom-call | flops 754974720 | bytes 4194304 | tf_op jit(solution)/shard_map/pallas_call | solution.py:446
  23.4 1.1 %collective-permute-start.6 = (bf16[144,384]{1,0:T(8,128)(2,1)S(1)}, bf16[144,384]{1,0:T(8,128)(2,1)S(1)}, u32[]{:S(2)}, u32[]{:S(2)}) collective-permute-start(bf16[144,384]{1,0:T(8,128)(2,1)S(1)} %fusion), channel_id=1, source_target_pairs={{0,2},{1,9},{2,0},{3,11},{4,6},{5,13},{6,4},{7,15},{8,10},{9,1},{1... | collective-permute-start | bytes 331784 | tf_op jit(solution)/shard_map/ppermute | solution.py:433
  24.5 1.1 %collective-permute-start.8 = (bf16[160,384]{1,0:T(8,128)(2,1)S(1)}, bf16[160,384]{1,0:T(8,128)(2,1)S(1)}, u32[]{:S(2)}, u32[]{:S(2)}) collective-permute-start(bf16[160,384]{1,0:T(8,128)(2,1)S(1)} %fusion.1), channel_id=1, source_target_pairs={{0,2},{1,9},{2,0},{3,11},{4,6},{5,13},{6,4},{7,15},{8,10},{9,1},{1... | collective-permute-start | bytes 368648 | tf_op jit(solution)/shard_map/ppermute | solution.py:433
  25.5 2.1 %shard_map.102 = bf16[512,384]{1,0:T(8,128)(2,1)} custom-call(bf16[544,384]{1,0:T(8,128)(2,1)S(1)} %get-tuple-element.49.gated, bf16[512,384]{1,0:T(8,128)(2,1)S(1)} %get-tuple-element.52.pooled, bf16[5,384,384]{2,1,0:T(8,128)(2,1)S(1)} %get-tuple-element.36.conv), custom_call_target="tpu_custom_call" | custom-call | flops 754974720 | bytes 4194304 | tf_op jit(solution)/shard_map/pallas_call | solution.py:446
  28.2 3.1 %collective-permute-start.7 = (bf16[144,384]{1,0:T(8,128)(2,1)S(1)}, bf16[144,384]{1,0:T(8,128)(2,1)S(1)}, u32[]{:S(2)}, u32[]{:S(2)}) collective-permute-start(bf16[144,384]{1,0:T(8,128)(2,1)S(1)} %fusion.2), channel_id=1, source_target_pairs={{0,8},{1,5},{2,10},{3,7},{4,12},{5,1},{6,14},{7,3},{8,0},{9,13},{1... | collective-permute-start | bytes 331784 | tf_op jit(solution)/shard_map/ppermute | solution.py:433
  31.3 1.3 %collective-permute-start.9 = (bf16[160,384]{1,0:T(8,128)(2,1)S(1)}, bf16[160,384]{1,0:T(8,128)(2,1)S(1)}, u32[]{:S(2)}, u32[]{:S(2)}) collective-permute-start(bf16[160,384]{1,0:T(8,128)(2,1)S(1)} %fusion.3), channel_id=1, source_target_pairs={{0,8},{1,5},{2,10},{3,7},{4,12},{5,1},{6,14},{7,3},{8,0},{9,13},{1... | collective-permute-start | bytes 368648 | tf_op jit(solution)/shard_map/ppermute | solution.py:433
  32.6 2.1 %collective-permute-done.7 = bf16[144,384]{1,0:T(8,128)(2,1)S(1)} collective-permute-done((bf16[144,384]{1,0:T(8,128)(2,1)S(1)}, bf16[144,384]{1,0:T(8,128)(2,1)S(1)}, u32[]{:S(2)}, u32[]{:S(2)}) %collective-permute-start.7) | collective-permute-done | bytes 110624 | tf_op jit(solution)/shard_map/ppermute | solution.py:433
  34.8 1.7 %collective-permute-start.13 = (bf16[144,384]{1,0:T(8,128)(2,1)S(1)}, bf16[144,384]{1,0:T(8,128)(2,1)S(1)}, u32[]{:S(2)}, u32[]{:S(2)}) collective-permute-start(bf16[144,384]{1,0:T(8,128)(2,1)S(1)} %convert_add_fusion.2), channel_id=1, source_target_pairs={{0,4},{1,17},{2,6},{3,19},{4,0},{5,21},{6,2},{7,23},{8,12},{9,25},... | collective-permute-start | bytes 331784 | tf_op jit(solution)/shard_map/ppermute | solution.py:433
  36.5 1.0 %collective-permute-done.9 = bf16[160,384]{1,0:T(8,128)(2,1)S(1)} collective-permute-done((bf16[160,384]{1,0:T(8,128)(2,1)S(1)}, bf16[160,384]{1,0:T(8,128)(2,1)S(1)}, u32[]{:S(2)}, u32[]{:S(2)}) %collective-permute-start.9) | collective-permute-done | bytes 122912 | tf_op jit(solution)/shard_map/ppermute | solution.py:433
  37.6 2.3 %collective-permute-start.10 = (bf16[160,384]{1,0:T(8,128)(2,1)S(1)}, bf16[160,384]{1,0:T(8,128)(2,1)S(1)}, u32[]{:S(2)}, u32[]{:S(2)}) collective-permute-start(bf16[160,384]{1,0:T(8,128)(2,1)S(1)} %pad_maximum_fusion.4), channel_id=1, source_target_pairs={{0,4},{1,17},{2,6},{3,19},{4,0},{5,21},{6,2},{7,23},{8,12},{9,25},... | collective-permute-start | bytes 368648 | tf_op jit(solution)/shard_map/ppermute | solution.py:433
  40.1 1.3 %collective-permute-start.14 = (bf16[288,384]{1,0:T(8,128)(2,1)S(1)}, bf16[288,384]{1,0:T(8,128)(2,1)S(1)}, u32[]{:S(2)}, u32[]{:S(2)}) collective-permute-start(bf16[288,384]{1,0:T(8,128)(2,1)S(1)} %pad_maximum_fusion.left), channel_id=1, source_target_pairs={{0,16},{1,3},{2,18},{3,1},{4,20},{5,7},{6,22},{7,5},{8,24},{9,11},... | collective-permute-start | bytes 663560 | tf_op jit(solution)/shard_map/ppermute | solution.py:433
  41.3 1.5 %collective-permute-done.10 = bf16[160,384]{1,0:T(8,128)(2,1)S(1)} collective-permute-done((bf16[160,384]{1,0:T(8,128)(2,1)S(1)}, bf16[160,384]{1,0:T(8,128)(2,1)S(1)}, u32[]{:S(2)}, u32[]{:S(2)}) %collective-permute-start.10) | collective-permute-done | bytes 122912 | tf_op jit(solution)/shard_map/ppermute | solution.py:433
  42.9 1.3 %collective-permute-start.11 = (bf16[256,384]{1,0:T(8,128)(2,1)S(1)}, bf16[256,384]{1,0:T(8,128)(2,1)S(1)}, u32[]{:S(2)}, u32[]{:S(2)}) collective-permute-start(bf16[256,384]{1,0:T(8,128)(2,1)S(1)} %pad_maximum_fusion.1), channel_id=1, source_target_pairs={{0,16},{1,3},{2,18},{3,1},{4,20},{5,7},{6,22},{7,5},{8,24},{9,11},... | collective-permute-start | bytes 589832 | tf_op jit(solution)/shard_map/ppermute | solution.py:433
  44.2 1.4 %collective-permute-done.16.got_right = bf16[192,384]{1,0:T(8,128)(2,1)S(1)} collective-permute-done((bf16[192,384]{1,0:T(8,128)(2,1)S(1)}, bf16[192,384]{1,0:T(8,128)(2,1)S(1)}, u32[]{:S(2)}, u32[]{:S(2)}) %collective-permute-start.16) | collective-permute-done | bytes 147488 | tf_op jit(solution)/shard_map/ppermute | solution.py:433
  45.6 1.2 %shard_map.103.whole = f32[5,384,384]{2,1,0:T(8,128)} custom-call(bf16[288,384]{1,0:T(8,128)(2,1)S(1)} %pad_maximum_fusion.left, bf16[192,384]{1,0:T(8,128)(2,1)S(1)} %pad_maximum_fusion.3.right, bf16[288,384]{1,0:T(8,128)(2,1)S(1)} %collective-permute-done.15.got_left, bf16[192,384]{1,0:T(8,128)(2,1)S(1)} %collective-permute-done.16.got_right), custom_call_target="tpu_custom_call" | custom-call | tf_op jit(solution)/shard_map/pallas_call | solution.py:446
  47.0 1.6 %collective-permute-done.11 = bf16[256,384]{1,0:T(8,128)(2,1)S(1)} collective-permute-done((bf16[256,384]{1,0:T(8,128)(2,1)S(1)}, bf16[256,384]{1,0:T(8,128)(2,1)S(1)}, u32[]{:S(2)}, u32[]{:S(2)}) %collective-permute-start.11) | collective-permute-done | bytes 196640 | tf_op jit(solution)/shard_map/ppermute | solution.py:433
  48.8 1.1 %shard_map.104.whole = f32[5,384,384]{2,1,0:T(8,128)} custom-call(bf16[288,384]{1,0:T(8,128)(2,1)S(1)} %collective-permute-done.14.left, bf16[192,384]{1,0:T(8,128)(2,1)S(1)} %slice.39.right, bf16[288,384]{1,0:T(8,128)(2,1)S(1)} %collective-permute-done.17.got_left, f32[5,384,384]{2,1,0:T(8,128)} %shard_map.103.whole), custom_call_target="tpu_custom_call", output_to_operand_aliasing={{}: (3, {})} | custom-call | tf_op jit(solution)/shard_map/pallas_call | solution.py:446
  (45 shorter events, 7.9 us)
Async XLA Ops:
  0.6 13.8 %collective-permute-start.3 = (bf16[512,384]{1,0:T(8,128)(2,1)}, bf16[512,384]{1,0:T(8,128)(2,1)S(1)}, u32[]{:S(2)}, u32[]{:S(2)}) collective-permute-start(bf16[512,384]{1,0:T(8,128)(2,1)} %bitcast.3), channel_id=1, source_target_pairs={{0,16},{1,17},{2,18},{3,19},{4,20},{5,21},{6,22},{7,23},{8,24},{9,... | collective-permute-start | bytes 1179656 | tf_op jit(solution)/shard_map/ppermute | solution.py:433
  4.8 3.6 %collective-permute-start.1 = (bf16[16,768]{1,0:T(8,128)(2,1)S(1)}, bf16[16,768]{1,0:T(8,128)(2,1)S(1)}, u32[]{:S(2)}, u32[]{:S(2)}) collective-permute-start(bf16[16,768]{1,0:T(8,128)(2,1)S(1)} %get-tuple-element.34), channel_id=1, source_target_pairs={{1,2},{2,1},{3,4},{4,3},{5,6},{6,5},{7,8},{8,7},{9,10},{10,9},{11,... | collective-permute-start | bytes 73736 | tf_op jit(solution)/shard_map/ppermute | solution.py:501
  5.5 3.8 %collective-permute-start = (bf16[16,768]{1,0:T(8,128)(2,1)S(1)}, bf16[16,768]{1,0:T(8,128)(2,1)S(1)}, u32[]{:S(2)}, u32[]{:S(2)}) collective-permute-start(bf16[16,768]{1,0:T(8,128)(2,1)S(1)} %get-tuple-element.33.near), channel_id=1, source_target_pairs={{0,1},{1,0},{2,3},{3,2},{4,5},{5,4},{6,7},{7,6},{8,9},{9,8},{10,11... | collective-permute-start | bytes 73736 | tf_op jit(solution)/shard_map/ppermute | solution.py:433
  9.2 4.3 %collective-permute-start.2 = (bf16[16,768]{1,0:T(8,128)(2,1)S(1)}, bf16[16,768]{1,0:T(8,128)(2,1)S(1)}, u32[]{:S(2)}, u32[]{:S(2)}) collective-permute-start(bf16[16,768]{1,0:T(8,128)(2,1)S(1)} %add_add_fusion), channel_id=1, source_target_pairs={{0,16},{1,17},{2,18},{3,19},{4,20},{5,21},{6,22},{7,23},{8,24},{9,... | collective-permute-start | bytes 73736 | tf_op jit(solution)/shard_map/ppermute | solution.py:433
  14.9 1.9 %collective-permute-start.4 = (bf16[480,384]{1,0:T(8,128)(2,1)S(1)}, bf16[480,384]{1,0:T(8,128)(2,1)S(1)}, u32[]{:S(2)}, u32[]{:S(2)}) collective-permute-start(bf16[480,384]{1,0:T(8,128)(2,1)S(1)} %shard_map.97), channel_id=1, source_target_pairs={{0,1},{1,0},{2,3},{3,2},{4,5},{5,4},{6,7},{7,6},{8,9},{9,8},{10,11... | collective-permute-start | bytes 1105928 | tf_op jit(solution)/shard_map/ppermute | solution.py:433
  16.9 6.4 %collective-permute-start.5 = (bf16[240,384]{1,0:T(8,128)(2,1)S(1)}, bf16[240,384]{1,0:T(8,128)(2,1)S(1)}, u32[]{:S(2)}, u32[]{:S(2)}) collective-permute-start(bf16[240,384]{1,0:T(8,128)(2,1)S(1)} %get-tuple-element.44), channel_id=1, source_target_pairs={{0,4},{1,3},{2,6},{3,1},{4,0},{5,7},{6,2},{7,5},{8,12},{9,11},{10,... | collective-permute-start | bytes 552968 | tf_op jit(solution)/shard_map/ppermute | solution.py:433
  23.4 4.8 %collective-permute-start.6 = (bf16[144,384]{1,0:T(8,128)(2,1)S(1)}, bf16[144,384]{1,0:T(8,128)(2,1)S(1)}, u32[]{:S(2)}, u32[]{:S(2)}) collective-permute-start(bf16[144,384]{1,0:T(8,128)(2,1)S(1)} %fusion), channel_id=1, source_target_pairs={{0,2},{1,9},{2,0},{3,11},{4,6},{5,13},{6,4},{7,15},{8,10},{9,1},{1... | collective-permute-start | bytes 331784 | tf_op jit(solution)/shard_map/ppermute | solution.py:433
  24.5 6.8 %collective-permute-start.8 = (bf16[160,384]{1,0:T(8,128)(2,1)S(1)}, bf16[160,384]{1,0:T(8,128)(2,1)S(1)}, u32[]{:S(2)}, u32[]{:S(2)}) collective-permute-start(bf16[160,384]{1,0:T(8,128)(2,1)S(1)} %fusion.1), channel_id=1, source_target_pairs={{0,2},{1,9},{2,0},{3,11},{4,6},{5,13},{6,4},{7,15},{8,10},{9,1},{1... | collective-permute-start | bytes 368648 | tf_op jit(solution)/shard_map/ppermute | solution.py:433
  28.2 6.5 %collective-permute-start.7 = (bf16[144,384]{1,0:T(8,128)(2,1)S(1)}, bf16[144,384]{1,0:T(8,128)(2,1)S(1)}, u32[]{:S(2)}, u32[]{:S(2)}) collective-permute-start(bf16[144,384]{1,0:T(8,128)(2,1)S(1)} %fusion.2), channel_id=1, source_target_pairs={{0,8},{1,5},{2,10},{3,7},{4,12},{5,1},{6,14},{7,3},{8,0},{9,13},{1... | collective-permute-start | bytes 331784 | tf_op jit(solution)/shard_map/ppermute | solution.py:433
  31.3 6.2 %collective-permute-start.9 = (bf16[160,384]{1,0:T(8,128)(2,1)S(1)}, bf16[160,384]{1,0:T(8,128)(2,1)S(1)}, u32[]{:S(2)}, u32[]{:S(2)}) collective-permute-start(bf16[160,384]{1,0:T(8,128)(2,1)S(1)} %fusion.3), channel_id=1, source_target_pairs={{0,8},{1,5},{2,10},{3,7},{4,12},{5,1},{6,14},{7,3},{8,0},{9,13},{1... | collective-permute-start | bytes 368648 | tf_op jit(solution)/shard_map/ppermute | solution.py:433
  34.8 5.2 %collective-permute-start.13 = (bf16[144,384]{1,0:T(8,128)(2,1)S(1)}, bf16[144,384]{1,0:T(8,128)(2,1)S(1)}, u32[]{:S(2)}, u32[]{:S(2)}) collective-permute-start(bf16[144,384]{1,0:T(8,128)(2,1)S(1)} %convert_add_fusion.2), channel_id=1, source_target_pairs={{0,4},{1,17},{2,6},{3,19},{4,0},{5,21},{6,2},{7,23},{8,12},{9,25},... | collective-permute-start | bytes 331784 | tf_op jit(solution)/shard_map/ppermute | solution.py:433
  37.6 5.2 %collective-permute-start.10 = (bf16[160,384]{1,0:T(8,128)(2,1)S(1)}, bf16[160,384]{1,0:T(8,128)(2,1)S(1)}, u32[]{:S(2)}, u32[]{:S(2)}) collective-permute-start(bf16[160,384]{1,0:T(8,128)(2,1)S(1)} %pad_maximum_fusion.4), channel_id=1, source_target_pairs={{0,4},{1,17},{2,6},{3,19},{4,0},{5,21},{6,2},{7,23},{8,12},{9,25},... | collective-permute-start | bytes 368648 | tf_op jit(solution)/shard_map/ppermute | solution.py:433
  40.0 5.6 %collective-permute-start.15 = (bf16[288,384]{1,0:T(8,128)(2,1)S(1)}, bf16[288,384]{1,0:T(8,128)(2,1)S(1)}, u32[]{:S(2)}, u32[]{:S(2)}) collective-permute-start(bf16[288,384]{1,0:T(8,128)(2,1)S(1)} %pad_maximum_fusion.left), channel_id=1, source_target_pairs={{0,1},{1,0},{2,3},{3,2},{4,5},{5,4},{6,7},{7,6},{8,9},{9,8},{10,11... | collective-permute-start | bytes 663560 | tf_op jit(solution)/shard_map/ppermute | solution.py:433
  40.1 6.8 %collective-permute-start.14 = (bf16[288,384]{1,0:T(8,128)(2,1)S(1)}, bf16[288,384]{1,0:T(8,128)(2,1)S(1)}, u32[]{:S(2)}, u32[]{:S(2)}) collective-permute-start(bf16[288,384]{1,0:T(8,128)(2,1)S(1)} %pad_maximum_fusion.left), channel_id=1, source_target_pairs={{0,16},{1,3},{2,18},{3,1},{4,20},{5,7},{6,22},{7,5},{8,24},{9,11},... | collective-permute-start | bytes 663560 | tf_op jit(solution)/shard_map/ppermute | solution.py:433
  42.9 5.7 %collective-permute-start.11 = (bf16[256,384]{1,0:T(8,128)(2,1)S(1)}, bf16[256,384]{1,0:T(8,128)(2,1)S(1)}, u32[]{:S(2)}, u32[]{:S(2)}) collective-permute-start(bf16[256,384]{1,0:T(8,128)(2,1)S(1)} %pad_maximum_fusion.1), channel_id=1, source_target_pairs={{0,16},{1,3},{2,18},{3,1},{4,20},{5,7},{6,22},{7,5},{8,24},{9,11},... | collective-permute-start | bytes 589832 | tf_op jit(solution)/shard_map/ppermute | solution.py:433
  44.2 1.4 %collective-permute-start.16 = (bf16[192,384]{1,0:T(8,128)(2,1)S(1)}, bf16[192,384]{1,0:T(8,128)(2,1)S(1)}, u32[]{:S(2)}, u32[]{:S(2)}) collective-permute-start(bf16[192,384]{1,0:T(8,128)(2,1)S(1)} %pad_maximum_fusion.3.right), channel_id=1, source_target_pairs={{0,1},{1,0},{2,3},{3,2},{4,5},{5,4},{6,7},{7,6},{8,9},{9,8},{10,11... | collective-permute-start | bytes 442376 | tf_op jit(solution)/shard_map/ppermute | solution.py:433
  46.8 2.0 %collective-permute-start.17 = (bf16[288,384]{1,0:T(8,128)(2,1)S(1)}, bf16[288,384]{1,0:T(8,128)(2,1)S(1)}, u32[]{:S(2)}, u32[]{:S(2)}) collective-permute-start(bf16[288,384]{1,0:T(8,128)(2,1)S(1)} %collective-permute-done.14.left), channel_id=1, source_target_pairs={{0,1},{1,0},{2,3},{3,2},{4,5},{5,4},{6,7},{7,6},{8,9},{9,8},{10,11... | collective-permute-start | bytes 663560 | tf_op jit(solution)/shard_map/ppermute | solution.py:433
  48.7 1.5 %collective-permute-start.12 = (bf16[256,384]{1,0:T(8,128)(2,1)S(1)}, bf16[256,384]{1,0:T(8,128)(2,1)S(1)}, u32[]{:S(2)}, u32[]{:S(2)}) collective-permute-start(bf16[256,384]{1,0:T(8,128)(2,1)S(1)} %pad_maximum_fusion.2), channel_id=1, source_target_pairs={{0,1},{1,0},{2,3},{3,2},{4,5},{5,4},{6,7},{7,6},{8,9},{9,8},{10,11... | collective-permute-start | bytes 589832 | tf_op jit(solution)/shard_map/ppermute | solution.py:433

commit v8 on v7

--- a/solution.py
+++ b/solution.py
@@ -266,10 +266,10 @@
     ext[0:LEAD, :] = blank
     ext[LEAD : LEAD + rows, :] = cot[...]
     ext[LEAD + rows :, :] = blank
-    for t in range(TAPS):
-        start = LEAD + 2 - t
-        term = turned(ext[start : start + rows, :], conv[t])
-        back[...] = term if t == 0 else back[...] + term
+    terms = [
+        turned(ext[LEAD + 2 - t : LEAD + 2 - t + rows, :], conv[t]) for t in range(TAPS)
+    ]
+    back[...] = sum(terms[1:], terms[0])
 
 
 def turned(left, right):

time: 51.2 us -> 51.2 us (level)
  no operation moved by 1% of the time
where the time goes in v8:
time: 51.2 us; the launch traced here: 51 us
  starting transfers between devices  23.6 us (46%)
  Pallas kernels  15.4 us (30%)
  waiting for transfers between devices  10.6 us (21%)
  between operations  0.88 us (2%)
    ppermute x17, starting transfers between devices, swap(): return lax.ppermute(value, AXES, pairs)  22.9 us
    pallas_call x13, Pallas kernels, call(): pl.pallas_call(kernel, out_shape=shapes, in_specs=[spec for _, spec in op...  15.4 us
    ppermute x17, waiting for transfers between devices, swap(): return lax.ppermute(value, AXES, pairs)  10.6 us
  transfers between devices with their start and end apart: 18, of which 10 were waited for; matrix products, arithmetic and copies ran while one was open for 1% of the time, Pallas kernels for 28%

profile of v8, /device:TPU:0, one launch (start us, length us, event | category | flops | bytes accessed | tf_op | source)
XLA Modules:
  0.0 51.0 jit_solution(2095206332209093491)
XLA Ops:
  0.6 3.0 %collective-permute-start.3 = (bf16[512,384]{1,0:T(8,128)(2,1)}, bf16[512,384]{1,0:T(8,128)(2,1)S(1)}, u32[]{:S(2)}, u32[]{:S(2)}) collective-permute-start(bf16[512,384]{1,0:T(8,128)(2,1)} %bitcast.3), channel_id=1, source_target_pairs={{0,16},{1,17},{2,18},{3,19},{4,20},{5,21},{6,22},{7,23},{8,24},{9,... | collective-permute-start | bytes 1179656 | tf_op jit(solution)/shard_map/ppermute | solution.py:433
  3.7 1.1 %shard_map.93 = (bf16[16,768]{1,0:T(8,128)(2,1)S(1)}, bf16[16,768]{1,0:T(8,128)(2,1)S(1)}, bf16[16,768]{1,0:T(8,128)(2,1)S(1)}) custom-call(s32[1,1024]{1,0:T(1,128)} %codes.1, s32[1,64]{1,0:T(1,128)} %positions.1, s32[1,64]{1,0:T(1,128)} %amounts.1, bf16[512,384]{1,0:T(8,128)(2,1)} %bitcast.4), custom_call_target="tpu_custom_call" | custom-call | tf_op jit(solution)/shard_map/pallas_call | solution.py:446
  5.5 2.9 %collective-permute-start = (bf16[16,768]{1,0:T(8,128)(2,1)S(1)}, bf16[16,768]{1,0:T(8,128)(2,1)S(1)}, u32[]{:S(2)}, u32[]{:S(2)}) collective-permute-start(bf16[16,768]{1,0:T(8,128)(2,1)S(1)} %get-tuple-element.33.near), channel_id=1, source_target_pairs={{0,1},{1,0},{2,3},{3,2},{4,5},{5,4},{6,7},{7,6},{8,9},{9,8},{10,11... | collective-permute-start | bytes 73736 | tf_op jit(solution)/shard_map/ppermute | solution.py:433
  9.7 1.6 %shard_map.94 = (bf16[192,768]{1,0:T(8,128)(2,1)S(1)}, bf16[192,384]{1,0:T(8,128)(2,1)S(1)}, bf16[512,384]{1,0:T(8,128)(2,1)S(1)}, bf16[5,384,384]{2,1,0:T(8,128)(2,1)S(1)}) custom-call(bf16[512,384]{1,0:T(8,128)(2,1)} %bitcast.5, f32[15,4,384]{2,1,0:T(4,128)} %stem_weight.1, bf16[5,384,384]{2,1,0:T(8,128)(2,1)} %conv.1, ...), custom_call_target="tpu_custom_call" | custom-call | tf_op jit(solution)/shard_map/pallas_call | solution.py:446
  11.3 1.4 %shard_map.95 = (f32[960,384]{1,0:T(8,128)S(1)}, f32[16,384]{1,0:T(8,128)S(1)}) custom-call(bf16[16,768]{1,0:T(8,128)(2,1)S(1)} %get-tuple-element.45.own, bf16[16,768]{1,0:T(8,128)(2,1)S(1)} %collective-permute-done.near, bf16[16,768]{1,0:T(8,128)(2,1)S(1)} %collective-permute-done.1.far, bf16[192,384]{1,0:T(8,128)(2,1)S(1)} %get-tuple-element.35.weight, ...), custom_call_target="tpu_custom_call" | custom-call | tf_op jit(solution)/shard_map/pallas_call | solution.py:446
  15.4 1.4 %shard_map.99.refs_2_ = f32[512,384]{1,0:T(8,128)S(1)} custom-call(bf16[5,384,384]{2,1,0:T(8,128)(2,1)S(1)} %get-tuple-element.36.conv, bf16[512,384]{1,0:T(8,128)(2,1)S(1)} %get-tuple-element.40.cot), custom_call_target="tpu_custom_call" | custom-call | flops 754974720 | bytes 4194304 | tf_op jit(solution)/shard_map/pallas_call | solution.py:446
  16.9 2.9 %collective-permute-start.5 = (bf16[240,384]{1,0:T(8,128)(2,1)S(1)}, bf16[240,384]{1,0:T(8,128)(2,1)S(1)}, u32[]{:S(2)}, u32[]{:S(2)}) collective-permute-start(bf16[240,384]{1,0:T(8,128)(2,1)S(1)} %get-tuple-element.44), channel_id=1, source_target_pairs={{0,4},{1,3},{2,6},{3,1},{4,0},{5,7},{6,2},{7,5},{8,12},{9,11},{10,... | collective-permute-start | bytes 552968 | tf_op jit(solution)/shard_map/ppermute | solution.py:433
  19.8 2.9 %shard_map.101 = (bf16[512,384]{1,0:T(8,128)(2,1)}, f32[64,384]{1,0:T(8,128)S(1)}, bf16[544,384]{1,0:T(8,128)(2,1)S(1)}, bf16[512,384]{1,0:T(8,128)(2,1)S(1)}) custom-call(bf16[16,768]{1,0:T(8,128)(2,1)S(1)} %get-tuple-element.45.own, bf16[16,768]{1,0:T(8,128)(2,1)S(1)} %collective-permute-done.near, bf16[16,768]{1,0:T(8,128)(2,1)S(1)} %collective-permute-done.1.far, ...), custom_call_target="tpu_custom_call" | custom-call | flops 754974720 | bytes 4194304 | tf_op jit(solution)/shard_map/pallas_call | solution.py:446
  23.4 1.1 %collective-permute-start.6 = (bf16[144,384]{1,0:T(8,128)(2,1)S(1)}, bf16[144,384]{1,0:T(8,128)(2,1)S(1)}, u32[]{:S(2)}, u32[]{:S(2)}) collective-permute-start(bf16[144,384]{1,0:T(8,128)(2,1)S(1)} %fusion), channel_id=1, source_target_pairs={{0,2},{1,9},{2,0},{3,11},{4,6},{5,13},{6,4},{7,15},{8,10},{9,1},{1... | collective-permute-start | bytes 331784 | tf_op jit(solution)/shard_map/ppermute | solution.py:433
  24.5 1.1 %collective-permute-start.8 = (bf16[160,384]{1,0:T(8,128)(2,1)S(1)}, bf16[160,384]{1,0:T(8,128)(2,1)S(1)}, u32[]{:S(2)}, u32[]{:S(2)}) collective-permute-start(bf16[160,384]{1,0:T(8,128)(2,1)S(1)} %fusion.1), channel_id=1, source_target_pairs={{0,2},{1,9},{2,0},{3,11},{4,6},{5,13},{6,4},{7,15},{8,10},{9,1},{1... | collective-permute-start | bytes 368648 | tf_op jit(solution)/shard_map/ppermute | solution.py:433
  25.5 2.1 %shard_map.102 = bf16[512,384]{1,0:T(8,128)(2,1)} custom-call(bf16[544,384]{1,0:T(8,128)(2,1)S(1)} %get-tuple-element.49.gated, bf16[512,384]{1,0:T(8,128)(2,1)S(1)} %get-tuple-element.52.pooled, bf16[5,384,384]{2,1,0:T(8,128)(2,1)S(1)} %get-tuple-element.36.conv), custom_call_target="tpu_custom_call" | custom-call | flops 754974720 | bytes 4194304 | tf_op jit(solution)/shard_map/pallas_call | solution.py:446
  28.2 3.1 %collective-permute-start.7 = (bf16[144,384]{1,0:T(8,128)(2,1)S(1)}, bf16[144,384]{1,0:T(8,128)(2,1)S(1)}, u32[]{:S(2)}, u32[]{:S(2)}) collective-permute-start(bf16[144,384]{1,0:T(8,128)(2,1)S(1)} %fusion.2), channel_id=1, source_target_pairs={{0,8},{1,5},{2,10},{3,7},{4,12},{5,1},{6,14},{7,3},{8,0},{9,13},{1... | collective-permute-start | bytes 331784 | tf_op jit(solution)/shard_map/ppermute | solution.py:433
  31.4 1.3 %collective-permute-start.9 = (bf16[160,384]{1,0:T(8,128)(2,1)S(1)}, bf16[160,384]{1,0:T(8,128)(2,1)S(1)}, u32[]{:S(2)}, u32[]{:S(2)}) collective-permute-start(bf16[160,384]{1,0:T(8,128)(2,1)S(1)} %fusion.3), channel_id=1, source_target_pairs={{0,8},{1,5},{2,10},{3,7},{4,12},{5,1},{6,14},{7,3},{8,0},{9,13},{1... | collective-permute-start | bytes 368648 | tf_op jit(solution)/shard_map/ppermute | solution.py:433
  32.6 2.1 %collective-permute-done.7 = bf16[144,384]{1,0:T(8,128)(2,1)S(1)} collective-permute-done((bf16[144,384]{1,0:T(8,128)(2,1)S(1)}, bf16[144,384]{1,0:T(8,128)(2,1)S(1)}, u32[]{:S(2)}, u32[]{:S(2)}) %collective-permute-start.7) | collective-permute-done | bytes 110624 | tf_op jit(solution)/shard_map/ppermute | solution.py:433
  34.8 1.7 %collective-permute-start.13 = (bf16[144,384]{1,0:T(8,128)(2,1)S(1)}, bf16[144,384]{1,0:T(8,128)(2,1)S(1)}, u32[]{:S(2)}, u32[]{:S(2)}) collective-permute-start(bf16[144,384]{1,0:T(8,128)(2,1)S(1)} %convert_add_fusion.2), channel_id=1, source_target_pairs={{0,4},{1,17},{2,6},{3,19},{4,0},{5,21},{6,2},{7,23},{8,12},{9,25},... | collective-permute-start | bytes 331784 | tf_op jit(solution)/shard_map/ppermute | solution.py:433
  36.5 1.0 %collective-permute-done.9 = bf16[160,384]{1,0:T(8,128)(2,1)S(1)} collective-permute-done((bf16[160,384]{1,0:T(8,128)(2,1)S(1)}, bf16[160,384]{1,0:T(8,128)(2,1)S(1)}, u32[]{:S(2)}, u32[]{:S(2)}) %collective-permute-start.9) | collective-permute-done | bytes 122912 | tf_op jit(solution)/shard_map/ppermute | solution.py:433
  37.6 2.3 %collective-permute-start.10 = (bf16[160,384]{1,0:T(8,128)(2,1)S(1)}, bf16[160,384]{1,0:T(8,128)(2,1)S(1)}, u32[]{:S(2)}, u32[]{:S(2)}) collective-permute-start(bf16[160,384]{1,0:T(8,128)(2,1)S(1)} %pad_maximum_fusion.4), channel_id=1, source_target_pairs={{0,4},{1,17},{2,6},{3,19},{4,0},{5,21},{6,2},{7,23},{8,12},{9,25},... | collective-permute-start | bytes 368648 | tf_op jit(solution)/shard_map/ppermute | solution.py:433
  40.1 1.3 %collective-permute-start.14 = (bf16[288,384]{1,0:T(8,128)(2,1)S(1)}, bf16[288,384]{1,0:T(8,128)(2,1)S(1)}, u32[]{:S(2)}, u32[]{:S(2)}) collective-permute-start(bf16[288,384]{1,0:T(8,128)(2,1)S(1)} %pad_maximum_fusion.left), channel_id=1, source_target_pairs={{0,16},{1,3},{2,18},{3,1},{4,20},{5,7},{6,22},{7,5},{8,24},{9,11},... | collective-permute-start | bytes 663560 | tf_op jit(solution)/shard_map/ppermute | solution.py:433
  41.3 1.5 %collective-permute-done.10 = bf16[160,384]{1,0:T(8,128)(2,1)S(1)} collective-permute-done((bf16[160,384]{1,0:T(8,128)(2,1)S(1)}, bf16[160,384]{1,0:T(8,128)(2,1)S(1)}, u32[]{:S(2)}, u32[]{:S(2)}) %collective-permute-start.10) | collective-permute-done | bytes 122912 | tf_op jit(solution)/shard_map/ppermute | solution.py:433
  42.9 1.3 %collective-permute-start.11 = (bf16[256,384]{1,0:T(8,128)(2,1)S(1)}, bf16[256,384]{1,0:T(8,128)(2,1)S(1)}, u32[]{:S(2)}, u32[]{:S(2)}) collective-permute-start(bf16[256,384]{1,0:T(8,128)(2,1)S(1)} %pad_maximum_fusion.1), channel_id=1, source_target_pairs={{0,16},{1,3},{2,18},{3,1},{4,20},{5,7},{6,22},{7,5},{8,24},{9,11},... | collective-permute-start | bytes 589832 | tf_op jit(solution)/shard_map/ppermute | solution.py:433
  44.2 1.4 %collective-permute-done.16.got_right = bf16[192,384]{1,0:T(8,128)(2,1)S(1)} collective-permute-done((bf16[192,384]{1,0:T(8,128)(2,1)S(1)}, bf16[192,384]{1,0:T(8,128)(2,1)S(1)}, u32[]{:S(2)}, u32[]{:S(2)}) %collective-permute-start.16) | collective-permute-done | bytes 147488 | tf_op jit(solution)/shard_map/ppermute | solution.py:433
  45.6 1.2 %shard_map.103.whole = f32[5,384,384]{2,1,0:T(8,128)} custom-call(bf16[288,384]{1,0:T(8,128)(2,1)S(1)} %pad_maximum_fusion.left, bf16[192,384]{1,0:T(8,128)(2,1)S(1)} %pad_maximum_fusion.3.right, bf16[288,384]{1,0:T(8,128)(2,1)S(1)} %collective-permute-done.15.got_left, bf16[192,384]{1,0:T(8,128)(2,1)S(1)} %collective-permute-done.16.got_right), custom_call_target="tpu_custom_call" | custom-call | tf_op jit(solution)/shard_map/pallas_call | solution.py:446
  47.0 1.6 %collective-permute-done.11 = bf16[256,384]{1,0:T(8,128)(2,1)S(1)} collective-permute-done((bf16[256,384]{1,0:T(8,128)(2,1)S(1)}, bf16[256,384]{1,0:T(8,128)(2,1)S(1)}, u32[]{:S(2)}, u32[]{:S(2)}) %collective-permute-start.11) | collective-permute-done | bytes 196640 | tf_op jit(solution)/shard_map/ppermute | solution.py:433
  48.8 1.1 %shard_map.104.whole = f32[5,384,384]{2,1,0:T(8,128)} custom-call(bf16[288,384]{1,0:T(8,128)(2,1)S(1)} %collective-permute-done.14.left, bf16[192,384]{1,0:T(8,128)(2,1)S(1)} %slice.39.right, bf16[288,384]{1,0:T(8,128)(2,1)S(1)} %collective-permute-done.17.got_left, f32[5,384,384]{2,1,0:T(8,128)} %shard_map.103.whole), custom_call_target="tpu_custom_call", output_to_operand_aliasing={{}: (3, {})} | custom-call | tf_op jit(solution)/shard_map/pallas_call | solution.py:446
  (45 shorter events, 7.9 us)
Async XLA Ops:
  0.6 13.8 %collective-permute-start.3 = (bf16[512,384]{1,0:T(8,128)(2,1)}, bf16[512,384]{1,0:T(8,128)(2,1)S(1)}, u32[]{:S(2)}, u32[]{:S(2)}) collective-permute-start(bf16[512,384]{1,0:T(8,128)(2,1)} %bitcast.3), channel_id=1, source_target_pairs={{0,16},{1,17},{2,18},{3,19},{4,20},{5,21},{6,22},{7,23},{8,24},{9,... | collective-permute-start | bytes 1179656 | tf_op jit(solution)/shard_map/ppermute | solution.py:433
  4.8 3.6 %collective-permute-start.1 = (bf16[16,768]{1,0:T(8,128)(2,1)S(1)}, bf16[16,768]{1,0:T(8,128)(2,1)S(1)}, u32[]{:S(2)}, u32[]{:S(2)}) collective-permute-start(bf16[16,768]{1,0:T(8,128)(2,1)S(1)} %get-tuple-element.34), channel_id=1, source_target_pairs={{1,2},{2,1},{3,4},{4,3},{5,6},{6,5},{7,8},{8,7},{9,10},{10,9},{11,... | collective-permute-start | bytes 73736 | tf_op jit(solution)/shard_map/ppermute | solution.py:501
  5.5 3.8 %collective-permute-start = (bf16[16,768]{1,0:T(8,128)(2,1)S(1)}, bf16[16,768]{1,0:T(8,128)(2,1)S(1)}, u32[]{:S(2)}, u32[]{:S(2)}) collective-permute-start(bf16[16,768]{1,0:T(8,128)(2,1)S(1)} %get-tuple-element.33.near), channel_id=1, source_target_pairs={{0,1},{1,0},{2,3},{3,2},{4,5},{5,4},{6,7},{7,6},{8,9},{9,8},{10,11... | collective-permute-start | bytes 73736 | tf_op jit(solution)/shard_map/ppermute | solution.py:433
  9.2 4.3 %collective-permute-start.2 = (bf16[16,768]{1,0:T(8,128)(2,1)S(1)}, bf16[16,768]{1,0:T(8,128)(2,1)S(1)}, u32[]{:S(2)}, u32[]{:S(2)}) collective-permute-start(bf16[16,768]{1,0:T(8,128)(2,1)S(1)} %add_add_fusion), channel_id=1, source_target_pairs={{0,16},{1,17},{2,18},{3,19},{4,20},{5,21},{6,22},{7,23},{8,24},{9,... | collective-permute-start | bytes 73736 | tf_op jit(solution)/shard_map/ppermute | solution.py:433
  14.9 1.9 %collective-permute-start.4 = (bf16[480,384]{1,0:T(8,128)(2,1)S(1)}, bf16[480,384]{1,0:T(8,128)(2,1)S(1)}, u32[]{:S(2)}, u32[]{:S(2)}) collective-permute-start(bf16[480,384]{1,0:T(8,128)(2,1)S(1)} %shard_map.97), channel_id=1, source_target_pairs={{0,1},{1,0},{2,3},{3,2},{4,5},{5,4},{6,7},{7,6},{8,9},{9,8},{10,11... | collective-permute-start | bytes 1105928 | tf_op jit(solution)/shard_map/ppermute | solution.py:433
  16.9 6.4 %collective-permute-start.5 = (bf16[240,384]{1,0:T(8,128)(2,1)S(1)}, bf16[240,384]{1,0:T(8,128)(2,1)S(1)}, u32[]{:S(2)}, u32[]{:S(2)}) collective-permute-start(bf16[240,384]{1,0:T(8,128)(2,1)S(1)} %get-tuple-element.44), channel_id=1, source_target_pairs={{0,4},{1,3},{2,6},{3,1},{4,0},{5,7},{6,2},{7,5},{8,12},{9,11},{10,... | collective-permute-start | bytes 552968 | tf_op jit(solution)/shard_map/ppermute | solution.py:433
  23.4 4.8 %collective-permute-start.6 = (bf16[144,384]{1,0:T(8,128)(2,1)S(1)}, bf16[144,384]{1,0:T(8,128)(2,1)S(1)}, u32[]{:S(2)}, u32[]{:S(2)}) collective-permute-start(bf16[144,384]{1,0:T(8,128)(2,1)S(1)} %fusion), channel_id=1, source_target_pairs={{0,2},{1,9},{2,0},{3,11},{4,6},{5,13},{6,4},{7,15},{8,10},{9,1},{1... | collective-permute-start | bytes 331784 | tf_op jit(solution)/shard_map/ppermute | solution.py:433
  24.5 6.8 %collective-permute-start.8 = (bf16[160,384]{1,0:T(8,128)(2,1)S(1)}, bf16[160,384]{1,0:T(8,128)(2,1)S(1)}, u32[]{:S(2)}, u32[]{:S(2)}) collective-permute-start(bf16[160,384]{1,0:T(8,128)(2,1)S(1)} %fusion.1), channel_id=1, source_target_pairs={{0,2},{1,9},{2,0},{3,11},{4,6},{5,13},{6,4},{7,15},{8,10},{9,1},{1... | collective-permute-start | bytes 368648 | tf_op jit(solution)/shard_map/ppermute | solution.py:433
  28.2 6.5 %collective-permute-start.7 = (bf16[144,384]{1,0:T(8,128)(2,1)S(1)}, bf16[144,384]{1,0:T(8,128)(2,1)S(1)}, u32[]{:S(2)}, u32[]{:S(2)}) collective-permute-start(bf16[144,384]{1,0:T(8,128)(2,1)S(1)} %fusion.2), channel_id=1, source_target_pairs={{0,8},{1,5},{2,10},{3,7},{4,12},{5,1},{6,14},{7,3},{8,0},{9,13},{1... | collective-permute-start | bytes 331784 | tf_op jit(solution)/shard_map/ppermute | solution.py:433
  31.4 6.2 %collective-permute-start.9 = (bf16[160,384]{1,0:T(8,128)(2,1)S(1)}, bf16[160,384]{1,0:T(8,128)(2,1)S(1)}, u32[]{:S(2)}, u32[]{:S(2)}) collective-permute-start(bf16[160,384]{1,0:T(8,128)(2,1)S(1)} %fusion.3), channel_id=1, source_target_pairs={{0,8},{1,5},{2,10},{3,7},{4,12},{5,1},{6,14},{7,3},{8,0},{9,13},{1... | collective-permute-start | bytes 368648 | tf_op jit(solution)/shard_map/ppermute | solution.py:433
  34.8 5.2 %collective-permute-start.13 = (bf16[144,384]{1,0:T(8,128)(2,1)S(1)}, bf16[144,384]{1,0:T(8,128)(2,1)S(1)}, u32[]{:S(2)}, u32[]{:S(2)}) collective-permute-start(bf16[144,384]{1,0:T(8,128)(2,1)S(1)} %convert_add_fusion.2), channel_id=1, source_target_pairs={{0,4},{1,17},{2,6},{3,19},{4,0},{5,21},{6,2},{7,23},{8,12},{9,25},... | collective-permute-start | bytes 331784 | tf_op jit(solution)/shard_map/ppermute | solution.py:433
  37.6 5.2 %collective-permute-start.10 = (bf16[160,384]{1,0:T(8,128)(2,1)S(1)}, bf16[160,384]{1,0:T(8,128)(2,1)S(1)}, u32[]{:S(2)}, u32[]{:S(2)}) collective-permute-start(bf16[160,384]{1,0:T(8,128)(2,1)S(1)} %pad_maximum_fusion.4), channel_id=1, source_target_pairs={{0,4},{1,17},{2,6},{3,19},{4,0},{5,21},{6,2},{7,23},{8,12},{9,25},... | collective-permute-start | bytes 368648 | tf_op jit(solution)/shard_map/ppermute | solution.py:433
  40.0 5.6 %collective-permute-start.15 = (bf16[288,384]{1,0:T(8,128)(2,1)S(1)}, bf16[288,384]{1,0:T(8,128)(2,1)S(1)}, u32[]{:S(2)}, u32[]{:S(2)}) collective-permute-start(bf16[288,384]{1,0:T(8,128)(2,1)S(1)} %pad_maximum_fusion.left), channel_id=1, source_target_pairs={{0,1},{1,0},{2,3},{3,2},{4,5},{5,4},{6,7},{7,6},{8,9},{9,8},{10,11... | collective-permute-start | bytes 663560 | tf_op jit(solution)/shard_map/ppermute | solution.py:433
  40.1 6.8 %collective-permute-start.14 = (bf16[288,384]{1,0:T(8,128)(2,1)S(1)}, bf16[288,384]{1,0:T(8,128)(2,1)S(1)}, u32[]{:S(2)}, u32[]{:S(2)}) collective-permute-start(bf16[288,384]{1,0:T(8,128)(2,1)S(1)} %pad_maximum_fusion.left), channel_id=1, source_target_pairs={{0,16},{1,3},{2,18},{3,1},{4,20},{5,7},{6,22},{7,5},{8,24},{9,11},... | collective-permute-start | bytes 663560 | tf_op jit(solution)/shard_map/ppermute | solution.py:433
  42.9 5.7 %collective-permute-start.11 = (bf16[256,384]{1,0:T(8,128)(2,1)S(1)}, bf16[256,384]{1,0:T(8,128)(2,1)S(1)}, u32[]{:S(2)}, u32[]{:S(2)}) collective-permute-start(bf16[256,384]{1,0:T(8,128)(2,1)S(1)} %pad_maximum_fusion.1), channel_id=1, source_target_pairs={{0,16},{1,3},{2,18},{3,1},{4,20},{5,7},{6,22},{7,5},{8,24},{9,11},... | collective-permute-start | bytes 589832 | tf_op jit(solution)/shard_map/ppermute | solution.py:433
  44.2 1.4 %collective-permute-start.16 = (bf16[192,384]{1,0:T(8,128)(2,1)S(1)}, bf16[192,384]{1,0:T(8,128)(2,1)S(1)}, u32[]{:S(2)}, u32[]{:S(2)}) collective-permute-start(bf16[192,384]{1,0:T(8,128)(2,1)S(1)} %pad_maximum_fusion.3.right), channel_id=1, source_target_pairs={{0,1},{1,0},{2,3},{3,2},{4,5},{5,4},{6,7},{7,6},{8,9},{9,8},{10,11... | collective-permute-start | bytes 442376 | tf_op jit(solution)/shard_map/ppermute | solution.py:433
  46.8 2.0 %collective-permute-start.17 = (bf16[288,384]{1,0:T(8,128)(2,1)S(1)}, bf16[288,384]{1,0:T(8,128)(2,1)S(1)}, u32[]{:S(2)}, u32[]{:S(2)}) collective-permute-start(bf16[288,384]{1,0:T(8,128)(2,1)S(1)} %collective-permute-done.14.left), channel_id=1, source_target_pairs={{0,1},{1,0},{2,3},{3,2},{4,5},{5,4},{6,7},{7,6},{8,9},{9,8},{10,11... | collective-permute-start | bytes 663560 | tf_op jit(solution)/shard_map/ppermute | solution.py:433
  48.7 1.5 %collective-permute-start.12 = (bf16[256,384]{1,0:T(8,128)(2,1)S(1)}, bf16[256,384]{1,0:T(8,128)(2,1)S(1)}, u32[]{:S(2)}, u32[]{:S(2)}) collective-permute-start(bf16[256,384]{1,0:T(8,128)(2,1)S(1)} %pad_maximum_fusion.2), channel_id=1, source_target_pairs={{0,1},{1,0},{2,3},{3,2},{4,5},{5,4},{6,7},{7,6},{8,9},{9,8},{10,11... | collective-permute-start | bytes 589832 | tf_op jit(solution)/shard_map/ppermute | solution.py:433
